TPU v7x, 128 devices: a whole 4x4x4 slice. The times are simulated.
128 devices in a mesh: pool: 4 (over x), dev: 32 (over z, y, core).
Axes of the slice: x: 4, y: 4, z: 4, core: 2. Of those that a mesh axis runs over, the one named last changes fastest.
Arguments:
- patches: bfloat16 [256, 128, 1280], P('dev', 'pool'), may hold values from -6 to 6
- enc_tiles: int32 [32], replicated, may hold values from 1 to 8, 128 in all
- req_tiles: int32 [64], replicated, may hold values from 1 to 4, 128 in all
- req_owner: int32 [64, 1], replicated, may hold values from 0 to 3; in each aligned block of 64 rows (0 to 63, 64 to 127, ...) at most 24 rows name the same one
- fc1_weight: bfloat16 [1280, 5120], P(None, 'pool'), may hold values from -0.15625 to 0.15625
- fc2_weight: bfloat16 [5120, 1280], P('pool'), may hold values from -0.078125 to 0.078125
- key_weight: bfloat16 [1280, 1024], replicated, may hold values from -0.15625 to 0.15625
- value_weight: bfloat16 [1280, 1024], replicated, may hold values from -0.15625 to 0.15625
- query_weight: bfloat16 [8192, 8192], P(None, 'dev'), may hold values from -0.0625 to 0.0625
- out_weight: bfloat16 [8192, 8192], P('dev'), may hold values from -0.0625 to 0.0625
- text_hidden: bfloat16 [96, 4, 8192], P('pool'), may hold values from -6 to 6
Outputs:
- mixed: bfloat16 [96, 4, 8192], P('pool', None, 'dev')
Inputs may be any that keep to these rules, and one draw needn't show every extreme that they name: `enc_tiles`: the entries sum to 128; the largest is 8. `req_tiles`: the entries sum to 128; the largest is 4. `req_owner`: no group owns more than 24 requests, and some group owns exactly 24.
All inputs are finite; a program needn't handle non-finite values.
Results may differ from a plain program's by a relative error of at most 0.008.
Values may be sent and summed in bfloat16 or wider, within the bound.
No kernel may reach another device: no remote copies, remote signals or barrier semaphores. Data moves between devices by JAX's collectives and lax.ppermute only.
A program may use at most 128 MiB of HBM per device.

v0:
```python
import jax
import jax.numpy as jnp
from jax import lax
from jax.sharding import PartitionSpec as P

HEADS = 64
KV_HEADS = 8
HEAD_DIM = 128
MAXT = 4


epsilon = 1e-05


def layer_stats(values_in):
    center = values_in - jnp.mean(values_in, axis=-1, keepdims=True)
    spread = jnp.mean(center * center, axis=-1, keepdims=True)
    return center / jnp.sqrt(spread + epsilon)


def rms_scale(values_in):
    return values_in / jnp.sqrt(jnp.mean(values_in * values_in, axis=-1, keepdims=True) + epsilon)


def slot_tables(enc_tiles, req_tiles, req_owner, groups, slots, capacity, most_tiles):
    enc_start = jnp.cumsum(enc_tiles) - enc_tiles
    req_start = jnp.cumsum(req_tiles) - req_tiles
    owner = req_owner[:, 0]
    group_ids = jnp.arange(groups, dtype=jnp.int32)
    member = (owner[:, None] == group_ids[None, :]).astype(jnp.int32)
    rank_in = jnp.sum((jnp.cumsum(member, axis=0) - 1) * member, axis=1)
    slot_ids = jnp.arange(slots, dtype=jnp.int32)
    match = (
        (owner[None, None, :] == group_ids[:, None, None])
        & (rank_in[None, None, :] == slot_ids[None, :, None])
    ).astype(jnp.int32)
    live = jnp.sum(match, axis=2) > 0
    length = jnp.sum(match * req_tiles[None, None, :], axis=2)
    first_tile = jnp.sum(match * req_start[None, None, :], axis=2)
    position = jnp.arange(most_tiles, dtype=jnp.int32)
    valid = position[None, None, :] < length[:, :, None]
    tile_index = first_tile[:, :, None] + position[None, None, :]
    column = jnp.sum((enc_start <= tile_index[..., None]).astype(jnp.int32), axis=-1) - 1
    column_hit = (column[..., None] == jnp.arange(enc_tiles.shape[0], dtype=jnp.int32)).astype(
        jnp.int32
    )
    column_start = jnp.sum(column_hit * enc_start, axis=-1)
    source = column * capacity + tile_index - column_start
    source = jnp.where(valid, source, 0)
    return (source, valid, live)


def place_tiles(received, source, valid):
    flat_rows = received.reshape((received.shape[0] * received.shape[1],) + received.shape[2:])
    picked = jnp.take(flat_rows, source.reshape(-1), axis=0)
    picked = picked.reshape(source.shape + flat_rows.shape[1:])
    return jnp.where(valid[..., None, None], picked, jnp.zeros_like(picked))


def body(
    patches,
    enc_tiles,
    req_tiles,
    req_owner,
    fc1_weight,
    fc2_weight,
    key_weight,
    value_weight,
    query_weight,
    out_weight,
    text_hidden,
):
    capacity, quarter, width_in = patches.shape
    groups = lax.axis_size("pool")
    devices = lax.axis_size("dev")
    share_count = devices // KV_HEADS
    local_heads = HEADS // devices
    slots, steps, model_width = text_hidden.shape
    flat_patches = patches.reshape(capacity * quarter, width_in)
    normed = layer_stats(flat_patches.astype(jnp.float32)).astype(jnp.bfloat16)
    widened = jax.nn.gelu(
        jnp.dot(
            lax.all_gather(normed, "pool", axis=0, tiled=True),
            fc1_weight,
            preferred_element_type=jnp.float32,
        ),
        approximate=False,
    ).astype(jnp.bfloat16)
    update = lax.psum_scatter(
        jnp.dot(widened, fc2_weight, preferred_element_type=jnp.float32),
        "pool",
        scatter_dimension=0,
        tiled=True,
    )
    vision = (flat_patches.astype(jnp.float32) + update).astype(jnp.bfloat16)
    key_rows = rms_scale(
        jnp.dot(vision, key_weight, preferred_element_type=jnp.float32).reshape(
            capacity * quarter, KV_HEADS, HEAD_DIM
        )
    ).astype(jnp.bfloat16)
    value_rows = (
        jnp.dot(vision, value_weight, preferred_element_type=jnp.float32)
        .astype(jnp.bfloat16)
        .reshape(capacity * quarter, KV_HEADS, HEAD_DIM)
    )
    paired_rows = jnp.concatenate([key_rows, value_rows], axis=-1).reshape(
        capacity, quarter, KV_HEADS, 2 * HEAD_DIM
    )
    heads_first = jnp.transpose(paired_rows, (2, 0, 1, 3))
    source, valid, live = slot_tables(
        enc_tiles, req_tiles, req_owner, groups, slots, capacity, MAXT
    )
    copies_out = jnp.repeat(heads_first, share_count, axis=0)
    received = lax.all_to_all(copies_out, "dev", split_axis=0, concat_axis=0, tiled=True)
    arrived = lax.all_to_all(
        place_tiles(received, source, valid), "pool", split_axis=0, concat_axis=0, tiled=True
    )
    group_index = lax.axis_index("pool")
    slot_valid = lax.dynamic_index_in_dim(valid, group_index, 0, keepdims=False).astype(jnp.float32)
    slot_live = lax.dynamic_index_in_dim(live, group_index, 0, keepdims=False)
    normed_text = (
        rms_scale(text_hidden.astype(jnp.float32))
        .astype(jnp.bfloat16)
        .reshape(slots * steps, model_width)
    )
    query = jnp.dot(normed_text, query_weight, preferred_element_type=jnp.float32).reshape(
        slots, steps * local_heads, HEAD_DIM
    )
    query = rms_scale(query).astype(jnp.bfloat16)
    scores = jnp.einsum(
        "rad,prmnd->rapmn", query, arrived[..., :HEAD_DIM], preferred_element_type=jnp.float32
    ) * HEAD_DIM ** (-0.5)
    weights = jnp.exp(scores) * slot_valid[:, None, None, :, None]
    total = jnp.sum(weights, axis=(2, 3, 4))
    total = jnp.where(slot_live[:, None], total, jnp.ones_like(total))
    weights = (weights / total[:, :, None, None, None]).astype(jnp.bfloat16)
    attended = jnp.einsum(
        "rapmn,prmnd->rad", weights, arrived[..., HEAD_DIM:], preferred_element_type=jnp.float32
    ).astype(jnp.bfloat16)
    partial_out = jnp.dot(
        attended.reshape(slots * steps, local_heads * HEAD_DIM),
        out_weight,
        preferred_element_type=jnp.float32,
    )
    summed = lax.psum_scatter(
        partial_out.astype(jnp.bfloat16), "dev", scatter_dimension=1, tiled=True
    ).astype(jnp.float32)
    width_out = model_width // devices
    residual = lax.dynamic_slice_in_dim(
        text_hidden, lax.axis_index("dev") * width_out, width_out, 2
    )
    mixed = (residual.reshape(slots * steps, width_out).astype(jnp.float32) + summed).astype(
        jnp.bfloat16
    )
    return mixed.reshape(slots, steps, width_out)


def solution(mesh):
    return jax.shard_map(
        body,
        mesh=mesh,
        in_specs=(
            P("dev", "pool", None),
            P(),
            P(),
            P(),
            P(None, "pool"),
            P("pool", None),
            P(),
            P(),
            P(None, "dev"),
            P("dev", None),
            P("pool", None, None),
        ),
        out_specs=P("pool", None, "dev"),
        check_vma=False,
    )
```

profile of v0, /device:TPU:6, one launch (start us, length us, event | category | flops | bytes accessed | tf_op | source)
XLA Modules:
  0.0 382.7 jit_solution(903922697695620529)
XLA Ops:
  6.5 1.4 convert_reduce_fusion
  8.0 1.4 fusion.21
  9.5 2.2 fusion.23
  11.7 35.7 %all-gather.2.cloned.1.call-done = bf16[1024,1280]{1,0:T(8,128)(2,1)} async-done(((bf16[256,1280]{1,0:T(8,128)(2,1)}), bf16[1024,1280]{1,0:T(8,128)(2,1)}) %all-gather.2.cloned.1.call-update) | async-done | bytes 2621456 | tf_op jit(solution)/shard_map/all_gather | solution.py:83
  47.5 20.5 %fusion.16 = f32[1024,1280]{1,0:T(8,128)} fusion(bf16[1280,1280]{1,0:T(8,128)(2,1)S(1)} %copy-done, bf16[1024,1280]{1,0:T(8,128)(2,1)} %all-gather.2.cloned.1.call-done, bf16[1280,1280]{1,0:T(8,128)(2,1)} %param.15), kind=kOutput, calls=%fused_computation.30 | convolution fusion | flops 6796083200 | bytes 14417920 | tf_op jit(solution)/shard_map/dot_general | solution.py:90
  68.0 55.6 %reduce-scatter.3.cloned.1.call-done = f32[256,1280]{1,0:T(8,128)} async-done(((f32[1024,1280]{1,0:T(8,128)}), f32[256,1280]{1,0:T(8,128)}) %reduce-scatter.3.cloned.1.call-update) | async-done | bytes 1310736 | tf_op jit(solution)/shard_map/reduce_scatter | solution.py:89
  123.6 1.4 fusion.24
  125.1 2.8 fusion.74
  127.9 0.1 multiply_bitcast_fusion
  128.0 0.2 copy.79
  128.2 0.3 reduce_sum.117
  128.6 0.2 copy.78
  128.8 2.8 fusion.25
  131.6 0.1 copy.80
  131.7 0.3 fusion.32
  132.1 0.1 maximum_bitcast_fusion
  132.2 0.2 copy.70
  132.5 2.5 broadcast_in_dim.40
  134.9 7.7 %all-to-all-start = ((bf16[32,8,32,256]{3,2,1,0:T(8,128)(2,1)}), bf16[32,8,32,256]{3,2,1,0:T(8,128)(2,1)}, u32[]{:S(2)}, u32[]{:S(2)}) async-start(bf16[32,8,32,256]{3,2,1,0:T(8,128)(2,1)} %bitcast.61), calls=%async_computation.1 | async-start | bytes 8388608 | tf_op jit(solution)/shard_map/all_to_all | solution.py:114
  142.7 0.1 copy.68
  142.8 0.1 reduce_window_sum.25
  143.0 0.1 reduce.3
  143.3 0.1 reduce.2
  143.4 0.2 select_reduce_fusion.1
  143.7 0.3 fusion.36
  144.0 0.5 convert_reduce_fusion.1
  144.4 0.5 select_reduce_fusion
  144.9 0.1 copy.71
  145.0 0.1 reshape.362
  145.1 0.1 copy.66
  145.2 0.1 copy.69
  145.4 50.6 %all-to-all-done = bf16[32,8,32,256]{3,2,1,0:T(8,128)(2,1)} async-done(((bf16[32,8,32,256]{3,2,1,0:T(8,128)(2,1)}), bf16[32,8,32,256]{3,2,1,0:T(8,128)(2,1)}, u32[]{:S(2)}, u32[]{:S(2)}) %all-to-all-start) | async-done | bytes 4194336 | tf_op jit(solution)/shard_map/all_to_all | solution.py:114
  196.0 5.8 %gather_fusion = bf16[384,32,256]{2,1,0:T(8,128)(2,1)} fusion(bf16[256,32,256]{2,1,0:T(8,128)(2,1)} %bitcast.9, s32[1024]{0:T(1024)S(1)} %pad_clamp_fusion), kind=kCustom, calls=%fused_computation | custom fusion | bytes 12584448 | tf_op jit(solution)/shard_map/jit(_take)/gather | solution.py:55
  201.8 6.8 %select_select_fusion = bf16[4,24,4,32,256]{4,3,2,1,0:T(8,128)(2,1)} fusion(bf16[4,24,4,32,256]{4,3,2,1,0:T(8,128)(2,1)} %bitcast.60, pred[4,24,4]{2,1,0:T(8,128)(4,1)S(1)} %copy.69, pred[4,24,4]{2,1,0:T(8,128)(4,1)S(1)} %copy.66), kind=kLoop, calls=%fused_computation.3 | loop fusion | flops 6291456 | bytes 12583680 | tf_op jit(solution)/shard_map/jit(_where)/select_n | solution.py:57
  208.6 7.7 %all-to-all-start.1 = ((bf16[4,24,4,32,256]{4,3,2,1,0:T(8,128)(2,1)}), bf16[4,24,4,32,256]{4,3,2,1,0:T(8,128)(2,1)}, u32[]{:S(2)}, u32[]{:S(2)}) async-start(bf16[4,24,4,32,256]{4,3,2,1,0:T(8,128)(2,1)} %select_select_fusion), calls=%async_computation.2 | async-start | bytes 12582912 | tf_op jit(solution)/shard_map/all_to_all | solution.py:115
  216.4 0.9 fusion.10
  217.3 1.0 fusion.11
  218.3 0.4 reshape.348
  218.7 3.0 fusion.73
  221.8 0.1 multiply_reduce_fusion
  221.9 61.1 %all-to-all-done.1 = bf16[4,24,4,32,256]{4,3,2,1,0:T(8,128)(2,1)} async-done(((bf16[4,24,4,32,256]{4,3,2,1,0:T(8,128)(2,1)}), bf16[4,24,4,32,256]{4,3,2,1,0:T(8,128)(2,1)}, u32[]{:S(2)}, u32[]{:S(2)}) %all-to-all-start.1) | async-done | bytes 6291488 | tf_op jit(solution)/shard_map/all_to_all | solution.py:115
  283.0 6.2 %fusion.70 = (f32[24,8]{1,0:T(8,128)S(1)}, f32[24,8,4,4,32]{4,1,3,2,0:T(8,128)S(1)}) fusion(f32[24,4]{1,0:T(8,128)S(1)} %copy.73, f32[24,8,128]{2,1,0:T(8,128)S(1)} %reshape.349, f32[24,8]{1,0:T(8,128)S(1)} %add_sqrt_fusion.2, bf16[4,24,4,32,256]{4,3,2,1,0:T(8,128)(2,1)} %all-to-all-done.1), kind=kOutput, calls=%fused_computation.118 | convolution fusion | flops 25509696 | bytes 3639168 | tf_op jit(solution)/shard_map/rad,prmnd->rapmn/dot_general | solution.py:130
  289.2 3.3 fusion.29
  292.6 4.1 %convolution_convert_fusion = bf16[96,8192]{1,0:T(8,128)(2,1)} fusion(bf16[96,256]{1,0:T(8,128)(2,1)S(1)} %reshape.357, bf16[256,8192]{1,0:T(8,128)(2,1)} %param.20), kind=kOutput, calls=%fused_computation.1 | convolution fusion | flops 403439616 | bytes 5816320 | tf_op jit(solution)/shard_map/dot_general | solution.py:140
  296.7 0.8 dynamic-slice_convert_fusion
  297.6 77.1 %reduce-scatter.5.cloned.1.call-done = bf16[96,256]{1,0:T(8,128)(2,1)} async-done(((bf16[96,8192]{1,0:T(8,128)(2,1)}), bf16[96,256]{1,0:T(8,128)(2,1)}) %reduce-scatter.5.cloned.1.call-update) | async-done | bytes 49168 | tf_op jit(solution)/shard_map/reduce_scatter | solution.py:145
  374.7 0.8 add_convert_fusion
  375.5 0.6 reshape.358
  (50 shorter events, 1.0 us)
Async XLA Ops:
  6.5 41.0 %copy-start = (bf16[1280,1280]{1,0:T(8,128)(2,1)S(1)}, bf16[1280,1280]{1,0:T(8,128)(2,1)}, u32[]{:S(2)}) copy-start(bf16[1280,1280]{1,0:T(8,128)(2,1)} %param.16) | copy-start | bytes 9830404
  6.5 40.9 %all-gather.2.cloned.1.call-start = ((), (), s32[]{:S(2)}) async-start(), calls=%async_computation.4 | async-start | bytes 3276800 | tf_op jit(solution)/shard_map/all_gather | solution.py:83
  11.7 111.9 %reduce-scatter.3.cloned.1.call-start = ((), (), s32[]{:S(2)}) async-start(), calls=%async_computation.5 | async-start | bytes 6553600 | tf_op jit(solution)/shard_map/reduce_scatter | solution.py:89
  68.0 55.6 %copy-start.2 = (bf16[8,32,1280]{2,1,0:T(8,128)(2,1)S(1)}, bf16[8,32,1280]{2,1,0:T(8,128)(2,1)}, u32[]{:S(2)}) copy-start(bf16[8,32,1280]{2,1,0:T(8,128)(2,1)} %param.11) | copy-start | bytes 1966084
  125.1 2.8 copy-start.4
  134.9 7.7 %copy-start.6 = (s32[64]{0:T(128)S(1)}, s32[64]{0:T(128)}, u32[]{:S(2)}) copy-start(s32[64]{0:T(128)} %param.13) | copy-start | bytes 772
  134.9 7.8 %copy-start.5 = (s32[64,1]{0,1:T(1,128)S(1)}, s32[64,1]{0,1:T(1,128)}, u32[]{:S(2)}) copy-start(s32[64,1]{0,1:T(1,128)} %param.14) | copy-start | bytes 772
  134.9 8.2 %copy-start.7 = (s32[32]{0:T(128)S(1)}, s32[32]{0:T(128)}, u32[]{:S(2)}) copy-start(s32[32]{0:T(128)} %param.12) | copy-start | bytes 388
  134.9 61.0 %all-to-all-start = ((bf16[32,8,32,256]{3,2,1,0:T(8,128)(2,1)}), bf16[32,8,32,256]{3,2,1,0:T(8,128)(2,1)}, u32[]{:S(2)}, u32[]{:S(2)}) async-start(bf16[32,8,32,256]{3,2,1,0:T(8,128)(2,1)} %bitcast.61), calls=%async_computation.1 | async-start | bytes 8388608 | tf_op jit(solution)/shard_map/all_to_all | solution.py:114
  208.6 7.8 %copy-start.3 = (bf16[24,4,8192]{2,1,0:T(4,128)(2,1)S(1)}, bf16[24,4,8192]{2,1,0:T(4,128)(2,1)}, u32[]{:S(2)}) copy-start(bf16[24,4,8192]{2,1,0:T(4,128)(2,1)} %param.21) | copy-start | bytes 4718596
  208.6 74.3 %all-to-all-start.1 = ((bf16[4,24,4,32,256]{4,3,2,1,0:T(8,128)(2,1)}), bf16[4,24,4,32,256]{4,3,2,1,0:T(8,128)(2,1)}, u32[]{:S(2)}, u32[]{:S(2)}) async-start(bf16[4,24,4,32,256]{4,3,2,1,0:T(8,128)(2,1)} %select_select_fusion), calls=%async_computation.2 | async-start | bytes 12582912 | tf_op jit(solution)/shard_map/all_to_all | solution.py:115
  216.3 158.4 %reduce-scatter.5.cloned.1.call-start = ((), (), s32[]{:S(2)}) async-start(), calls=%async_computation.6 | async-start | bytes 1622016 | tf_op jit(solution)/shard_map/reduce_scatter | solution.py:145
  289.2 87.0 %copy-start.1 = (bf16[1280,1280]{1,0:T(8,128)(2,1)S(1)}, bf16[1280,1280]{1,0:T(8,128)(2,1)}, u32[]{:S(2)}) copy-start(bf16[1280,1280]{1,0:T(8,128)(2,1)} %param.16) | copy-start | bytes 9830404
Sparse Core Ops, SparseCore 0:
  11.8 35.6 all-gather.1
  68.1 55.4 reduce-scatter.2
  296.9 77.8 reduce-scatter.4
where the time goes:
time: 384 us; the launch traced here: 383 us
  waiting for transfers between devices  280 us (73%)
  matrix products  42.7 us (11%)
  other arithmetic  19.9 us (5%)
  starting transfers between devices  15.5 us (4%)
  between operations  13.4 us (3%)
  local copies, waits for them, and re-layouts  11.1 us (3%)
    reduce_scatter x1, waiting for transfers between devices, body(): lax.psum_scatter(partial_out.astype(jnp.bfloat16), 'dev', scatter_dimensi...  77.1 us
    all_to_all x1, waiting for transfers between devices, body(): lax.all_to_all(place_tiles(received, source, valid), 'pool', split_axis=0...  61.1 us
    reduce_scatter x1, waiting for transfers between devices, body(): lax.psum_scatter(jnp.dot(widened, fc2_weight, preferred_element_type=jnp....  55.6 us
    all_to_all x1, waiting for transfers between devices, body(): lax.all_to_all(copies_out, 'dev', split_axis=0, concat_axis=0, tiled=True)  50.6 us
    all_gather x1, waiting for transfers between devices, body(): lax.all_gather(normed, 'pool', axis=0, tiled=True)  35.7 us
    dot_general x1, matrix products, body(): jnp.dot(widened, fc2_weight, preferred_element_type=jnp.float32)  20.5 us
    all_to_all x1, starting transfers between devices, body(): lax.all_to_all(copies_out, 'dev', split_axis=0, concat_axis=0, tiled=True)  7.71 us
    all_to_all x1, starting transfers between devices, body(): lax.all_to_all(place_tiles(received, source, valid), 'pool', split_axis=0...  7.71 us
  transfers between devices with their start and end apart: 5, of which 5 were waited for; matrix products, arithmetic and copies ran while one was open for 2% of the time, Pallas kernels for 0%

commit v1 on v0

v1 whole, which is shorter than its diff:
```python
import functools

import jax
import jax.numpy as jnp
from jax import lax
from jax.experimental import pallas as pl
from jax.experimental.pallas import tpu as pltpu
from jax.sharding import PartitionSpec as P

HEADS = 64
KV_HEADS = 8
HEAD_DIM = 128
CORES = 2
RING = 4
BLOCK = 256
F32, BF16 = jnp.float32, jnp.bfloat16

epsilon = 1e-05

VMEM = pl.BlockSpec(memory_space=pltpu.VMEM)
SMEM = pl.BlockSpec(memory_space=pltpu.SMEM)


def params(mib):
    return pltpu.CompilerParams(vmem_limit_bytes=mib * 1024 * 1024)


def pool_shift(x, by):
    return lax.ppermute(x, "pool", [(i, (i + by) % RING) for i in range(RING)])


def dev_shift(x, by_z, by_y, by_core):
    pairs = []
    for z in range(RING):
        for y in range(RING):
            for k in range(CORES):
                to = ((z + by_z) % RING, (y + by_y) % RING, (k + by_core) % CORES)
                pairs.append(((z * RING + y) * CORES + k, (to[0] * RING + to[1]) * CORES + to[2]))
    return lax.ppermute(x, "dev", pairs)


def normalize_kernel(half, at_ref, patches_ref, rows_ref):
    for r in range(RING):
        slot = lax.rem(at_ref[0] + r, RING) + half * RING
        values = patches_ref[slot].astype(F32)
        center = values - jnp.mean(values, axis=-1, keepdims=True)
        spread = jnp.mean(center * center, axis=-1, keepdims=True)
        rows_ref[r] = (center / jnp.sqrt(spread + epsilon)).astype(BF16)


def normalize(at, patches, half):
    _, quarter, width = patches.shape
    return pl.pallas_call(
        functools.partial(normalize_kernel, half),
        out_shape=jax.ShapeDtypeStruct((RING, quarter, width), BF16),
        in_specs=[SMEM, VMEM],
        out_specs=VMEM,
        compiler_params=params(16),
    )(at, patches)


def feed_forward_kernel(
    half, quarter, at_ref, patches_ref, own_ref, left_ref, right_ref, far_left_ref, far_right_ref,
    fc1_ref, fc2_ref, total_ref, one_ref, two_ref, three_ref, rows_ref, wide_ref,
):
    width, hidden = fc1_ref.shape
    rows = RING * quarter
    for at, ref in ((0, own_ref), (1, left_ref), (3, right_ref)):
        rows_ref[at * rows : (at + 1) * rows] = ref[...].reshape(rows, width)
    rows_ref[2 * rows : 2 * rows + rows // 2] = far_left_ref[...].reshape(rows // 2, width)
    rows_ref[2 * rows + rows // 2 : 3 * rows] = far_right_ref[...].reshape(rows // 2, width)

    def widen(step, _):
        at = pl.ds(pl.multiple_of(step * BLOCK, BLOCK), BLOCK)
        values = jnp.dot(rows_ref[...], fc1_ref[:, at], preferred_element_type=F32)
        wide_ref[:, at] = (0.5 * values * (1.0 + lax.erf(values * 0.5**0.5))).astype(BF16)
        return 0

    lax.fori_loop(0, hidden // BLOCK, widen, 0)
    outs = (total_ref, one_ref, two_ref, three_ref)

    def narrow(step, _):
        at = pl.ds(pl.multiple_of(step * BLOCK, BLOCK), BLOCK)
        sums = jnp.dot(wide_ref[...], fc2_ref[:, at], preferred_element_type=F32)
        for source in range(RING):
            for m in range(RING):
                piece = sums[source * rows + m * quarter : source * rows + (m + 1) * quarter]
                shift = (m - source) % RING
                if source == 0:
                    slot = lax.rem(at_ref[0] + m, RING) + half * RING
                    piece = piece + patches_ref[slot, :, at].astype(F32)
                outs[shift][m, :, at] = piece.astype(outs[shift].dtype)
        return 0

    lax.fori_loop(0, width // BLOCK, narrow, 0)


def feed_forward(at, patches, own, left, right, far_left, far_right, fc1, fc2, half):
    _, quarter, width = patches.shape
    hidden = fc1.shape[1]
    shape = (RING, quarter, width)
    sent = jax.ShapeDtypeStruct(shape, BF16)
    return pl.pallas_call(
        functools.partial(feed_forward_kernel, half, quarter),
        out_shape=(jax.ShapeDtypeStruct(shape, F32), sent, sent, sent),
        in_specs=[SMEM] + [VMEM] * 8,
        out_specs=(VMEM,) * 4,
        scratch_shapes=[
            pltpu.VMEM((RING * RING * quarter, width), BF16),
            pltpu.VMEM((RING * RING * quarter, hidden), BF16),
        ],
        compiler_params=params(32),
        cost_estimate=pl.CostEstimate(
            flops=4 * RING * RING * quarter * width * hidden,
            bytes_accessed=4 * width * hidden,
            transcendentals=0,
        ),
    )(at, patches, own, left, right, far_left, far_right, fc1, fc2)


def query_kernel(text_ref, weight_ref, query_ref, total_ref, square_ref):
    step = pl.program_id(0)

    @pl.when(step == 0)
    def _():
        total_ref[...] = jnp.zeros_like(total_ref)
        square_ref[...] = jnp.zeros_like(square_ref)

    text = text_ref[...]
    total_ref[...] += jnp.dot(text, weight_ref[...], preferred_element_type=F32)
    wide = text.astype(F32)
    square_ref[...] += jnp.sum(wide * wide, axis=-1, keepdims=True)

    @pl.when(step == pl.num_programs(0) - 1)
    def _():
        width = text_ref.shape[1] * pl.num_programs(0)
        values = total_ref[...] / jnp.sqrt(square_ref[...] / width + epsilon)
        for head in range(query_ref.shape[0]):
            part = values[:, head * HEAD_DIM : (head + 1) * HEAD_DIM]
            mean = jnp.mean(part * part, axis=-1, keepdims=True)
            query_ref[head] = (part / jnp.sqrt(mean + epsilon)).astype(BF16)


def make_query(text, weight):
    rows, width = text.shape
    columns = weight.shape[1]
    depth = 2048
    return pl.pallas_call(
        query_kernel,
        grid=(width // depth,),
        out_shape=jax.ShapeDtypeStruct((columns // HEAD_DIM, rows, HEAD_DIM), BF16),
        in_specs=[
            pl.BlockSpec((rows, depth), lambda k: (0, k)),
            pl.BlockSpec((depth, columns), lambda k: (k, 0)),
        ],
        out_specs=pl.BlockSpec((columns // HEAD_DIM, rows, HEAD_DIM), lambda k: (0, 0, 0)),
        scratch_shapes=[pltpu.VMEM((rows, columns), F32), pltpu.VMEM((rows, 1), F32)],
        compiler_params=params(16),
        cost_estimate=pl.CostEstimate(
            flops=2 * rows * width * columns,
            bytes_accessed=2 * width * (columns + rows),
            transcendentals=0,
        ),
    )(text, weight)


def iota(shape, dim):
    return lax.broadcasted_iota(jnp.int32, shape, dim)


def select_kernel(
    slots, steps, heads, capacity, at_ref, enc_ref, req_ref, owner_ref,
    own_ref, one_ref, two_ref, three_ref, chosen_ref, target_ref,
):
    here = at_ref[0]
    columns, requests = enc_ref.shape[1], req_ref.shape[1]
    halves = capacity // RING
    per_group = heads * slots * steps
    rows = columns * halves * heads * steps
    before = iota((requests, requests), 0) < iota((requests, requests), 1)
    equal = iota((requests, requests), 0) == iota((requests, requests), 1)
    req_row = req_ref[...]
    req_column = jnp.sum(jnp.where(equal, req_row, 0), axis=1, keepdims=True)
    req_start = jnp.sum(jnp.where(before, req_column, 0), axis=0, keepdims=True)
    owner_column = owner_ref[...]
    owner_row = jnp.sum(jnp.where(equal, owner_column, 0), axis=0, keepdims=True)
    rank = jnp.sum(
        jnp.where(before & (owner_column == owner_row), 1, 0), axis=0, keepdims=True
    )
    place = owner_row * per_group + rank * steps
    enc_row = enc_ref[...]
    enc_equal = iota((columns, columns), 0) == iota((columns, columns), 1)
    enc_before = iota((columns, columns), 0) < iota((columns, columns), 1)
    enc_column = jnp.sum(jnp.where(enc_equal, enc_row, 0), axis=1, keepdims=True)
    enc_start = jnp.sum(jnp.where(enc_before, enc_column, 0), axis=0, keepdims=True)

    row = iota((rows, 1), 0)
    per_tile = heads * steps
    column = row // (halves * per_tile)
    slot = row // per_tile % halves * RING + here
    hit = column == iota((rows, columns), 1)
    count = jnp.sum(jnp.where(hit, enc_row, 0), axis=1, keepdims=True)
    start = jnp.sum(jnp.where(hit, enc_start, 0), axis=1, keepdims=True)
    tile = jnp.where(slot < count, start + slot, -1)
    has = (req_start <= tile) & (tile < req_start + req_row)
    base = jnp.sum(jnp.where(has, place + 1, 0), axis=1, keepdims=True) - 1
    within = row % per_tile
    target = jnp.where(base < 0, -1, base + within // steps * (slots * steps) + within % steps)
    target_ref[...] = target
    chosen = jnp.zeros((rows, HEAD_DIM), F32)
    for shift, ref in enumerate((own_ref, one_ref, two_ref, three_ref)):
        group = lax.rem(here - shift + RING, RING)
        match = target == iota((rows, per_group), 1) + group * per_group
        chosen = chosen + jnp.dot(
            jnp.where(match, 1.0, 0.0).astype(BF16),
            ref[...].reshape(per_group, HEAD_DIM),
            preferred_element_type=F32,
        )
    chosen_ref[...] = chosen.astype(BF16)


def select(at, enc, req, owner, queries, slots, steps, capacity):
    heads = queries[0].shape[0]
    rows = enc.shape[1] * (capacity // RING) * heads * steps
    return pl.pallas_call(
        functools.partial(select_kernel, slots, steps, heads, capacity),
        out_shape=(
            jax.ShapeDtypeStruct((rows, HEAD_DIM), BF16),
            jax.ShapeDtypeStruct((rows, 1), jnp.int32),
        ),
        in_specs=[SMEM] + [VMEM] * 7,
        out_specs=(VMEM, VMEM),
        compiler_params=params(16),
    )(at, enc, req, owner, *queries)


def attend_kernel(half, first, quarter, *refs):
    if first:
        total_ref, one_ref, two_ref, three_ref, key_ref, value_ref, query_ref, out_ref, vision = refs
    else:
        (total_ref, one_ref, two_ref, three_ref, key_ref, value_ref, query_ref, before_ref,
         out_ref, vision) = refs
    rows = RING * quarter

    @pl.when(pl.program_id(0) == 0)
    def _():
        summed = total_ref[...]
        for ref in (one_ref, two_ref, three_ref):
            summed = summed + ref[...].astype(F32)
        vision[...] = summed.astype(BF16).reshape(rows, vision.shape[1])

    keys = jnp.dot(vision[...], key_ref[...], preferred_element_type=F32)
    values = jnp.dot(vision[...], value_ref[...], preferred_element_type=F32).astype(BF16)
    per_head, per_device = query_ref.shape[1], query_ref.shape[2]
    count = per_head * per_device
    mine = iota((count, 1), 0) % per_device // (per_device // 2) == half
    for head in range(query_ref.shape[0]):
        at = slice(head * HEAD_DIM, (head + 1) * HEAD_DIM)
        key = keys[:, at]
        mean = jnp.mean(key * key, axis=-1, keepdims=True)
        key = (key / jnp.sqrt(mean + epsilon)).astype(BF16)
        query = query_ref[head].reshape(count, HEAD_DIM)
        scores = lax.dot_general(
            query, key, (((1,), (1,)), ((), ())), preferred_element_type=F32
        ) * HEAD_DIM ** (-0.5)
        weights = jnp.where(mine, jnp.exp(scores), 0.0)
        divisor = jnp.sum(weights, axis=-1, keepdims=True)
        numerator = jnp.dot(weights.astype(BF16), values[:, at], preferred_element_type=F32)
        packed = jnp.concatenate(
            [numerator, jnp.broadcast_to(divisor, numerator.shape)], axis=1
        ).reshape(per_head, per_device, 2 * HEAD_DIM)
        if not first:
            packed = packed + before_ref[head].astype(F32)
        out_ref[head] = packed.astype(BF16)


def attend(total, received, key_weight, value_weight, queries, half, before):
    _, quarter, width = total.shape
    heads, per_head, per_device, _ = queries.shape
    columns = key_weight.shape[1]
    grid = 4
    each = heads // grid
    sums = pl.BlockSpec((RING, quarter, width), lambda h: (0, 0, 0))
    weight = pl.BlockSpec((width, columns // grid), lambda h: (0, h))
    packed = pl.BlockSpec((each, per_head, per_device, 2 * HEAD_DIM), lambda h: (h, 0, 0, 0))
    first = before is None
    return pl.pallas_call(
        functools.partial(attend_kernel, half, first, quarter),
        grid=(grid,),
        out_shape=jax.ShapeDtypeStruct((heads, per_head, per_device, 2 * HEAD_DIM), BF16),
        in_specs=[sums] * 4
        + [weight] * 2
        + [pl.BlockSpec((each, per_head, per_device, HEAD_DIM), lambda h: (h, 0, 0, 0))]
        + ([] if first else [packed]),
        out_specs=packed,
        scratch_shapes=[pltpu.VMEM((RING * quarter, width), BF16)],
        compiler_params=params(24),
        cost_estimate=pl.CostEstimate(
            flops=4 * RING * quarter * width * columns,
            bytes_accessed=4 * width * columns,
            transcendentals=0,
        ),
    )(total, *received, key_weight, value_weight, queries, *([] if first else [before]))


def combine_kernel(at_ref, target_ref, packed_ref, own_ref, one_ref, two_ref, three_ref):
    target = target_ref[...]
    per_group = own_ref.shape[0]
    for shift, ref in enumerate((own_ref, one_ref, two_ref, three_ref)):
        group = lax.rem(at_ref[0] + shift, RING)
        match = target == iota((target.shape[0], per_group), 1) + group * per_group
        ref[...] = lax.dot_general(
            jnp.where(match, 1.0, 0.0).astype(BF16),
            packed_ref[...],
            (((0,), (0,)), ((), ())),
            preferred_element_type=F32,
        ).astype(ref.dtype)


def combine(at, target, packed, per_group):
    shape = (per_group, packed.shape[1])
    sent = jax.ShapeDtypeStruct(shape, BF16)
    return pl.pallas_call(
        combine_kernel,
        out_shape=(jax.ShapeDtypeStruct(shape, F32), sent, sent, sent),
        in_specs=[SMEM, VMEM, VMEM],
        out_specs=(VMEM,) * 4,
        compiler_params=params(16),
    )(at, target, packed)


def project_kernel(core, at_ref, own_ref, one_ref, two_ref, three_ref, weight_ref, out_ref):
    summed = own_ref[...]
    for ref in (one_ref, two_ref, three_ref):
        summed = summed + ref[...].astype(F32)
    divisor = summed[:, HEAD_DIM:]
    attended = summed[:, :HEAD_DIM] / jnp.where(divisor > 0.0, divisor, 1.0)
    half = attended.shape[0] // 2
    attended = jnp.concatenate([attended[:half], attended[half:]], axis=1).astype(BF16)
    here = at_ref[1]
    y_at, core_at = here // CORES % RING, here % CORES
    column = lax.rem(core_at + core, CORES)
    for y in range(RING):
        block = lax.rem(y_at + y, RING) * CORES + column
        at = pl.ds(pl.multiple_of(block * BLOCK, BLOCK), BLOCK)
        out_ref[0, y] = jnp.dot(
            attended, weight_ref[:, at], preferred_element_type=F32
        ).astype(BF16)


def project(at, own, received, weight, core):
    depth, columns = weight.shape
    rows = own.shape[0] // 2
    whole = pl.BlockSpec(own.shape, lambda z, at_ref: (0, 0))
    grid_spec = pltpu.PrefetchScalarGridSpec(
        num_scalar_prefetch=1,
        grid=(RING,),
        in_specs=[whole] * 4
        + [
            pl.BlockSpec(
                (depth, columns // RING),
                lambda z, at_ref: (0, lax.rem(at_ref[1] // (RING * CORES) + z, RING)),
            )
        ],
        out_specs=pl.BlockSpec((1, RING, rows, BLOCK), lambda z, at_ref: (z, 0, 0, 0)),
    )
    return pl.pallas_call(
        functools.partial(project_kernel, core),
        grid_spec=grid_spec,
        out_shape=jax.ShapeDtypeStruct((RING, RING, rows, BLOCK), BF16),
        compiler_params=params(16),
        cost_estimate=pl.CostEstimate(
            flops=rows * depth * columns, bytes_accessed=2 * depth * columns, transcendentals=0
        ),
    )(at, own, *received, weight)


def first_sum_kernel(kept_ref, got_ref, own_ref, one_ref, two_ref, three_ref):
    for shift, ref in enumerate((own_ref, one_ref, two_ref, three_ref)):
        ref[...] = (kept_ref[shift].astype(F32) + got_ref[shift].astype(F32)).astype(ref.dtype)


def first_sum(kept, got):
    sent = jax.ShapeDtypeStruct(kept.shape[1:], BF16)
    return pl.pallas_call(
        first_sum_kernel,
        out_shape=(jax.ShapeDtypeStruct(kept.shape[1:], F32), sent, sent, sent),
        in_specs=[VMEM, VMEM],
        out_specs=(VMEM,) * 4,
        compiler_params=params(16),
    )(kept, got)


def second_sum_kernel(kept_ref, a_ref, b_ref, c_ref, own_ref, one_ref, two_ref, three_ref):
    for shift, ref in enumerate((own_ref, one_ref, two_ref, three_ref)):
        summed = kept_ref[shift]
        for got in (a_ref, b_ref, c_ref):
            summed = summed + got[shift].astype(F32)
        ref[...] = summed.astype(ref.dtype)


def second_sum(kept, got):
    sent = jax.ShapeDtypeStruct(kept.shape[1:], BF16)
    return pl.pallas_call(
        second_sum_kernel,
        out_shape=(jax.ShapeDtypeStruct(kept.shape[1:], F32), sent, sent, sent),
        in_specs=[VMEM] * 4,
        out_specs=(VMEM,) * 4,
        compiler_params=params(16),
    )(kept, *got)


def last_sum_kernel(kept_ref, a_ref, b_ref, c_ref, residual_ref, out_ref):
    summed = kept_ref[...]
    for got in (a_ref, b_ref, c_ref):
        summed = summed + got[...].astype(F32)
    out_ref[...] = (residual_ref[...].astype(F32) + summed).astype(BF16)


def last_sum(kept, got, residual):
    return pl.pallas_call(
        last_sum_kernel,
        out_shape=jax.ShapeDtypeStruct(kept.shape, BF16),
        in_specs=[VMEM] * 5,
        out_specs=VMEM,
        compiler_params=params(16),
    )(kept, *got, residual)


def body(
    patches,
    enc_tiles,
    req_tiles,
    req_owner,
    fc1_weight,
    fc2_weight,
    key_weight,
    value_weight,
    query_weight,
    out_weight,
    text_hidden,
):
    capacity = patches.shape[0]
    devices = lax.axis_size("dev")
    local_heads = HEADS // devices
    slots, steps, model_width = text_hidden.shape
    dev_at = lax.axis_index("dev")
    at = jnp.stack([lax.axis_index("pool"), dev_at]).astype(jnp.int32)
    halves = capacity // RING

    own = [normalize(at, patches, i) for i in range(halves)]
    left = [pool_shift(own[i], 1) for i in range(halves)]
    right = [pool_shift(own[i], -1) for i in range(halves)]
    far_left = [pool_shift(left[i][: RING // 2], 1) for i in range(halves)]
    far_right = [pool_shift(right[i][RING // 2 :], -1) for i in range(halves)]

    text = text_hidden.reshape(slots * steps, model_width)
    query = make_query(text, query_weight)
    queries = [query] + [pool_shift(query, s) for s in range(1, RING)]
    chosen, target = select(
        at,
        enc_tiles.reshape(1, -1),
        req_tiles.reshape(1, -1),
        req_owner,
        queries,
        slots,
        steps,
        capacity,
    )
    per_device = halves * local_heads * steps
    tile_queries = lax.all_to_all(
        chosen.reshape(devices, per_device, HEAD_DIM), "dev", split_axis=0, concat_axis=0, tiled=True
    ).reshape(KV_HEADS, devices // KV_HEADS, per_device, HEAD_DIM)

    packed = None
    for i in range(halves):
        total, *messages = feed_forward(
            at, patches, own[i], left[i], right[i], far_left[i], far_right[i],
            fc1_weight, fc2_weight, i,
        )
        received = [pool_shift(messages[s - 1], s) for s in range(1, RING)]
        packed = attend(total, received, key_weight, value_weight, tile_queries, i, packed)
    packed = lax.all_to_all(
        packed.reshape(devices, per_device, 2 * HEAD_DIM),
        "dev",
        split_axis=0,
        concat_axis=0,
        tiled=True,
    ).reshape(devices * per_device, 2 * HEAD_DIM)
    summed, *messages = combine(at, target, packed, local_heads * slots * steps)
    received = [pool_shift(messages[s - 1], s) for s in range(1, RING)]

    away = dev_shift(project(at, summed, received, out_weight, 1), 0, 0, 1)
    kept = project(at, summed, received, out_weight, 0)
    kept, *messages = first_sum(kept, away)
    received = [dev_shift(messages[s - 1], s, 0, 0) for s in range(1, RING)]
    kept, *messages = second_sum(kept, received)
    received = [dev_shift(messages[s - 1], 0, s, 0) for s in range(1, RING)]
    width_out = model_width // devices
    residual = lax.dynamic_slice_in_dim(text, dev_at * width_out, width_out, 1)
    mixed = last_sum(kept, received, residual)
    return mixed.reshape(slots, steps, width_out)


def solution(mesh):
    return jax.shard_map(
        body,
        mesh=mesh,
        in_specs=(
            P("dev", "pool", None),
            P(),
            P(),
            P(),
            P(None, "pool"),
            P("pool", None),
            P(),
            P(),
            P(None, "dev"),
            P("dev", None),
            P("pool", None, None),
        ),
        out_specs=P("pool", None, "dev"),
        check_vma=False,
    )
```

time: 384 us -> 139 us (0.36)
  waiting for transfers between devices: 280 us -> 23.7 us
  matrix products: 42.7 us -> 0 us
  Pallas kernels: 0 us -> 34.1 us
  blocking collectives: 0 us -> 28.3 us
  starting transfers between devices: 15.5 us -> 35.7 us
  other arithmetic: 19.9 us -> 0.07 us
  between operations: 13.4 us -> 0.36 us
  local copies, waits for them, and re-layouts: 11.1 us -> 16.4 us
    reduce_scatter x2 -> x0, waiting for transfers between devices: 133 us -> none  [the longest x1 77.1 us: body(): lax.psum_scatter(partial_out.astype(jnp.bfloat16), 'dev', scatter_dimensi...]
    all_to_all x2 -> x0, waiting for transfers between devices: 112 us -> none  [the longest x1 61.1 us: body(): lax.all_to_all(place_tiles(received, source, valid), 'pool', split_axis=0...]
    dot_general x7 -> x0, matrix products: 42.7 us -> none  [the longest x1 20.5 us: body(): jnp.dot(widened, fc2_weight, preferred_element_type=jnp.float32)]
    all_gather x1 -> x0, waiting for transfers between devices: 35.7 us -> none  [body(): lax.all_gather(normed, 'pool', axis=0, tiled=True)]
    ppermute x0 -> x27, starting transfers between devices: none -> 35.7 us  [the longest x20 27.9 us: pool_shift(): return lax.ppermute(x, 'pool', [(i, (i + by) % RING) for i in range(RING)])]
    pallas_call x0 -> x14, Pallas kernels: none -> 34.1 us  [the longest x2 14 us: feed_forward(): pl.pallas_call(functools.partial(feed_forward_kernel, half, quarter), out...]
    all_to_all x0 -> x2, blocking collectives: none -> 28.3 us  [the longest x1 15.9 us: body(): lax.all_to_all(chosen.reshape(devices, per_device, HEAD_DIM), 'dev', spli...]
    ppermute x0 -> x27, waiting for transfers between devices: none -> 23.7 us  [the longest x7 12 us: dev_shift(): return lax.ppermute(x, 'dev', pairs)]
  transfers between devices with their start and end apart: 5 -> 27, of which waited for: 5 -> 10; matrix products, arithmetic and copies ran while one was open for 2% -> 3% of each run, Pallas kernels for 0% -> 18%
where the time goes in v1:
time: 139 us
  starting transfers between devices  35.7 us (26%)
  Pallas kernels  34.1 us (25%)
  blocking collectives  28.3 us (20%)
  waiting for transfers between devices  23.7 us (17%)
  local copies, waits for them, and re-layouts  16.4 us (12%)
    ppermute x20, starting transfers between devices, pool_shift(): return lax.ppermute(x, 'pool', [(i, (i + by) % RING) for i in range(RING)])  27.9 us
    all_to_all x1, blocking collectives, body(): lax.all_to_all(chosen.reshape(devices, per_device, HEAD_DIM), 'dev', spli...  15.9 us
    pallas_call x2, Pallas kernels, feed_forward(): pl.pallas_call(functools.partial(feed_forward_kernel, half, quarter), out...  14 us
    all_to_all x1, blocking collectives, body(): lax.all_to_all(packed.reshape(devices, per_device, 2 * HEAD_DIM), 'dev',...  12.4 us
    ppermute x7, waiting for transfers between devices, dev_shift(): return lax.ppermute(x, 'dev', pairs)  12 us
    unnamed x51, local copies, waits for them, and re-layouts  11.9 us
    ppermute x20, waiting for transfers between devices, pool_shift(): return lax.ppermute(x, 'pool', [(i, (i + by) % RING) for i in range(RING)])  11.7 us
    pallas_call x2, Pallas kernels, attend(): pl.pallas_call(functools.partial(attend_kernel, half, first, quarter), gr...  9.62 us
  transfers between devices with their start and end apart: 27, of which 10 were waited for; matrix products, arithmetic and copies ran while one was open for 3% of the time, Pallas kernels for 18%

profile of v1, /device:TPU:6, one launch (start us, length us, event | category | flops | bytes accessed | tf_op | source)
XLA Modules:
  0.0 138.7 jit_solution(4997243949392912833)
XLA Ops:
  0.1 1.1 copy-done.5
  1.2 0.8 shard_map.113.own_ref
  2.0 0.9 collective-permute-start.11
  2.9 2.4 %collective-permute-start.10 = (bf16[4,32,1280]{2,1,0:T(8,128)(2,1)S(1)}, bf16[4,32,1280]{2,1,0:T(8,128)(2,1)S(1)}, u32[]{:S(2)}, u32[]{:S(2)}) collective-permute-start(bf16[4,32,1280]{2,1,0:T(8,128)(2,1)S(1)} %shard_map.113.own_ref), channel_id=1, source_target_pairs={{0,32},{32,64},{64,96},{96,0},{1,33},{33,65},{65,97},{97,1},{2,34}... | collective-permute-start | bytes 983048 | tf_op jit(solution)/shard_map/ppermute | solution.py:29
  5.3 0.8 shard_map.111.own_ref
  6.2 3.2 %collective-permute-start.3 = (bf16[4,32,1280]{2,1,0:T(8,128)(2,1)S(1)}, bf16[4,32,1280]{2,1,0:T(8,128)(2,1)S(1)}, u32[]{:S(2)}, u32[]{:S(2)}) collective-permute-start(bf16[4,32,1280]{2,1,0:T(8,128)(2,1)S(1)} %shard_map.111.own_ref), channel_id=1, source_target_pairs={{0,32},{32,64},{64,96},{96,0},{1,33},{33,65},{65,97},{97,1},{2,34}... | collective-permute-start | bytes 983048 | tf_op jit(solution)/shard_map/ppermute | solution.py:29
  9.5 4.4 %collective-permute-done.11.right_ref = bf16[4,32,1280]{2,1,0:T(8,128)(2,1)S(1)} collective-permute-done((bf16[4,32,1280]{2,1,0:T(8,128)(2,1)S(1)}, bf16[4,32,1280]{2,1,0:T(8,128)(2,1)S(1)}, u32[]{:S(2)}, u32[]{:S(2)}) %collective-permute-start.11) | collective-permute-done | bytes 327712 | tf_op jit(solution)/shard_map/ppermute | solution.py:29
  14.8 3.2 %collective-permute-start.12 = (bf16[2,32,1280]{2,1,0:T(8,128)(2,1)}, bf16[2,32,1280]{2,1,0:T(8,128)(2,1)}, u32[]{:S(2)}, u32[]{:S(2)}) collective-permute-start(bf16[2,32,1280]{2,1,0:T(8,128)(2,1)} %slice.18), channel_id=1, source_target_pairs={{0,32},{32,64},{64,96},{96,0},{1,33},{33,65},{65,97},{97,1},{2,34}... | collective-permute-start | bytes 491528 | tf_op jit(solution)/shard_map/ppermute | solution.py:29
  18.0 2.3 %reshape.26.text_ref = bf16[96,8192]{1,0:T(8,128)(2,1)S(1)} reshape(bf16[24,4,8192]{2,1,0:T(4,128)(2,1)} %param.21) | data formatting | bytes 3145728 | tf_op jit(solution)/shard_map/reshape | solution.py:457
  20.4 2.2 %copy-done.4 = bf16[8192,256]{1,0:T(8,128)(2,1)S(1)} copy-done((bf16[8192,256]{1,0:T(8,128)(2,1)S(1)}, bf16[8192,256]{1,0:T(8,128)(2,1)}, u32[]{:S(2)}) %copy-start.4) | copy-done | bytes 4194328
  22.5 1.7 %shard_map.109.own_ref = bf16[2,96,128]{2,1,0:T(8,128)(2,1)S(1)} custom-call(bf16[96,8192]{1,0:T(8,128)(2,1)S(1)} %reshape.26.text_ref, bf16[8192,256]{1,0:T(8,128)(2,1)S(1)} %copy-done.4), custom_call_target="tpu_custom_call" | custom-call | flops 402653184 | bytes 5767168 | tf_op jit(solution)/shard_map/pallas_call | solution.py:148
  24.5 3.3 %collective-permute-start.5 = (bf16[2,32,1280]{2,1,0:T(8,128)(2,1)S(1)}, bf16[2,32,1280]{2,1,0:T(8,128)(2,1)S(1)}, u32[]{:S(2)}, u32[]{:S(2)}) collective-permute-start(bf16[2,32,1280]{2,1,0:T(8,128)(2,1)S(1)} %slice.16), channel_id=1, source_target_pairs={{0,32},{32,64},{64,96},{96,0},{1,33},{33,65},{65,97},{97,1},{2,34}... | collective-permute-start | bytes 491528 | tf_op jit(solution)/shard_map/ppermute | solution.py:29
  27.8 1.9 %copy-done.22 = bf16[1280,1280]{1,0:T(8,128)(2,1)S(1)} copy-done((bf16[1280,1280]{1,0:T(8,128)(2,1)S(1)}, bf16[1280,1280]{1,0:T(8,128)(2,1)}, u32[]{:S(2)}) %copy-start.22) | copy-done | bytes 3276824
  29.8 7.2 %shard_map.114 = (f32[4,32,1280]{2,1,0:T(8,128)S(1)}, bf16[4,32,1280]{2,1,0:T(8,128)(2,1)S(1)}, bf16[4,32,1280]{2,1,0:T(8,128)(2,1)}, bf16[4,32,1280]{2,1,0:T(8,128)(2,1)}) custom-call(s32[2]{0:T(128)S(1)} %pad_add_fusion.at_ref, bf16[8,32,1280]{2,1,0:T(8,128)(2,1)S(1)} %copy-done.6, bf16[4,32,1280]{2,1,0:T(8,128)(2,1)S(1)} %shard_map.113.own_ref, ...), custom_call_target="tpu_custom_call" | custom-call | flops 3355443200 | bytes 6553600 | tf_op jit(solution)/shard_map/pallas_call | solution.py:103
  37.0 2.1 %collective-permute-start.14 = (bf16[4,32,1280]{2,1,0:T(8,128)(2,1)S(1)}, bf16[4,32,1280]{2,1,0:T(8,128)(2,1)S(1)}, u32[]{:S(2)}, u32[]{:S(2)}) collective-permute-start(bf16[4,32,1280]{2,1,0:T(8,128)(2,1)S(1)} %get-tuple-element.34), channel_id=1, source_target_pairs={{0,32},{32,64},{64,96},{96,0},{1,33},{33,65},{65,97},{97,1},{2,34}... | collective-permute-start | bytes 983048 | tf_op jit(solution)/shard_map/ppermute | solution.py:29
  39.0 2.7 %collective-permute-start = (bf16[2,96,128]{2,1,0:T(8,128)(2,1)S(1)}, bf16[2,96,128]{2,1,0:T(8,128)(2,1)S(1)}, u32[]{:S(2)}, u32[]{:S(2)}) collective-permute-start(bf16[2,96,128]{2,1,0:T(8,128)(2,1)S(1)} %shard_map.109.own_ref), channel_id=1, source_target_pairs={{0,32},{32,64},{64,96},{96,0},{1,33},{33,65},{65,97},{97,1},{2,34}... | collective-permute-start | bytes 147464 | tf_op jit(solution)/shard_map/ppermute | solution.py:29
  41.8 0.9 collective-permute-start.15
  42.7 1.3 collective-permute-start.16
  44.0 1.0 copy-done.14
  45.0 1.0 copy-done.16
  46.0 6.8 %shard_map.112 = (f32[4,32,1280]{2,1,0:T(8,128)S(1)}, bf16[4,32,1280]{2,1,0:T(8,128)(2,1)}, bf16[4,32,1280]{2,1,0:T(8,128)(2,1)}, bf16[4,32,1280]{2,1,0:T(8,128)(2,1)}) custom-call(s32[2]{0:T(128)S(1)} %pad_add_fusion.at_ref, bf16[8,32,1280]{2,1,0:T(8,128)(2,1)S(1)} %copy-done.6, bf16[4,32,1280]{2,1,0:T(8,128)(2,1)S(1)} %copy-done.12, ...), custom_call_target="tpu_custom_call" | custom-call | flops 3355443200 | bytes 6553600 | tf_op jit(solution)/shard_map/pallas_call | solution.py:103
  52.7 1.9 %collective-permute-start.7 = (bf16[4,32,1280]{2,1,0:T(8,128)(2,1)}, bf16[4,32,1280]{2,1,0:T(8,128)(2,1)}, u32[]{:S(2)}, u32[]{:S(2)}) collective-permute-start(bf16[4,32,1280]{2,1,0:T(8,128)(2,1)} %get-tuple-element.29), channel_id=1, source_target_pairs={{0,32},{32,64},{64,96},{96,0},{1,33},{33,65},{65,97},{97,1},{2,34}... | collective-permute-start | bytes 983048 | tf_op jit(solution)/shard_map/ppermute | solution.py:29
  54.6 1.4 %collective-permute-start.8 = (bf16[4,32,1280]{2,1,0:T(8,128)(2,1)}, bf16[4,32,1280]{2,1,0:T(8,128)(2,1)}, u32[]{:S(2)}, u32[]{:S(2)}) collective-permute-start(bf16[4,32,1280]{2,1,0:T(8,128)(2,1)} %get-tuple-element.30), channel_id=1, source_target_pairs={{0,64},{32,96},{64,0},{96,32},{1,65},{33,97},{65,1},{97,33},{2,66}... | collective-permute-start | bytes 983048 | tf_op jit(solution)/shard_map/ppermute | solution.py:29
  56.0 0.7 copy-done.9
  56.8 1.5 %shard_map.110 = (bf16[512,128]{1,0:T(8,128)(2,1)S(1)}, s32[512,1]{1,0:T(8,128)S(1)}) custom-call(s32[2]{0:T(128)S(1)} %pad_add_fusion.at_ref, s32[1,32]{1,0:T(1,128)S(1)} %bitcast.13, s32[1,64]{1,0:T(1,128)S(1)} %bitcast.14, s32[64,1]{1,0:T(8,128)S(1)} %copy.12.owner_ref, bf16[2,96,128]{2,1,0:T(8,128)(2,1)S(1)} %shard_map.109.own_ref, ...), custom_call_target="tpu_custom_call" | custom-call | tf_op jit(solution)/shard_map/pallas_call | solution.py:225
  58.4 15.9 %all_to_all.10 = bf16[32,16,128]{2,1,0:T(8,128)(2,1)S(1)} all-to-all(bf16[32,16,128]{2,1,0:T(8,128)(2,1)S(1)} %bitcast.12), channel_id=1, replica_groups=mesh['pool'=4,'dev'=32] {'dev'}, dimensions={0} | all-to-all | bytes 262144 | tf_op jit(solution)/shard_map/all_to_all | solution.py:471
  74.3 1.7 %copy-done.2 = bf16[1280,1024]{1,0:T(8,128)(2,1)S(1)} copy-done((bf16[1280,1024]{1,0:T(8,128)(2,1)S(1)}, bf16[1280,1024]{1,0:T(8,128)(2,1)}, u32[]{:S(2)}) %copy-start.2) | copy-done | bytes 2621464
  76.1 1.1 copy-done.8
  77.2 1.0 copy-done.10
  78.1 4.7 %shard_map.115.refs_7_ = bf16[8,4,16,256]{3,2,1,0:T(8,128)(2,1)S(1)} custom-call(f32[4,32,1280]{2,1,0:T(8,128)S(1)} %copy-done.8, bf16[4,32,1280]{2,1,0:T(8,128)(2,1)S(1)} %copy-done.10, bf16[4,32,1280]{2,1,0:T(8,128)(2,1)} %collective-permute-done.15.refs_2_, bf16[4,32,1280]{2,1,0:T(8,128)(2,1)} %collective-permute-done.16.refs_3_, ...), custom_call_target="tpu_custom_call" | custom-call | flops 671088640 | bytes 5242880 | tf_op jit(solution)/shard_map/pallas_call | solution.py:287
  82.9 4.9 %shard_map.116 = bf16[8,4,16,256]{3,2,1,0:T(8,128)(2,1)S(1)} custom-call(f32[4,32,1280]{2,1,0:T(8,128)S(1)} %get-tuple-element.28.refs_0_, bf16[4,32,1280]{2,1,0:T(8,128)(2,1)} %collective-permute-done.7.refs_1_, bf16[4,32,1280]{2,1,0:T(8,128)(2,1)} %collective-permute-done.8.refs_2_, bf16[4,32,1280]{2,1,0:T(8,128)(2,1)} %collective-permute-done.9.refs_3_, ...), custom_call_target="tpu_custom_call" | custom-call | flops 671088640 | bytes 5242880 | tf_op jit(solution)/shard_map/pallas_call | solution.py:287
  87.8 12.4 %all_to_all.11 = bf16[32,16,256]{2,1,0:T(8,128)(2,1)S(1)} all-to-all(bf16[32,16,256]{2,1,0:T(8,128)(2,1)S(1)} %bitcast.10), channel_id=1, replica_groups=mesh['pool'=4,'dev'=32] {'dev'}, dimensions={0} | all-to-all | bytes 524288 | tf_op jit(solution)/shard_map/all_to_all | solution.py:483
  100.2 1.2 shard_map.117
  101.4 3.3 %collective-permute-start.17 = (bf16[192,256]{1,0:T(8,128)(2,1)S(1)}, bf16[192,256]{1,0:T(8,128)(2,1)S(1)}, u32[]{:S(2)}, u32[]{:S(2)}) collective-permute-start(bf16[192,256]{1,0:T(8,128)(2,1)S(1)} %get-tuple-element.38), channel_id=1, source_target_pairs={{0,32},{32,64},{64,96},{96,0},{1,33},{33,65},{65,97},{97,1},{2,34}... | collective-permute-start | bytes 294920 | tf_op jit(solution)/shard_map/ppermute | solution.py:29
  104.7 0.9 collective-permute-start.18
  105.7 3.6 %collective-permute-done.17.one_ref = bf16[192,256]{1,0:T(8,128)(2,1)S(1)} collective-permute-done((bf16[192,256]{1,0:T(8,128)(2,1)S(1)}, bf16[192,256]{1,0:T(8,128)(2,1)S(1)}, u32[]{:S(2)}, u32[]{:S(2)}) %collective-permute-start.17) | collective-permute-done | bytes 98336 | tf_op jit(solution)/shard_map/ppermute | solution.py:29
  109.3 2.6 %collective-permute-done.18.two_ref = bf16[192,256]{1,0:T(8,128)(2,1)S(1)} collective-permute-done((bf16[192,256]{1,0:T(8,128)(2,1)S(1)}, bf16[192,256]{1,0:T(8,128)(2,1)S(1)}, u32[]{:S(2)}, u32[]{:S(2)}) %collective-permute-start.18) | collective-permute-done | bytes 98336 | tf_op jit(solution)/shard_map/ppermute | solution.py:29
  111.8 1.1 collective-permute-done.19.three_ref
  113.0 2.1 %shard_map.119 = bf16[4,4,96,256]{3,2,1,0:T(8,128)(2,1)S(1)} custom-call(s32[2]{0:T(128)S(1)} %pad_add_fusion.at_ref, f32[192,256]{1,0:T(8,128)S(1)} %get-tuple-element.37.own_ref, bf16[192,256]{1,0:T(8,128)(2,1)S(1)} %collective-permute-done.17.one_ref, bf16[192,256]{1,0:T(8,128)(2,1)S(1)} %collective-permute-done.18.two_ref, ...), custom_call_target="tpu_custom_call" | custom-call | flops 201326592 | bytes 4194304 | tf_op jit(solution)/shard_map/pallas_call | solution.py:367
  115.2 2.1 %shard_map.118.kept_ref = bf16[4,4,96,256]{3,2,1,0:T(8,128)(2,1)S(1)} custom-call(s32[2]{0:T(128)S(1)} %pad_add_fusion.at_ref, f32[192,256]{1,0:T(8,128)S(1)} %get-tuple-element.37.own_ref, bf16[192,256]{1,0:T(8,128)(2,1)S(1)} %collective-permute-done.17.one_ref, bf16[192,256]{1,0:T(8,128)(2,1)S(1)} %collective-permute-done.18.two_ref, ...), custom_call_target="tpu_custom_call" | custom-call | flops 201326592 | bytes 4194304 | tf_op jit(solution)/shard_map/pallas_call | solution.py:367
  118.3 2.0 %collective-permute-start.22 = (bf16[4,96,256]{2,1,0:T(8,128)(2,1)S(1)}, bf16[4,96,256]{2,1,0:T(8,128)(2,1)S(1)}, u32[]{:S(2)}, u32[]{:S(2)}) collective-permute-start(bf16[4,96,256]{2,1,0:T(8,128)(2,1)S(1)} %get-tuple-element.43), channel_id=1, source_target_pairs={{0,16},{1,17},{2,18},{3,19},{4,20},{5,21},{6,22},{7,23},{8,24},{9,... | collective-permute-start | bytes 589832 | tf_op jit(solution)/shard_map/ppermute | solution.py:39
  120.3 1.4 %collective-permute-start.23 = (bf16[4,96,256]{2,1,0:T(8,128)(2,1)S(1)}, bf16[4,96,256]{2,1,0:T(8,128)(2,1)S(1)}, u32[]{:S(2)}, u32[]{:S(2)}) collective-permute-start(bf16[4,96,256]{2,1,0:T(8,128)(2,1)S(1)} %get-tuple-element.44), channel_id=1, source_target_pairs={{0,24},{1,25},{2,26},{3,27},{4,28},{5,29},{6,30},{7,31},{8,0},{9,1... | collective-permute-start | bytes 589832 | tf_op jit(solution)/shard_map/ppermute | solution.py:39
  121.7 8.5 %collective-permute-done.21.a_ref = bf16[4,96,256]{2,1,0:T(8,128)(2,1)S(1)} collective-permute-done((bf16[4,96,256]{2,1,0:T(8,128)(2,1)S(1)}, bf16[4,96,256]{2,1,0:T(8,128)(2,1)S(1)}, u32[]{:S(2)}, u32[]{:S(2)}) %collective-permute-start.21) | collective-permute-done | bytes 196640 | tf_op jit(solution)/shard_map/ppermute | solution.py:39
  130.9 0.8 collective-permute-start.24
  131.8 2.1 %collective-permute-start.25 = (bf16[96,256]{1,0:T(8,128)(2,1)S(1)}, bf16[96,256]{1,0:T(8,128)(2,1)S(1)}, u32[]{:S(2)}, u32[]{:S(2)}) collective-permute-start(bf16[96,256]{1,0:T(8,128)(2,1)S(1)} %get-tuple-element.47), channel_id=1, source_target_pairs={{0,4},{1,5},{2,6},{3,7},{4,0},{5,1},{6,2},{7,3},{8,12},{9,13},{10,... | collective-permute-start | bytes 147464 | tf_op jit(solution)/shard_map/ppermute | solution.py:39
  134.5 0.8 constant_dynamic-slice_fusion.residual_ref
  135.3 1.0 collective-permute-done.24.a_ref
  136.3 1.0 collective-permute-done.25.b_ref
  (81 shorter events, 5.3 us)
Async XLA Ops:
  0.1 1.1 copy-start.5
  2.0 11.9 %collective-permute-start.11 = (bf16[4,32,1280]{2,1,0:T(8,128)(2,1)S(1)}, bf16[4,32,1280]{2,1,0:T(8,128)(2,1)S(1)}, u32[]{:S(2)}, u32[]{:S(2)}) collective-permute-start(bf16[4,32,1280]{2,1,0:T(8,128)(2,1)S(1)} %shard_map.113.own_ref), channel_id=1, source_target_pairs={{0,96},{32,0},{64,32},{96,64},{1,97},{33,1},{65,33},{97,65},{2,98}... | collective-permute-start | bytes 983048 | tf_op jit(solution)/shard_map/ppermute | solution.py:29
  2.9 11.1 %collective-permute-start.10 = (bf16[4,32,1280]{2,1,0:T(8,128)(2,1)S(1)}, bf16[4,32,1280]{2,1,0:T(8,128)(2,1)S(1)}, u32[]{:S(2)}, u32[]{:S(2)}) collective-permute-start(bf16[4,32,1280]{2,1,0:T(8,128)(2,1)S(1)} %shard_map.113.own_ref), channel_id=1, source_target_pairs={{0,32},{32,64},{64,96},{96,0},{1,33},{33,65},{65,97},{97,1},{2,34}... | collective-permute-start | bytes 983048 | tf_op jit(solution)/shard_map/ppermute | solution.py:29
  6.1 18.1 %copy-start.11 = (bf16[4,32,1280]{2,1,0:T(8,128)(2,1)}, bf16[4,32,1280]{2,1,0:T(8,128)(2,1)S(1)}, u32[]{:S(2)}) copy-start(bf16[4,32,1280]{2,1,0:T(8,128)(2,1)S(1)} %shard_map.111.own_ref) | copy-start | bytes 983044
  6.1 18.2 %collective-permute-start.4 = (bf16[4,32,1280]{2,1,0:T(8,128)(2,1)S(1)}, bf16[4,32,1280]{2,1,0:T(8,128)(2,1)S(1)}, u32[]{:S(2)}, u32[]{:S(2)}) collective-permute-start(bf16[4,32,1280]{2,1,0:T(8,128)(2,1)S(1)} %shard_map.111.own_ref), channel_id=1, source_target_pairs={{0,96},{32,0},{64,32},{96,64},{1,97},{33,1},{65,33},{97,65},{2,98}... | collective-permute-start | bytes 983048 | tf_op jit(solution)/shard_map/ppermute | solution.py:29
  6.2 18.2 %collective-permute-start.3 = (bf16[4,32,1280]{2,1,0:T(8,128)(2,1)S(1)}, bf16[4,32,1280]{2,1,0:T(8,128)(2,1)S(1)}, u32[]{:S(2)}, u32[]{:S(2)}) collective-permute-start(bf16[4,32,1280]{2,1,0:T(8,128)(2,1)S(1)} %shard_map.111.own_ref), channel_id=1, source_target_pairs={{0,32},{32,64},{64,96},{96,0},{1,33},{33,65},{65,97},{97,1},{2,34}... | collective-permute-start | bytes 983048 | tf_op jit(solution)/shard_map/ppermute | solution.py:29
  13.9 13.9 %collective-permute-start.13 = (bf16[2,32,1280]{2,1,0:T(8,128)(2,1)S(1)}, bf16[2,32,1280]{2,1,0:T(8,128)(2,1)}, u32[]{:S(2)}, u32[]{:S(2)}) collective-permute-start(bf16[2,32,1280]{2,1,0:T(8,128)(2,1)S(1)} %slice.19), channel_id=1, source_target_pairs={{0,96},{32,0},{64,32},{96,64},{1,97},{33,1},{65,33},{97,65},{2,98}... | collective-permute-start | bytes 491528 | tf_op jit(solution)/shard_map/ppermute | solution.py:29
  14.8 13.0 %collective-permute-start.12 = (bf16[2,32,1280]{2,1,0:T(8,128)(2,1)}, bf16[2,32,1280]{2,1,0:T(8,128)(2,1)}, u32[]{:S(2)}, u32[]{:S(2)}) collective-permute-start(bf16[2,32,1280]{2,1,0:T(8,128)(2,1)} %slice.18), channel_id=1, source_target_pairs={{0,32},{32,64},{64,96},{96,0},{1,33},{33,65},{65,97},{97,1},{2,34}... | collective-permute-start | bytes 491528 | tf_op jit(solution)/shard_map/ppermute | solution.py:29
  20.3 2.2 %copy-start.4 = (bf16[8192,256]{1,0:T(8,128)(2,1)S(1)}, bf16[8192,256]{1,0:T(8,128)(2,1)}, u32[]{:S(2)}) copy-start(bf16[8192,256]{1,0:T(8,128)(2,1)} %weight_ref.3) | copy-start | bytes 12582916
  22.5 1.7 %copy-start.3 = (bf16[96,8192]{1,0:T(8,128)(2,1)}, bf16[96,8192]{1,0:T(8,128)(2,1)S(1)}, u32[]{:S(2)}) copy-start(bf16[96,8192]{1,0:T(8,128)(2,1)S(1)} %reshape.26.text_ref) | copy-start | bytes 4718596
  22.5 5.3 %copy-start.6 = (bf16[8,32,1280]{2,1,0:T(8,128)(2,1)S(1)}, bf16[8,32,1280]{2,1,0:T(8,128)(2,1)}, u32[]{:S(2)}) copy-start(bf16[8,32,1280]{2,1,0:T(8,128)(2,1)} %patches_ref.7) | copy-start | bytes 1966084
  22.5 5.3 %copy-start.18 = (bf16[4,32,1280]{2,1,0:T(8,128)(2,1)S(1)}, bf16[4,32,1280]{2,1,0:T(8,128)(2,1)}, u32[]{:S(2)}) copy-start(bf16[4,32,1280]{2,1,0:T(8,128)(2,1)} %copy-done.17) | copy-start | bytes 983044
  22.5 5.3 %copy-start.21 = (bf16[1280,1280]{1,0:T(8,128)(2,1)S(1)}, bf16[1280,1280]{1,0:T(8,128)(2,1)}, u32[]{:S(2)}) copy-start(bf16[1280,1280]{1,0:T(8,128)(2,1)} %fc1_ref.3) | copy-start | bytes 9830404
  24.3 14.8 %collective-permute-start.2 = (bf16[2,96,128]{2,1,0:T(8,128)(2,1)S(1)}, bf16[2,96,128]{2,1,0:T(8,128)(2,1)S(1)}, u32[]{:S(2)}, u32[]{:S(2)}) collective-permute-start(bf16[2,96,128]{2,1,0:T(8,128)(2,1)S(1)} %shard_map.109.own_ref), channel_id=1, source_target_pairs={{0,96},{32,0},{64,32},{96,64},{1,97},{33,1},{65,33},{97,65},{2,98}... | collective-permute-start | bytes 147464 | tf_op jit(solution)/shard_map/ppermute | solution.py:29
  24.4 12.6 %copy-start.13 = (bf16[4,32,1280]{2,1,0:T(8,128)(2,1)}, bf16[4,32,1280]{2,1,0:T(8,128)(2,1)S(1)}, u32[]{:S(2)}) copy-start(bf16[4,32,1280]{2,1,0:T(8,128)(2,1)S(1)} %collective-permute-done.4.right_ref) | copy-start | bytes 983044
  24.4 17.4 %collective-permute-start.6 = (bf16[2,32,1280]{2,1,0:T(8,128)(2,1)S(1)}, bf16[2,32,1280]{2,1,0:T(8,128)(2,1)S(1)}, u32[]{:S(2)}, u32[]{:S(2)}) collective-permute-start(bf16[2,32,1280]{2,1,0:T(8,128)(2,1)S(1)} %slice.17), channel_id=1, source_target_pairs={{0,96},{32,0},{64,32},{96,64},{1,97},{33,1},{65,33},{97,65},{2,98}... | collective-permute-start | bytes 491528 | tf_op jit(solution)/shard_map/ppermute | solution.py:29
  24.5 12.5 %copy-start.15 = (bf16[4,32,1280]{2,1,0:T(8,128)(2,1)}, bf16[4,32,1280]{2,1,0:T(8,128)(2,1)S(1)}, u32[]{:S(2)}) copy-start(bf16[4,32,1280]{2,1,0:T(8,128)(2,1)S(1)} %collective-permute-done.3.left_ref) | copy-start | bytes 983044
  24.5 19.5 %copy-start.12 = (bf16[4,32,1280]{2,1,0:T(8,128)(2,1)S(1)}, bf16[4,32,1280]{2,1,0:T(8,128)(2,1)}, u32[]{:S(2)}) copy-start(bf16[4,32,1280]{2,1,0:T(8,128)(2,1)} %copy-done.11) | copy-start | bytes 983044
  24.5 18.1 %collective-permute-start.5 = (bf16[2,32,1280]{2,1,0:T(8,128)(2,1)S(1)}, bf16[2,32,1280]{2,1,0:T(8,128)(2,1)S(1)}, u32[]{:S(2)}, u32[]{:S(2)}) collective-permute-start(bf16[2,32,1280]{2,1,0:T(8,128)(2,1)S(1)} %slice.16), channel_id=1, source_target_pairs={{0,32},{32,64},{64,96},{96,0},{1,33},{33,65},{65,97},{97,1},{2,34}... | collective-permute-start | bytes 491528 | tf_op jit(solution)/shard_map/ppermute | solution.py:29
  27.8 1.9 %copy-start.22 = (bf16[1280,1280]{1,0:T(8,128)(2,1)S(1)}, bf16[1280,1280]{1,0:T(8,128)(2,1)}, u32[]{:S(2)}) copy-start(bf16[1280,1280]{1,0:T(8,128)(2,1)} %fc2_ref.3) | copy-start | bytes 9830404
  29.8 14.3 %copy-start.23 = (bf16[1280,1280]{1,0:T(8,128)(2,1)S(1)}, bf16[1280,1280]{1,0:T(8,128)(2,1)}, u32[]{:S(2)}) copy-start(bf16[1280,1280]{1,0:T(8,128)(2,1)} %fc2_ref.3) | copy-start | bytes 9830404
  37.0 15.7 %copy-start.7 = (f32[4,32,1280]{2,1,0:T(8,128)}, f32[4,32,1280]{2,1,0:T(8,128)S(1)}, u32[]{:S(2)}) copy-start(f32[4,32,1280]{2,1,0:T(8,128)S(1)} %get-tuple-element.33.refs_0_) | copy-start | bytes 1966084
  37.0 19.0 %collective-permute-start.14 = (bf16[4,32,1280]{2,1,0:T(8,128)(2,1)S(1)}, bf16[4,32,1280]{2,1,0:T(8,128)(2,1)S(1)}, u32[]{:S(2)}, u32[]{:S(2)}) collective-permute-start(bf16[4,32,1280]{2,1,0:T(8,128)(2,1)S(1)} %get-tuple-element.34), channel_id=1, source_target_pairs={{0,32},{32,64},{64,96},{96,0},{1,33},{33,65},{65,97},{97,1},{2,34}... | collective-permute-start | bytes 983048 | tf_op jit(solution)/shard_map/ppermute | solution.py:29
  39.0 13.7 %collective-permute-start.1 = (bf16[2,96,128]{2,1,0:T(8,128)(2,1)S(1)}, bf16[2,96,128]{2,1,0:T(8,128)(2,1)S(1)}, u32[]{:S(2)}, u32[]{:S(2)}) collective-permute-start(bf16[2,96,128]{2,1,0:T(8,128)(2,1)S(1)} %shard_map.109.own_ref), channel_id=1, source_target_pairs={{0,64},{32,96},{64,0},{96,32},{1,65},{33,97},{65,1},{97,33},{2,66}... | collective-permute-start | bytes 147464 | tf_op jit(solution)/shard_map/ppermute | solution.py:29
  39.0 15.6 %collective-permute-start = (bf16[2,96,128]{2,1,0:T(8,128)(2,1)S(1)}, bf16[2,96,128]{2,1,0:T(8,128)(2,1)S(1)}, u32[]{:S(2)}, u32[]{:S(2)}) collective-permute-start(bf16[2,96,128]{2,1,0:T(8,128)(2,1)S(1)} %shard_map.109.own_ref), channel_id=1, source_target_pairs={{0,32},{32,64},{64,96},{96,0},{1,33},{33,65},{65,97},{97,1},{2,34}... | collective-permute-start | bytes 147464 | tf_op jit(solution)/shard_map/ppermute | solution.py:29
  41.8 32.6 %collective-permute-start.15 = (bf16[4,32,1280]{2,1,0:T(8,128)(2,1)}, bf16[4,32,1280]{2,1,0:T(8,128)(2,1)}, u32[]{:S(2)}, u32[]{:S(2)}) collective-permute-start(bf16[4,32,1280]{2,1,0:T(8,128)(2,1)} %get-tuple-element.35), channel_id=1, source_target_pairs={{0,64},{32,96},{64,0},{96,32},{1,65},{33,97},{65,1},{97,33},{2,66}... | collective-permute-start | bytes 983048 | tf_op jit(solution)/shard_map/ppermute | solution.py:29
  42.7 31.7 %copy-start.1 = (bf16[1280,1024]{1,0:T(8,128)(2,1)S(1)}, bf16[1280,1024]{1,0:T(8,128)(2,1)}, u32[]{:S(2)}) copy-start(bf16[1280,1024]{1,0:T(8,128)(2,1)} %refs_4_.3) | copy-start | bytes 7864324
  42.7 31.7 %collective-permute-start.16 = (bf16[4,32,1280]{2,1,0:T(8,128)(2,1)}, bf16[4,32,1280]{2,1,0:T(8,128)(2,1)}, u32[]{:S(2)}, u32[]{:S(2)}) collective-permute-start(bf16[4,32,1280]{2,1,0:T(8,128)(2,1)} %get-tuple-element.36), channel_id=1, source_target_pairs={{0,96},{32,0},{64,32},{96,64},{1,97},{33,1},{65,33},{97,65},{2,98}... | collective-permute-start | bytes 983048 | tf_op jit(solution)/shard_map/ppermute | solution.py:29
  44.0 1.0 copy-start.14
  46.0 10.8 %copy-start.24 = (s32[64,1]{0,1:T(1,128)S(1)}, s32[64,1]{0,1:T(1,128)}, u32[]{:S(2)}) copy-start(s32[64,1]{0,1:T(1,128)} %param.14) | copy-start | bytes 772
  46.0 10.9 %copy-start.19 = (s32[32]{0:T(128)S(1)}, s32[32]{0:T(128)}, u32[]{:S(2)}) copy-start(s32[32]{0:T(128)} %param.12) | copy-start | bytes 388
  46.0 10.9 %copy-start.20 = (s32[64]{0:T(128)S(1)}, s32[64]{0:T(128)}, u32[]{:S(2)}) copy-start(s32[64]{0:T(128)} %param.13) | copy-start | bytes 772
  52.7 30.1 %collective-permute-start.7 = (bf16[4,32,1280]{2,1,0:T(8,128)(2,1)}, bf16[4,32,1280]{2,1,0:T(8,128)(2,1)}, u32[]{:S(2)}, u32[]{:S(2)}) collective-permute-start(bf16[4,32,1280]{2,1,0:T(8,128)(2,1)} %get-tuple-element.29), channel_id=1, source_target_pairs={{0,32},{32,64},{64,96},{96,0},{1,33},{33,65},{65,97},{97,1},{2,34}... | collective-permute-start | bytes 983048 | tf_op jit(solution)/shard_map/ppermute | solution.py:29
  54.6 28.2 %collective-permute-start.8 = (bf16[4,32,1280]{2,1,0:T(8,128)(2,1)}, bf16[4,32,1280]{2,1,0:T(8,128)(2,1)}, u32[]{:S(2)}, u32[]{:S(2)}) collective-permute-start(bf16[4,32,1280]{2,1,0:T(8,128)(2,1)} %get-tuple-element.30), channel_id=1, source_target_pairs={{0,64},{32,96},{64,0},{96,32},{1,65},{33,97},{65,1},{97,33},{2,66}... | collective-permute-start | bytes 983048 | tf_op jit(solution)/shard_map/ppermute | solution.py:29
  56.7 26.1 %collective-permute-start.9 = (bf16[4,32,1280]{2,1,0:T(8,128)(2,1)}, bf16[4,32,1280]{2,1,0:T(8,128)(2,1)}, u32[]{:S(2)}, u32[]{:S(2)}) collective-permute-start(bf16[4,32,1280]{2,1,0:T(8,128)(2,1)} %get-tuple-element.31), channel_id=1, source_target_pairs={{0,96},{32,0},{64,32},{96,64},{1,97},{33,1},{65,33},{97,65},{2,98}... | collective-permute-start | bytes 983048 | tf_op jit(solution)/shard_map/ppermute | solution.py:29
  74.3 1.7 %copy-start.2 = (bf16[1280,1024]{1,0:T(8,128)(2,1)S(1)}, bf16[1280,1024]{1,0:T(8,128)(2,1)}, u32[]{:S(2)}) copy-start(bf16[1280,1024]{1,0:T(8,128)(2,1)} %refs_5_.3) | copy-start | bytes 7864324
  76.1 1.1 copy-start.8
  82.8 30.1 %copy-start = (bf16[256,8192]{1,0:T(8,128)(2,1)S(1)}, bf16[256,8192]{1,0:T(8,128)(2,1)}, u32[]{:S(2)}) copy-start(bf16[256,8192]{1,0:T(8,128)(2,1)} %weight_ref.5) | copy-start | bytes 12582916
  101.4 7.9 %collective-permute-start.17 = (bf16[192,256]{1,0:T(8,128)(2,1)S(1)}, bf16[192,256]{1,0:T(8,128)(2,1)S(1)}, u32[]{:S(2)}, u32[]{:S(2)}) collective-permute-start(bf16[192,256]{1,0:T(8,128)(2,1)S(1)} %get-tuple-element.38), channel_id=1, source_target_pairs={{0,32},{32,64},{64,96},{96,0},{1,33},{33,65},{65,97},{97,1},{2,34}... | collective-permute-start | bytes 294920 | tf_op jit(solution)/shard_map/ppermute | solution.py:29
  104.7 7.2 %collective-permute-start.18 = (bf16[192,256]{1,0:T(8,128)(2,1)S(1)}, bf16[192,256]{1,0:T(8,128)(2,1)S(1)}, u32[]{:S(2)}, u32[]{:S(2)}) collective-permute-start(bf16[192,256]{1,0:T(8,128)(2,1)S(1)} %get-tuple-element.39), channel_id=1, source_target_pairs={{0,64},{32,96},{64,0},{96,32},{1,65},{33,97},{65,1},{97,33},{2,66}... | collective-permute-start | bytes 294920 | tf_op jit(solution)/shard_map/ppermute | solution.py:29
  105.6 7.4 %collective-permute-start.19 = (bf16[192,256]{1,0:T(8,128)(2,1)S(1)}, bf16[192,256]{1,0:T(8,128)(2,1)S(1)}, u32[]{:S(2)}, u32[]{:S(2)}) collective-permute-start(bf16[192,256]{1,0:T(8,128)(2,1)S(1)} %get-tuple-element.40), channel_id=1, source_target_pairs={{0,96},{32,0},{64,32},{96,64},{1,97},{33,1},{65,33},{97,65},{2,98}... | collective-permute-start | bytes 294920 | tf_op jit(solution)/shard_map/ppermute | solution.py:29
  115.1 2.4 %collective-permute-start.20 = (bf16[4,4,96,256]{3,2,1,0:T(8,128)(2,1)S(1)}, bf16[4,4,96,256]{3,2,1,0:T(8,128)(2,1)S(1)}, u32[]{:S(2)}, u32[]{:S(2)}) collective-permute-start(bf16[4,4,96,256]{3,2,1,0:T(8,128)(2,1)S(1)} %shard_map.119), channel_id=1, source_target_pairs={{0,1},{1,0},{2,3},{3,2},{4,5},{5,4},{6,7},{7,6},{8,9},{9,8},{10,11... | collective-permute-start | bytes 2359304 | tf_op jit(solution)/shard_map/ppermute | solution.py:39
  117.6 12.6 %collective-permute-start.21 = (bf16[4,96,256]{2,1,0:T(8,128)(2,1)S(1)}, bf16[4,96,256]{2,1,0:T(8,128)(2,1)S(1)}, u32[]{:S(2)}, u32[]{:S(2)}) collective-permute-start(bf16[4,96,256]{2,1,0:T(8,128)(2,1)S(1)} %get-tuple-element.42), channel_id=1, source_target_pairs={{0,8},{1,9},{2,10},{3,11},{4,12},{5,13},{6,14},{7,15},{8,16},{9,17... | collective-permute-start | bytes 589832 | tf_op jit(solution)/shard_map/ppermute | solution.py:39
  118.3 11.9 %collective-permute-start.22 = (bf16[4,96,256]{2,1,0:T(8,128)(2,1)S(1)}, bf16[4,96,256]{2,1,0:T(8,128)(2,1)S(1)}, u32[]{:S(2)}, u32[]{:S(2)}) collective-permute-start(bf16[4,96,256]{2,1,0:T(8,128)(2,1)S(1)} %get-tuple-element.43), channel_id=1, source_target_pairs={{0,16},{1,17},{2,18},{3,19},{4,20},{5,21},{6,22},{7,23},{8,24},{9,... | collective-permute-start | bytes 589832 | tf_op jit(solution)/shard_map/ppermute | solution.py:39
  120.3 10.6 %collective-permute-start.23 = (bf16[4,96,256]{2,1,0:T(8,128)(2,1)S(1)}, bf16[4,96,256]{2,1,0:T(8,128)(2,1)S(1)}, u32[]{:S(2)}, u32[]{:S(2)}) collective-permute-start(bf16[4,96,256]{2,1,0:T(8,128)(2,1)S(1)} %get-tuple-element.44), channel_id=1, source_target_pairs={{0,24},{1,25},{2,26},{3,27},{4,28},{5,29},{6,30},{7,31},{8,0},{9,1... | collective-permute-start | bytes 589832 | tf_op jit(solution)/shard_map/ppermute | solution.py:39
  130.9 5.4 %collective-permute-start.24 = (bf16[96,256]{1,0:T(8,128)(2,1)S(1)}, bf16[96,256]{1,0:T(8,128)(2,1)S(1)}, u32[]{:S(2)}, u32[]{:S(2)}) collective-permute-start(bf16[96,256]{1,0:T(8,128)(2,1)S(1)} %get-tuple-element.46), channel_id=1, source_target_pairs={{0,2},{1,3},{2,4},{3,5},{4,6},{5,7},{6,0},{7,1},{8,10},{9,11},{10,... | collective-permute-start | bytes 147464 | tf_op jit(solution)/shard_map/ppermute | solution.py:39
  131.8 5.6 %collective-permute-start.25 = (bf16[96,256]{1,0:T(8,128)(2,1)S(1)}, bf16[96,256]{1,0:T(8,128)(2,1)S(1)}, u32[]{:S(2)}, u32[]{:S(2)}) collective-permute-start(bf16[96,256]{1,0:T(8,128)(2,1)S(1)} %get-tuple-element.47), channel_id=1, source_target_pairs={{0,4},{1,5},{2,6},{3,7},{4,0},{5,1},{6,2},{7,3},{8,12},{9,13},{10,... | collective-permute-start | bytes 147464 | tf_op jit(solution)/shard_map/ppermute | solution.py:39
  133.9 4.1 %collective-permute-start.26 = (bf16[96,256]{1,0:T(8,128)(2,1)S(1)}, bf16[96,256]{1,0:T(8,128)(2,1)S(1)}, u32[]{:S(2)}, u32[]{:S(2)}) collective-permute-start(bf16[96,256]{1,0:T(8,128)(2,1)S(1)} %get-tuple-element.48), channel_id=1, source_target_pairs={{0,6},{1,7},{2,0},{3,1},{4,2},{5,3},{6,4},{7,5},{8,14},{9,15},{10,... | collective-permute-start | bytes 147464 | tf_op jit(solution)/shard_map/ppermute | solution.py:39
  (4 other events, 3.5 us)

commit v2 on v1

v2 whole, which is shorter than its diff:
```python
import functools

import jax
import jax.numpy as jnp
from jax import lax
from jax.experimental import pallas as pl
from jax.experimental.pallas import tpu as pltpu
from jax.sharding import PartitionSpec as P

HEADS = 64
KV_HEADS = 8
HEAD_DIM = 128
CORES = 2
RING = 4
BLOCK = 256
TOTAL_ROWS = 16
F32, BF16 = jnp.float32, jnp.bfloat16

epsilon = 1e-05

VMEM = pl.BlockSpec(memory_space=pltpu.VMEM)
SMEM = pl.BlockSpec(memory_space=pltpu.SMEM)


def params(mib):
    return pltpu.CompilerParams(vmem_limit_bytes=mib * 1024 * 1024)


def pool_shift(x, by):
    return lax.ppermute(x, "pool", [(i, (i + by) % RING) for i in range(RING)])


def dev_shift(x, by_z, by_y, by_core):
    pairs = []
    for z in range(RING):
        for y in range(RING):
            for k in range(CORES):
                to = ((z + by_z) % RING, (y + by_y) % RING, (k + by_core) % CORES)
                pairs.append(((z * RING + y) * CORES + k, (to[0] * RING + to[1]) * CORES + to[2]))
    return lax.ppermute(x, "dev", pairs)


def layer_rows(values):
    center = values - jnp.mean(values, axis=-1, keepdims=True)
    spread = jnp.mean(center * center, axis=-1, keepdims=True)
    return (center / jnp.sqrt(spread + epsilon)).astype(BF16)


def normalize_kernel(half, at_ref, patches_ref, rows_ref):
    for r in range(RING):
        slot = lax.rem(at_ref[0] + r, RING) + half * RING
        rows_ref[r] = layer_rows(patches_ref[slot].astype(F32))


def normalize(at, patches):
    _, quarter, width = patches.shape
    return pl.pallas_call(
        functools.partial(normalize_kernel, 0),
        out_shape=jax.ShapeDtypeStruct((RING, quarter, width), BF16),
        in_specs=[SMEM, VMEM],
        out_specs=VMEM,
        compiler_params=params(8),
    )(at, patches)


def hold_kernel(one_ref, two_ref, _, out_ref):
    out_ref[...] = jnp.zeros_like(out_ref)


def hold(one, two, after):
    return pl.pallas_call(
        hold_kernel,
        out_shape=jax.ShapeDtypeStruct((8, 128), F32),
        in_specs=[VMEM, VMEM, pl.BlockSpec(memory_space=pl.ANY)],
        out_specs=VMEM,
        compiler_params=params(8),
    )(one, two, after)


def feed_forward_kernel(
    half, at_ref, patches_ref, own_rows, one_rows, two_rows, three_rows, fc1_ref, fc2_ref, *refs
):
    total_ref, one_ref, two_ref, three_ref, rows_ref, wide_ref = refs[-6:]
    hidden, width = fc2_ref.shape
    quarter = patches_ref.shape[1]
    rows = RING * quarter
    for source, ref in enumerate((own_rows, one_rows, two_rows, three_rows)):
        rows_ref[source * rows : (source + 1) * rows] = ref[:RING].reshape(rows, width)
    for step in range(hidden // BLOCK):
        at = slice(step * BLOCK, (step + 1) * BLOCK)
        values = jnp.dot(rows_ref[...], fc1_ref[:, at], preferred_element_type=F32)
        wide_ref[:, at] = (0.5 * values * (1.0 + lax.erf(values * 0.5**0.5))).astype(BF16)
    outs = (total_ref, one_ref, two_ref, three_ref)
    for step in range(width // BLOCK):
        at = slice(step * BLOCK, (step + 1) * BLOCK)
        sums = jnp.dot(wide_ref[...], fc2_ref[:, at], preferred_element_type=F32)
        for source in range(RING):
            for m in range(RING):
                piece = sums[source * rows + m * quarter : source * rows + (m + 1) * quarter]
                shift = (m - source) % RING
                if source == 0:
                    slot = lax.rem(at_ref[0] + m, RING) + half * RING
                    piece = piece + patches_ref[slot, :, at].astype(F32)
                outs[shift][m, :, at] = piece.astype(outs[shift].dtype)


def feed_forward(at, patches, sources, fc1, fc2, half, after):
    _, quarter, width = patches.shape
    hidden = fc1.shape[1]
    shape = (RING, quarter, width)
    sent = jax.ShapeDtypeStruct(shape, BF16)
    return pl.pallas_call(
        functools.partial(feed_forward_kernel, half),
        out_shape=(sent,) * 4,
        in_specs=[SMEM] + [VMEM] * (7 + len(after)),
        out_specs=(VMEM,) * 4,
        scratch_shapes=[
            pltpu.VMEM((RING * RING * quarter, width), BF16),
            pltpu.VMEM((RING * RING * quarter, hidden), BF16),
        ],
        compiler_params=params(14),
        cost_estimate=pl.CostEstimate(
            flops=4 * RING * RING * quarter * width * hidden,
            bytes_accessed=4 * width * hidden,
            transcendentals=0,
        ),
    )(at, patches, *sources, fc1, fc2, *after)


def query_kernel(at_ref, text_ref, weight_ref, patches_ref, sent_ref, total_ref, square_ref):
    step = pl.program_id(0)
    rows, columns = total_ref.shape

    @pl.when(step == 0)
    def _():
        total_ref[...] = jnp.zeros_like(total_ref)
        square_ref[...] = jnp.zeros_like(square_ref)

    slot = lax.rem(at_ref[0] + step, RING) + RING
    sent_ref[step] = layer_rows(patches_ref[slot].astype(F32))
    text = text_ref[...].reshape(rows, text_ref.shape[-1])
    total_ref[...] += jnp.dot(text, weight_ref[...], preferred_element_type=F32)
    wide = text.astype(F32)
    square_ref[...] += jnp.sum(wide * wide, axis=-1, keepdims=True)

    @pl.when(step == pl.num_programs(0) - 1)
    def _():
        width = text_ref.shape[-1] * pl.num_programs(0)
        values = total_ref[...] / jnp.sqrt(square_ref[...] / width + epsilon)
        quarter = sent_ref.shape[1]
        for head in range(columns // HEAD_DIM):
            part = values[:, head * HEAD_DIM : (head + 1) * HEAD_DIM]
            mean = jnp.mean(part * part, axis=-1, keepdims=True)
            part = (part / jnp.sqrt(mean + epsilon)).astype(BF16)
            for piece in range(rows // quarter):
                lane = (head * (rows // quarter) + piece) * HEAD_DIM
                sent_ref[RING, :, lane : lane + HEAD_DIM] = part[
                    piece * quarter : (piece + 1) * quarter
                ]
        filled = columns // HEAD_DIM * (rows // quarter) * HEAD_DIM
        sent_ref[RING, :, filled:] = jnp.zeros((quarter, sent_ref.shape[2] - filled), BF16)


def second_half(at, text, weight, patches):
    slots, steps, model = text.shape
    rows = slots * steps
    _, quarter, width = patches.shape
    columns = weight.shape[1]
    depth = model // RING
    return pl.pallas_call(
        query_kernel,
        grid=(RING,),
        out_shape=jax.ShapeDtypeStruct((RING + 1, quarter, width), BF16),
        in_specs=[
            SMEM,
            pl.BlockSpec((slots, steps, depth), lambda k: (0, 0, k)),
            pl.BlockSpec((depth, columns), lambda k: (k, 0)),
            pl.BlockSpec(patches.shape, lambda k: (0, 0, 0)),
        ],
        out_specs=pl.BlockSpec((RING + 1, quarter, width), lambda k: (0, 0, 0)),
        scratch_shapes=[pltpu.VMEM((rows, columns), F32), pltpu.VMEM((rows, 1), F32)],
        compiler_params=params(12),
        cost_estimate=pl.CostEstimate(
            flops=2 * rows * model * columns,
            bytes_accessed=2 * model * (columns + rows),
            transcendentals=0,
        ),
    )(at, text, weight, patches)


def iota(shape, dim):
    return lax.broadcasted_iota(jnp.int32, shape, dim)


def select_kernel(
    slots, steps, heads, capacity, at_ref, enc_ref, req_ref, owner_ref,
    *refs,
):
    *sources, chosen_ref, target_ref = refs
    here = at_ref[0]
    columns, requests = enc_ref.shape[1], req_ref.shape[1]
    halves = capacity // RING
    per_group = heads * slots * steps
    rows = columns * halves * heads * steps
    before = iota((requests, requests), 0) < iota((requests, requests), 1)
    equal = iota((requests, requests), 0) == iota((requests, requests), 1)
    req_row = req_ref[...]
    req_column = jnp.sum(jnp.where(equal, req_row, 0), axis=1, keepdims=True)
    req_start = jnp.sum(jnp.where(before, req_column, 0), axis=0, keepdims=True)
    owner_column = owner_ref[...]
    owner_row = jnp.sum(jnp.where(equal, owner_column, 0), axis=0, keepdims=True)
    rank = jnp.sum(
        jnp.where(before & (owner_column == owner_row), 1, 0), axis=0, keepdims=True
    )
    place = owner_row * per_group + rank * steps
    enc_row = enc_ref[...]
    enc_equal = iota((columns, columns), 0) == iota((columns, columns), 1)
    enc_before = iota((columns, columns), 0) < iota((columns, columns), 1)
    enc_column = jnp.sum(jnp.where(enc_equal, enc_row, 0), axis=1, keepdims=True)
    enc_start = jnp.sum(jnp.where(enc_before, enc_column, 0), axis=0, keepdims=True)

    row = iota((rows, 1), 0)
    per_tile = heads * steps
    column = row // (halves * per_tile)
    slot = row // per_tile % halves * RING + here
    hit = column == iota((rows, columns), 1)
    count = jnp.sum(jnp.where(hit, enc_row, 0), axis=1, keepdims=True)
    start = jnp.sum(jnp.where(hit, enc_start, 0), axis=1, keepdims=True)
    tile = jnp.where(slot < count, start + slot, -1)
    has = (req_start <= tile) & (tile < req_start + req_row)
    base = jnp.sum(jnp.where(has, place + 1, 0), axis=1, keepdims=True) - 1
    within = row % per_tile
    target = jnp.where(base < 0, -1, base + within // steps * (slots * steps) + within % steps)
    target_ref[...] = target
    chosen = jnp.zeros((rows, HEAD_DIM), F32)
    for shift in range(RING):
        group = lax.rem(here - shift + RING, RING)
        ref = sources[0].at[group] if len(sources) == 1 else sources[shift]
        match = target == iota((rows, per_group), 1) + group * per_group
        chosen = chosen + jnp.dot(
            jnp.where(match, 1.0, 0.0).astype(BF16),
            jnp.concatenate(
                [
                    ref[RING, :, lane : lane + HEAD_DIM]
                    for lane in range(0, per_group // ref.shape[1] * HEAD_DIM, HEAD_DIM)
                ],
                axis=0,
            ),
            preferred_element_type=F32,
        )
    chosen_ref[...] = chosen.astype(BF16)


def select(at, enc, req, owner, queries, slots, steps, heads, capacity):
    rows = enc.shape[1] * (capacity // RING) * heads * steps
    return pl.pallas_call(
        functools.partial(select_kernel, slots, steps, heads, capacity),
        out_shape=(
            jax.ShapeDtypeStruct((rows, HEAD_DIM), BF16),
            jax.ShapeDtypeStruct((rows, 1), jnp.int32),
        ),
        in_specs=[SMEM] + [VMEM] * (3 + len(queries)),
        out_specs=(VMEM, VMEM),
        compiler_params=params(8),
    )(at, enc, req, owner, *queries)


def attend_kernel(half, total_ref, one_ref, two_ref, three_ref, key_ref, value_ref, query_ref, *refs):
    out_ref = refs[-1]
    _, quarter, width = total_ref.shape
    summed = total_ref[...].astype(F32)
    for ref in (one_ref, two_ref, three_ref):
        summed = summed + ref[...].astype(F32)
    vision = summed.astype(BF16).reshape(RING * quarter, width)
    heads, per_head, per_device, _ = query_ref.shape
    count = per_head * per_device
    mine = iota((count, 1), 0) % per_device // (per_device // 2) == half
    together = BLOCK // HEAD_DIM
    for pair in range(heads // together):
        at = slice(pair * BLOCK, (pair + 1) * BLOCK)
        keys = jnp.dot(vision, key_ref[:, at], preferred_element_type=F32)
        values = jnp.dot(vision, value_ref[:, at], preferred_element_type=F32).astype(BF16)
        for place in range(together):
            head = pair * together + place
            at = slice(place * HEAD_DIM, (place + 1) * HEAD_DIM)
            key = keys[:, at]
            mean = jnp.mean(key * key, axis=-1, keepdims=True)
            key = (key / jnp.sqrt(mean + epsilon)).astype(BF16)
            query = query_ref[head].reshape(count, HEAD_DIM)
            scores = lax.dot_general(
                query, key, (((1,), (1,)), ((), ())), preferred_element_type=F32
            ) * HEAD_DIM ** (-0.5)
            weights = jnp.where(mine, jnp.exp(scores), 0.0)
            divisor = jnp.sum(weights, axis=-1, keepdims=True)
            numerator = jnp.dot(weights.astype(BF16), values[:, at], preferred_element_type=F32)
            packed = jnp.concatenate(
                [numerator, jnp.broadcast_to(divisor, numerator.shape)], axis=1
            ).reshape(per_head, per_device, 2 * HEAD_DIM)
            if len(refs) > 1:
                packed = packed + refs[0][head].astype(F32)
            out_ref[head] = packed.astype(BF16)


def attend(total, received, key_weight, value_weight, queries, half, before):
    _, quarter, width = total.shape
    heads, per_head, per_device, _ = queries.shape
    columns = key_weight.shape[1]
    before = [] if before is None else [before]
    return pl.pallas_call(
        functools.partial(attend_kernel, half),
        out_shape=jax.ShapeDtypeStruct((heads, per_head, per_device, 2 * HEAD_DIM), BF16),
        in_specs=[VMEM] * (7 + len(before)),
        out_specs=VMEM,
        compiler_params=params(12),
        cost_estimate=pl.CostEstimate(
            flops=4 * RING * quarter * width * columns,
            bytes_accessed=4 * width * columns,
            transcendentals=0,
        ),
    )(total, *received, key_weight, value_weight, queries, *before)


def combine_kernel(at_ref, target_ref, packed_ref, own_ref, one_ref, two_ref, three_ref):
    target = target_ref[...]
    per_group = own_ref.shape[0] - TOTAL_ROWS
    for shift, ref in enumerate((own_ref, one_ref, two_ref, three_ref)):
        group = lax.rem(at_ref[0] + shift, RING)
        match = target == iota((target.shape[0], per_group), 1) + group * per_group
        summed = lax.dot_general(
            jnp.where(match, 1.0, 0.0).astype(BF16),
            packed_ref[...],
            (((0,), (0,)), ((), ())),
            preferred_element_type=F32,
        )
        ref[:per_group] = summed[:, :HEAD_DIM].astype(ref.dtype)
        totals = jnp.zeros((TOTAL_ROWS, HEAD_DIM), F32)
        for row, first in enumerate(range(0, per_group, HEAD_DIM)):
            part = summed[first : first + HEAD_DIM, HEAD_DIM:]
            lane = iota(part.shape, 0) == iota(part.shape, 1)
            part = jnp.sum(jnp.where(lane, part, 0.0), axis=0, keepdims=True)
            totals = jnp.where(iota(totals.shape, 0) == row, part, totals)
        ref[per_group:] = totals.astype(ref.dtype)


def combine(at, target, packed, per_group):
    shape = (per_group + TOTAL_ROWS, HEAD_DIM)
    sent = jax.ShapeDtypeStruct(shape, BF16)
    return pl.pallas_call(
        combine_kernel,
        out_shape=(jax.ShapeDtypeStruct(shape, F32), sent, sent, sent),
        in_specs=[SMEM, VMEM, VMEM],
        out_specs=(VMEM,) * 4,
        compiler_params=params(8),
    )(at, target, packed)


def project_kernel(core, at_ref, own_ref, one_ref, two_ref, three_ref, weight_ref, out_ref):
    summed = own_ref[...]
    for ref in (one_ref, two_ref, three_ref):
        summed = summed + ref[...].astype(F32)
    per_group = summed.shape[0] - TOTAL_ROWS
    attended = []
    for row, first in enumerate(range(0, per_group, HEAD_DIM)):
        part = summed[first : min(first + HEAD_DIM, per_group)]
        totals = jnp.broadcast_to(summed[per_group + row : per_group + row + 1], part.shape)
        lane = iota(part.shape, 0) == iota(part.shape, 1)
        divisor = jnp.sum(jnp.where(lane, totals, 0.0), axis=1, keepdims=True)
        attended.append(part / jnp.where(divisor > 0.0, divisor, 1.0))
    attended = jnp.concatenate(attended, axis=0)
    half = per_group // 2
    attended = jnp.concatenate([attended[:half], attended[half:]], axis=1).astype(BF16)
    here = at_ref[1]
    z_at, y_at, core_at = here // (RING * CORES), here // CORES % RING, here % CORES
    column = lax.rem(core_at + core, CORES)
    for z in range(RING):
        for y in range(RING):
            block = (
                lax.rem(z_at + z, RING) * RING + lax.rem(y_at + y, RING)
            ) * CORES + column
            at = pl.ds(pl.multiple_of(block * BLOCK, BLOCK), BLOCK)
            out_ref[z, y] = jnp.dot(
                attended, weight_ref[:, at], preferred_element_type=F32
            ).astype(BF16)


def project(at, own, received, weight, core):
    depth, columns = weight.shape
    rows = (own.shape[0] - TOTAL_ROWS) // 2
    return pl.pallas_call(
        functools.partial(project_kernel, core),
        out_shape=jax.ShapeDtypeStruct((RING, RING, rows, BLOCK), BF16),
        in_specs=[SMEM] + [VMEM] * 5,
        out_specs=VMEM,
        compiler_params=params(8),
        cost_estimate=pl.CostEstimate(
            flops=rows * depth * columns, bytes_accessed=2 * depth * columns, transcendentals=0
        ),
    )(at, own, *received, weight)


def first_sum_kernel(kept_ref, got_ref, own_ref, one_ref, two_ref, three_ref):
    for shift, ref in enumerate((own_ref, one_ref, two_ref, three_ref)):
        ref[...] = (kept_ref[shift].astype(F32) + got_ref[shift].astype(F32)).astype(ref.dtype)


def first_sum(kept, got):
    sent = jax.ShapeDtypeStruct(kept.shape[1:], BF16)
    return pl.pallas_call(
        first_sum_kernel,
        out_shape=(jax.ShapeDtypeStruct(kept.shape[1:], F32), sent, sent, sent),
        in_specs=[VMEM, VMEM],
        out_specs=(VMEM,) * 4,
        compiler_params=params(8),
    )(kept, got)


def second_sum_kernel(kept_ref, a_ref, b_ref, c_ref, own_ref, one_ref, two_ref, three_ref):
    for shift, ref in enumerate((own_ref, one_ref, two_ref, three_ref)):
        summed = kept_ref[shift]
        for got in (a_ref, b_ref, c_ref):
            summed = summed + got[shift].astype(F32)
        ref[...] = summed.astype(ref.dtype)


def second_sum(kept, got):
    sent = jax.ShapeDtypeStruct(kept.shape[1:], BF16)
    return pl.pallas_call(
        second_sum_kernel,
        out_shape=(jax.ShapeDtypeStruct(kept.shape[1:], F32), sent, sent, sent),
        in_specs=[VMEM] * 4,
        out_specs=(VMEM,) * 4,
        compiler_params=params(8),
    )(kept, *got)


def last_sum_kernel(kept_ref, a_ref, b_ref, c_ref, residual_ref, out_ref):
    summed = kept_ref[...]
    for got in (a_ref, b_ref, c_ref):
        summed = summed + got[...].astype(F32)
    out_ref[...] = (residual_ref[...].astype(F32) + summed.reshape(out_ref.shape)).astype(BF16)


def last_sum(kept, got, residual):
    return pl.pallas_call(
        last_sum_kernel,
        out_shape=jax.ShapeDtypeStruct(residual.shape, BF16),
        in_specs=[VMEM] * 5,
        out_specs=VMEM,
        compiler_params=params(8),
    )(kept, *got, residual)


def body(
    patches,
    enc_tiles,
    req_tiles,
    req_owner,
    fc1_weight,
    fc2_weight,
    key_weight,
    value_weight,
    query_weight,
    out_weight,
    text_hidden,
):
    capacity = patches.shape[0]
    devices = lax.axis_size("dev")
    local_heads = HEADS // devices
    slots, steps, model_width = text_hidden.shape
    dev_at = lax.axis_index("dev")
    at = jnp.stack([lax.axis_index("pool"), dev_at]).astype(jnp.int32)
    halves = capacity // RING

    own = [normalize(at, patches), second_half(at, text_hidden, query_weight, patches)]
    sources = [[rows] + [pool_shift(rows, s) for s in range(1, RING)] for rows in own]
    chosen, target = select(
        at,
        enc_tiles.reshape(1, -1),
        req_tiles.reshape(1, -1),
        req_owner,
        sources[1],
        slots,
        steps,
        local_heads,
        capacity,
    )
    per_device = halves * local_heads * steps
    tile_queries = lax.all_to_all(
        chosen.reshape(devices, per_device, HEAD_DIM), "dev", split_axis=0, concat_axis=0, tiled=True
    ).reshape(KV_HEADS, devices // KV_HEADS, per_device, HEAD_DIM)

    held = hold(fc1_weight, fc2_weight, sources[1][0])
    packed = None
    for i in range(halves):
        total, *messages = feed_forward(
            at, patches, sources[i], fc1_weight, fc2_weight, i,
            (held,),
        )
        received = [pool_shift(messages[s - 1], s) for s in range(1, RING)]
        packed = attend(total, received, key_weight, value_weight, tile_queries, i, packed)
    packed = lax.all_to_all(
        packed.reshape(devices, per_device, 2 * HEAD_DIM),
        "dev",
        split_axis=0,
        concat_axis=0,
        tiled=True,
    ).reshape(devices * per_device, 2 * HEAD_DIM)
    summed, *messages = combine(at, target, packed, local_heads * slots * steps)
    received = [pool_shift(messages[s - 1], s) for s in range(1, RING)]

    away = dev_shift(project(at, summed, received, out_weight, 1), 0, 0, 1)
    kept = project(at, summed, received, out_weight, 0)
    kept, *messages = first_sum(kept, away)
    received = [dev_shift(messages[s - 1], s, 0, 0) for s in range(1, RING)]
    kept, *messages = second_sum(kept, received)
    received = [dev_shift(messages[s - 1], 0, s, 0) for s in range(1, RING)]
    width_out = model_width // devices
    residual = lax.dynamic_slice_in_dim(text_hidden, dev_at * width_out, width_out, 2)
    return last_sum(kept, received, residual)


def solution(mesh):
    return jax.shard_map(
        body,
        mesh=mesh,
        in_specs=(
            P("dev", "pool", None),
            P(),
            P(),
            P(),
            P(None, "pool"),
            P("pool", None),
            P(),
            P(),
            P(None, "dev"),
            P("dev", None),
            P("pool", None, None),
        ),
        out_specs=P("pool", None, "dev"),
        check_vma=False,
    )
```

time: 139 us -> 128 us (0.921)
  Pallas kernels: 34.1 us -> 26.6 us
  local copies, waits for them, and re-layouts: 16.4 us -> 13.8 us
    pallas_call x10, Pallas kernels: 31.1 us -> 23.6 us  [the longest x2 10.3 us: feed_forward(): pl.pallas_call(functools.partial(feed_forward_kernel, half), out_shape=(s...]
    reshape x2 -> x0, local copies, waits for them, and re-layouts: 2.99 us -> none  [the longest x1 2.35 us: body(): text = text_hidden.reshape(slots * steps, model_width)]
    ppermute x20 -> x15, waiting for transfers between devices: 11.7 us -> 10.5 us  [pool_shift(): return lax.ppermute(x, 'pool', [(i, (i + by) % RING) for i in range(RING)])]
    unnamed x51 -> x45, local copies, waits for them, and re-layouts: 11.9 us -> 13 us
    ppermute x20 -> x15, starting transfers between devices: 27.9 us -> 27.2 us  [pool_shift(): return lax.ppermute(x, 'pool', [(i, (i + by) % RING) for i in range(RING)])]
  transfers between devices with their start and end apart: 27 -> 22, of which waited for: 10 -> 11; matrix products, arithmetic and copies ran while one was open for 3% -> 1% of each run, Pallas kernels for 18% -> 15%
where the time goes in v2:
time: 128 us; the launch traced here: 127 us
  starting transfers between devices  35.1 us (27%)
  blocking collectives  28.3 us (22%)
  Pallas kernels  26.6 us (21%)
  waiting for transfers between devices  23.2 us (18%)
  local copies, waits for them, and re-layouts  13.8 us (11%)
    ppermute x15, starting transfers between devices, pool_shift(): return lax.ppermute(x, 'pool', [(i, (i + by) % RING) for i in range(RING)])  27.2 us
    all_to_all x1, blocking collectives, body(): lax.all_to_all(chosen.reshape(devices, per_device, HEAD_DIM), 'dev', spli...  15.9 us
    unnamed x45, local copies, waits for them, and re-layouts  13 us
    ppermute x7, waiting for transfers between devices, dev_shift(): return lax.ppermute(x, 'dev', pairs)  12.7 us
    all_to_all x1, blocking collectives, body(): lax.all_to_all(packed.reshape(devices, per_device, 2 * HEAD_DIM), 'dev',...  12.4 us
    ppermute x15, waiting for transfers between devices, pool_shift(): return lax.ppermute(x, 'pool', [(i, (i + by) % RING) for i in range(RING)])  10.5 us
    pallas_call x2, Pallas kernels, feed_forward(): pl.pallas_call(functools.partial(feed_forward_kernel, half), out_shape=(s...  10.3 us
    ppermute x7, starting transfers between devices, dev_shift(): return lax.ppermute(x, 'dev', pairs)  7.88 us
  transfers between devices with their start and end apart: 22, of which 11 were waited for; matrix products, arithmetic and copies ran while one was open for 1% of the time, Pallas kernels for 15%

profile of v2, /device:TPU:6, one launch (start us, length us, event | category | flops | bytes accessed | tf_op | source)
XLA Modules:
  0.0 127.3 jit_solution(8656202321062489250)
XLA Ops:
  0.1 1.1 copy-done.6
  1.2 0.8 shard_map.113.own_rows
  2.5 2.5 %collective-permute-start.7 = (bf16[4,32,1280]{2,1,0:T(8,128)(2,1)S(1)}, bf16[4,32,1280]{2,1,0:T(8,128)(2,1)S(1)}, u32[]{:S(2)}, u32[]{:S(2)}) collective-permute-start(bf16[4,32,1280]{2,1,0:T(8,128)(2,1)S(1)} %shard_map.113.own_rows), channel_id=1, source_target_pairs={{0,64},{32,96},{64,0},{96,32},{1,65},{33,97},{65,1},{97,33},{2,66}... | collective-permute-start | bytes 983048 | tf_op jit(solution)/shard_map/ppermute | solution.py:30
  5.0 2.2 %copy-done.3 = bf16[8192,256]{1,0:T(8,128)(2,1)S(1)} copy-done((bf16[8192,256]{1,0:T(8,128)(2,1)S(1)}, bf16[8192,256]{1,0:T(8,128)(2,1)}, u32[]{:S(2)}) %copy-start.3) | copy-done | bytes 4194328
  7.2 1.1 copy-done.7
  8.2 1.4 %copy-done.8 = bf16[24,4,8192]{2,1,0:T(4,128)(2,1)S(1)} copy-done((bf16[24,4,8192]{2,1,0:T(4,128)(2,1)S(1)}, bf16[24,4,8192]{2,1,0:T(4,128)(2,1)}, u32[]{:S(2)}) %copy-start.8) | copy-done | bytes 1572888
  9.7 2.2 %shard_map.109.refs_0_._.own_rows = bf16[5,32,1280]{2,1,0:T(8,128)(2,1)S(1)} custom-call(s32[2]{0:T(128)S(1)} %pad_add_fusion.at_ref, bf16[24,4,8192]{2,1,0:T(4,128)(2,1)S(1)} %copy-done.8, bf16[8192,256]{1,0:T(8,128)(2,1)S(1)} %copy-done.3, bf16[8,32,1280]{2,1,0:T(8,128)(2,1)S(1)} %copy-done.7), custom_call_target="tpu_custom_call" | custom-call | flops 402653184 | bytes 5767168 | tf_op jit(solution)/shard_map/pallas_call | solution.py:170
  11.9 3.3 %collective-permute-start = (bf16[5,32,1280]{2,1,0:T(8,128)(2,1)S(1)}, bf16[5,32,1280]{2,1,0:T(8,128)(2,1)S(1)}, u32[]{:S(2)}, u32[]{:S(2)}) collective-permute-start(bf16[5,32,1280]{2,1,0:T(8,128)(2,1)S(1)} %shard_map.109.refs_0_._.own_rows), channel_id=1, source_target_pairs={{0,32},{32,64},{64,96},{96,0},{1,33},{33,65},{65,97},{97,1},{2,34}... | collective-permute-start | bytes 1228808 | tf_op jit(solution)/shard_map/ppermute | solution.py:30
  15.3 1.3 %collective-permute-start.2 = (bf16[5,32,1280]{2,1,0:T(8,128)(2,1)S(1)}, bf16[5,32,1280]{2,1,0:T(8,128)(2,1)S(1)}, u32[]{:S(2)}, u32[]{:S(2)}) collective-permute-start(bf16[5,32,1280]{2,1,0:T(8,128)(2,1)S(1)} %shard_map.109.refs_0_._.own_rows), channel_id=1, source_target_pairs={{0,96},{32,0},{64,32},{96,64},{1,97},{33,1},{65,33},{97,65},{2,98}... | collective-permute-start | bytes 1228808 | tf_op jit(solution)/shard_map/ppermute | solution.py:30
  16.6 5.1 %collective-permute-done.8.three_rows = bf16[4,32,1280]{2,1,0:T(8,128)(2,1)S(1)} collective-permute-done((bf16[4,32,1280]{2,1,0:T(8,128)(2,1)S(1)}, bf16[4,32,1280]{2,1,0:T(8,128)(2,1)S(1)}, u32[]{:S(2)}, u32[]{:S(2)}) %collective-permute-start.8) | collective-permute-done | bytes 327712 | tf_op jit(solution)/shard_map/ppermute | solution.py:30
  21.7 5.1 %shard_map.114 = (bf16[4,32,1280]{2,1,0:T(8,128)(2,1)S(1)}, bf16[4,32,1280]{2,1,0:T(8,128)(2,1)}, bf16[4,32,1280]{2,1,0:T(8,128)(2,1)S(1)}, bf16[4,32,1280]{2,1,0:T(8,128)(2,1)}) custom-call(s32[2]{0:T(128)S(1)} %pad_add_fusion.at_ref, bf16[8,32,1280]{2,1,0:T(8,128)(2,1)S(1)} %copy-done.7, bf16[4,32,1280]{2,1,0:T(8,128)(2,1)S(1)} %shard_map.113.own_rows, ...), custom_call_target="tpu_custom_call" | custom-call | flops 3355443200 | bytes 6553600 | tf_op jit(solution)/shard_map/pallas_call | solution.py:112
  26.8 8.5 %collective-permute-start.10 = (bf16[4,32,1280]{2,1,0:T(8,128)(2,1)S(1)}, bf16[4,32,1280]{2,1,0:T(8,128)(2,1)S(1)}, u32[]{:S(2)}, u32[]{:S(2)}) collective-permute-start(bf16[4,32,1280]{2,1,0:T(8,128)(2,1)S(1)} %get-tuple-element.35), channel_id=1, source_target_pairs={{0,64},{32,96},{64,0},{96,32},{1,65},{33,97},{65,1},{97,33},{2,66}... | collective-permute-start | bytes 983048 | tf_op jit(solution)/shard_map/ppermute | solution.py:30
  35.4 3.3 %collective-permute-start.9 = (bf16[4,32,1280]{2,1,0:T(8,128)(2,1)}, bf16[4,32,1280]{2,1,0:T(8,128)(2,1)}, u32[]{:S(2)}, u32[]{:S(2)}) collective-permute-start(bf16[4,32,1280]{2,1,0:T(8,128)(2,1)} %get-tuple-element.34), channel_id=1, source_target_pairs={{0,32},{32,64},{64,96},{96,0},{1,33},{33,65},{65,97},{97,1},{2,34}... | collective-permute-start | bytes 983048 | tf_op jit(solution)/shard_map/ppermute | solution.py:30
  39.3 5.2 %shard_map.112 = (bf16[4,32,1280]{2,1,0:T(8,128)(2,1)S(1)}, bf16[4,32,1280]{2,1,0:T(8,128)(2,1)}, bf16[4,32,1280]{2,1,0:T(8,128)(2,1)}, bf16[4,32,1280]{2,1,0:T(8,128)(2,1)}) custom-call(s32[2]{0:T(128)S(1)} %pad_add_fusion.at_ref, bf16[8,32,1280]{2,1,0:T(8,128)(2,1)S(1)} %copy-done.7, bf16[5,32,1280]{2,1,0:T(8,128)(2,1)S(1)} %shard_map.109.refs_0_._.own_rows, ...), custom_call_target="tpu_custom_call" | custom-call | flops 3355443200 | bytes 6553600 | tf_op jit(solution)/shard_map/pallas_call | solution.py:112
  44.5 0.7 copy-done.13
  45.3 0.8 collective-permute-start.3
  46.0 2.2 %collective-permute-start.4 = (bf16[4,32,1280]{2,1,0:T(8,128)(2,1)}, bf16[4,32,1280]{2,1,0:T(8,128)(2,1)}, u32[]{:S(2)}, u32[]{:S(2)}) collective-permute-start(bf16[4,32,1280]{2,1,0:T(8,128)(2,1)} %get-tuple-element.30), channel_id=1, source_target_pairs={{0,64},{32,96},{64,0},{96,32},{1,65},{33,97},{65,1},{97,33},{2,66}... | collective-permute-start | bytes 983048 | tf_op jit(solution)/shard_map/ppermute | solution.py:30
  48.3 0.7 copy-done.17
  49.0 0.9 collective-permute-start.5
  50.0 1.0 copy-done.10
  51.0 1.0 copy-done.12
  52.0 1.5 %shard_map.110 = (bf16[512,128]{1,0:T(8,128)(2,1)S(1)}, s32[512,1]{1,0:T(8,128)S(1)}) custom-call(s32[2]{0:T(128)S(1)} %pad_add_fusion.at_ref, s32[1,32]{1,0:T(1,128)S(1)} %bitcast.13, s32[1,64]{1,0:T(1,128)S(1)} %bitcast.14, s32[64,1]{1,0:T(8,128)S(1)} %copy.12.owner_ref, bf16[5,32,1280]{2,1,0:T(8,128)(2,1)S(1)} %shard_map.109.refs_0_._.own_rows, ...), custom_call_target="tpu_custom_call" | custom-call | tf_op jit(solution)/shard_map/pallas_call | solution.py:256
  53.5 15.9 %all_to_all.10 = bf16[32,16,128]{2,1,0:T(8,128)(2,1)S(1)} all-to-all(bf16[32,16,128]{2,1,0:T(8,128)(2,1)S(1)} %bitcast.12), channel_id=1, replica_groups=mesh['pool'=4,'dev'=32] {'dev'}, dimensions={0} | all-to-all | bytes 262144 | tf_op jit(solution)/shard_map/all_to_all | solution.py:488
  69.5 1.7 %copy-done.2 = bf16[1280,1024]{1,0:T(8,128)(2,1)S(1)} copy-done((bf16[1280,1024]{1,0:T(8,128)(2,1)S(1)}, bf16[1280,1024]{1,0:T(8,128)(2,1)}, u32[]{:S(2)}) %copy-start.2) | copy-done | bytes 2621464
  71.2 1.0 copy-done.16
  72.2 1.0 copy-done.18
  73.2 3.6 %shard_map.115.refs_0_ = bf16[8,4,16,256]{3,2,1,0:T(8,128)(2,1)S(1)} custom-call(bf16[4,32,1280]{2,1,0:T(8,128)(2,1)S(1)} %copy-done.16, bf16[4,32,1280]{2,1,0:T(8,128)(2,1)} %collective-permute-done.9.one_ref, bf16[4,32,1280]{2,1,0:T(8,128)(2,1)S(1)} %copy-done.18, bf16[4,32,1280]{2,1,0:T(8,128)(2,1)} %collective-permute-done.11.three_ref, ...), custom_call_target="tpu_custom_call" | custom-call | flops 671088640 | bytes 5242880 | tf_op jit(solution)/shard_map/pallas_call | solution.py:309
  76.8 3.9 %shard_map.116 = bf16[8,4,16,256]{3,2,1,0:T(8,128)(2,1)S(1)} custom-call(bf16[4,32,1280]{2,1,0:T(8,128)(2,1)S(1)} %copy-done.14, bf16[4,32,1280]{2,1,0:T(8,128)(2,1)} %collective-permute-done.3.one_ref, bf16[4,32,1280]{2,1,0:T(8,128)(2,1)} %collective-permute-done.4.two_ref, bf16[4,32,1280]{2,1,0:T(8,128)(2,1)} %collective-permute-done.5.three_ref, ...), custom_call_target="tpu_custom_call" | custom-call | flops 671088640 | bytes 5242880 | tf_op jit(solution)/shard_map/pallas_call | solution.py:309
  80.7 12.4 %all_to_all.11 = bf16[32,16,256]{2,1,0:T(8,128)(2,1)S(1)} all-to-all(bf16[32,16,256]{2,1,0:T(8,128)(2,1)S(1)} %bitcast.10), channel_id=1, replica_groups=mesh['pool'=4,'dev'=32] {'dev'}, dimensions={0} | all-to-all | bytes 524288 | tf_op jit(solution)/shard_map/all_to_all | solution.py:501
  93.1 1.2 shard_map.117
  94.3 2.4 %collective-permute-start.12 = (bf16[208,128]{1,0:T(8,128)(2,1)S(1)}, bf16[208,128]{1,0:T(8,128)(2,1)S(1)}, u32[]{:S(2)}, u32[]{:S(2)}) collective-permute-start(bf16[208,128]{1,0:T(8,128)(2,1)S(1)} %get-tuple-element.38), channel_id=1, source_target_pairs={{0,32},{32,64},{64,96},{96,0},{1,33},{33,65},{65,97},{97,1},{2,34}... | collective-permute-start | bytes 159752 | tf_op jit(solution)/shard_map/ppermute | solution.py:30
  96.7 1.3 %collective-permute-start.14 = (bf16[208,128]{1,0:T(8,128)(2,1)S(1)}, bf16[208,128]{1,0:T(8,128)(2,1)S(1)}, u32[]{:S(2)}, u32[]{:S(2)}) collective-permute-start(bf16[208,128]{1,0:T(8,128)(2,1)S(1)} %get-tuple-element.40), channel_id=1, source_target_pairs={{0,96},{32,0},{64,32},{96,64},{1,97},{33,1},{65,33},{97,65},{2,98}... | collective-permute-start | bytes 159752 | tf_op jit(solution)/shard_map/ppermute | solution.py:30
  98.1 0.7 collective-permute-done.12.one_ref
  98.8 3.7 %collective-permute-done.13.two_ref = bf16[208,128]{1,0:T(8,128)(2,1)S(1)} collective-permute-done((bf16[208,128]{1,0:T(8,128)(2,1)S(1)}, bf16[208,128]{1,0:T(8,128)(2,1)S(1)}, u32[]{:S(2)}, u32[]{:S(2)}) %collective-permute-start.13) | collective-permute-done | bytes 53280 | tf_op jit(solution)/shard_map/ppermute | solution.py:30
  102.8 1.1 shard_map.119
  104.0 1.1 shard_map.118.kept_ref
  105.1 1.2 collective-permute-done.15.got_ref
  106.5 0.7 collective-permute-start.16
  107.1 2.0 %collective-permute-start.17 = (bf16[4,96,256]{2,1,0:T(8,128)(2,1)S(1)}, bf16[4,96,256]{2,1,0:T(8,128)(2,1)S(1)}, u32[]{:S(2)}, u32[]{:S(2)}) collective-permute-start(bf16[4,96,256]{2,1,0:T(8,128)(2,1)S(1)} %get-tuple-element.43), channel_id=1, source_target_pairs={{0,16},{1,17},{2,18},{3,19},{4,20},{5,21},{6,22},{7,23},{8,24},{9,... | collective-permute-start | bytes 589832 | tf_op jit(solution)/shard_map/ppermute | solution.py:40
  109.1 1.4 %collective-permute-start.18 = (bf16[4,96,256]{2,1,0:T(8,128)(2,1)S(1)}, bf16[4,96,256]{2,1,0:T(8,128)(2,1)S(1)}, u32[]{:S(2)}, u32[]{:S(2)}) collective-permute-start(bf16[4,96,256]{2,1,0:T(8,128)(2,1)S(1)} %get-tuple-element.44), channel_id=1, source_target_pairs={{0,24},{1,25},{2,26},{3,27},{4,28},{5,29},{6,30},{7,31},{8,0},{9,1... | collective-permute-start | bytes 589832 | tf_op jit(solution)/shard_map/ppermute | solution.py:40
  110.6 8.3 %collective-permute-done.16.a_ref = bf16[4,96,256]{2,1,0:T(8,128)(2,1)S(1)} collective-permute-done((bf16[4,96,256]{2,1,0:T(8,128)(2,1)S(1)}, bf16[4,96,256]{2,1,0:T(8,128)(2,1)S(1)}, u32[]{:S(2)}, u32[]{:S(2)}) %collective-permute-start.16) | collective-permute-done | bytes 196640 | tf_op jit(solution)/shard_map/ppermute | solution.py:40
  119.6 0.8 collective-permute-start.19
  120.4 2.1 %collective-permute-start.20 = (bf16[96,256]{1,0:T(8,128)(2,1)S(1)}, bf16[96,256]{1,0:T(8,128)(2,1)S(1)}, u32[]{:S(2)}, u32[]{:S(2)}) collective-permute-start(bf16[96,256]{1,0:T(8,128)(2,1)S(1)} %get-tuple-element.47), channel_id=1, source_target_pairs={{0,4},{1,5},{2,6},{3,7},{4,0},{5,1},{6,2},{7,3},{8,12},{9,13},{10,... | collective-permute-start | bytes 147464 | tf_op jit(solution)/shard_map/ppermute | solution.py:40
  122.6 0.7 collective-permute-start.21
  123.3 0.8 constant_dynamic-slice_fusion.residual_ref
  124.1 0.9 collective-permute-done.19.a_ref
  125.0 1.0 collective-permute-done.20.b_ref
  126.7 0.7 shard_map.122
  (59 shorter events, 3.5 us)
Async XLA Ops:
  0.1 1.1 copy-start.6
  2.0 13.3 %collective-permute-start.6 = (bf16[4,32,1280]{2,1,0:T(8,128)(2,1)S(1)}, bf16[4,32,1280]{2,1,0:T(8,128)(2,1)S(1)}, u32[]{:S(2)}, u32[]{:S(2)}) collective-permute-start(bf16[4,32,1280]{2,1,0:T(8,128)(2,1)S(1)} %shard_map.113.own_rows), channel_id=1, source_target_pairs={{0,32},{32,64},{64,96},{96,0},{1,33},{33,65},{65,97},{97,1},{2,34}... | collective-permute-start | bytes 983048 | tf_op jit(solution)/shard_map/ppermute | solution.py:30
  2.5 14.2 %collective-permute-start.7 = (bf16[4,32,1280]{2,1,0:T(8,128)(2,1)S(1)}, bf16[4,32,1280]{2,1,0:T(8,128)(2,1)S(1)}, u32[]{:S(2)}, u32[]{:S(2)}) collective-permute-start(bf16[4,32,1280]{2,1,0:T(8,128)(2,1)S(1)} %shard_map.113.own_rows), channel_id=1, source_target_pairs={{0,64},{32,96},{64,0},{96,32},{1,65},{33,97},{65,1},{97,33},{2,66}... | collective-permute-start | bytes 983048 | tf_op jit(solution)/shard_map/ppermute | solution.py:30
  5.0 16.8 %collective-permute-start.8 = (bf16[4,32,1280]{2,1,0:T(8,128)(2,1)S(1)}, bf16[4,32,1280]{2,1,0:T(8,128)(2,1)S(1)}, u32[]{:S(2)}, u32[]{:S(2)}) collective-permute-start(bf16[4,32,1280]{2,1,0:T(8,128)(2,1)S(1)} %shard_map.113.own_rows), channel_id=1, source_target_pairs={{0,96},{32,0},{64,32},{96,64},{1,97},{33,1},{65,33},{97,65},{2,98}... | collective-permute-start | bytes 983048 | tf_op jit(solution)/shard_map/ppermute | solution.py:30
  5.0 2.2 %copy-start.3 = (bf16[8192,256]{1,0:T(8,128)(2,1)S(1)}, bf16[8192,256]{1,0:T(8,128)(2,1)}, u32[]{:S(2)}) copy-start(bf16[8192,256]{1,0:T(8,128)(2,1)} %weight_ref.3) | copy-start | bytes 12582916
  7.2 1.1 copy-start.7
  8.2 1.4 %copy-start.8 = (bf16[24,4,8192]{2,1,0:T(4,128)(2,1)S(1)}, bf16[24,4,8192]{2,1,0:T(4,128)(2,1)}, u32[]{:S(2)}) copy-start(bf16[24,4,8192]{2,1,0:T(4,128)(2,1)} %text_ref.1) | copy-start | bytes 4718596
  9.7 7.0 %copy-start.4 = (bf16[1280,1280]{1,0:T(8,128)(2,1)S(1)}, bf16[1280,1280]{1,0:T(8,128)(2,1)}, u32[]{:S(2)}) copy-start(bf16[1280,1280]{1,0:T(8,128)(2,1)} %fc1_ref.3) | copy-start | bytes 9830404
  9.7 7.0 %copy-start.5 = (bf16[1280,1280]{1,0:T(8,128)(2,1)S(1)}, bf16[1280,1280]{1,0:T(8,128)(2,1)}, u32[]{:S(2)}) copy-start(bf16[1280,1280]{1,0:T(8,128)(2,1)} %fc2_ref.3) | copy-start | bytes 9830404
  11.9 23.5 %collective-permute-start = (bf16[5,32,1280]{2,1,0:T(8,128)(2,1)S(1)}, bf16[5,32,1280]{2,1,0:T(8,128)(2,1)S(1)}, u32[]{:S(2)}, u32[]{:S(2)}) collective-permute-start(bf16[5,32,1280]{2,1,0:T(8,128)(2,1)S(1)} %shard_map.109.refs_0_._.own_rows), channel_id=1, source_target_pairs={{0,32},{32,64},{64,96},{96,0},{1,33},{33,65},{65,97},{97,1},{2,34}... | collective-permute-start | bytes 1228808 | tf_op jit(solution)/shard_map/ppermute | solution.py:30
  15.2 23.5 %collective-permute-start.1 = (bf16[5,32,1280]{2,1,0:T(8,128)(2,1)S(1)}, bf16[5,32,1280]{2,1,0:T(8,128)(2,1)S(1)}, u32[]{:S(2)}, u32[]{:S(2)}) collective-permute-start(bf16[5,32,1280]{2,1,0:T(8,128)(2,1)S(1)} %shard_map.109.refs_0_._.own_rows), channel_id=1, source_target_pairs={{0,64},{32,96},{64,0},{96,32},{1,65},{33,97},{65,1},{97,33},{2,66}... | collective-permute-start | bytes 1228808 | tf_op jit(solution)/shard_map/ppermute | solution.py:30
  15.3 24.0 %collective-permute-start.2 = (bf16[5,32,1280]{2,1,0:T(8,128)(2,1)S(1)}, bf16[5,32,1280]{2,1,0:T(8,128)(2,1)S(1)}, u32[]{:S(2)}, u32[]{:S(2)}) collective-permute-start(bf16[5,32,1280]{2,1,0:T(8,128)(2,1)S(1)} %shard_map.109.refs_0_._.own_rows), channel_id=1, source_target_pairs={{0,96},{32,0},{64,32},{96,64},{1,97},{33,1},{65,33},{97,65},{2,98}... | collective-permute-start | bytes 1228808 | tf_op jit(solution)/shard_map/ppermute | solution.py:30
  26.8 17.7 %copy-start.15 = (bf16[4,32,1280]{2,1,0:T(8,128)(2,1)}, bf16[4,32,1280]{2,1,0:T(8,128)(2,1)S(1)}, u32[]{:S(2)}) copy-start(bf16[4,32,1280]{2,1,0:T(8,128)(2,1)S(1)} %get-tuple-element.33.total_ref) | copy-start | bytes 983044
  26.8 21.4 %collective-permute-start.10 = (bf16[4,32,1280]{2,1,0:T(8,128)(2,1)S(1)}, bf16[4,32,1280]{2,1,0:T(8,128)(2,1)S(1)}, u32[]{:S(2)}, u32[]{:S(2)}) collective-permute-start(bf16[4,32,1280]{2,1,0:T(8,128)(2,1)S(1)} %get-tuple-element.35), channel_id=1, source_target_pairs={{0,64},{32,96},{64,0},{96,32},{1,65},{33,97},{65,1},{97,33},{2,66}... | collective-permute-start | bytes 983048 | tf_op jit(solution)/shard_map/ppermute | solution.py:30
  35.4 34.1 %collective-permute-start.11 = (bf16[4,32,1280]{2,1,0:T(8,128)(2,1)}, bf16[4,32,1280]{2,1,0:T(8,128)(2,1)}, u32[]{:S(2)}, u32[]{:S(2)}) collective-permute-start(bf16[4,32,1280]{2,1,0:T(8,128)(2,1)} %get-tuple-element.36), channel_id=1, source_target_pairs={{0,96},{32,0},{64,32},{96,64},{1,97},{33,1},{65,33},{97,65},{2,98}... | collective-permute-start | bytes 983048 | tf_op jit(solution)/shard_map/ppermute | solution.py:30
  35.4 14.6 %copy-start.21 = (s32[64,1]{0,1:T(1,128)S(1)}, s32[64,1]{0,1:T(1,128)}, u32[]{:S(2)}) copy-start(s32[64,1]{0,1:T(1,128)} %param.14) | copy-start | bytes 772
  35.4 14.7 %copy-start.19 = (s32[32]{0:T(128)S(1)}, s32[32]{0:T(128)}, u32[]{:S(2)}) copy-start(s32[32]{0:T(128)} %param.12) | copy-start | bytes 388
  35.4 14.7 %copy-start.20 = (s32[64]{0:T(128)S(1)}, s32[64]{0:T(128)}, u32[]{:S(2)}) copy-start(s32[64]{0:T(128)} %param.13) | copy-start | bytes 772
  35.4 34.1 %collective-permute-start.9 = (bf16[4,32,1280]{2,1,0:T(8,128)(2,1)}, bf16[4,32,1280]{2,1,0:T(8,128)(2,1)}, u32[]{:S(2)}, u32[]{:S(2)}) collective-permute-start(bf16[4,32,1280]{2,1,0:T(8,128)(2,1)} %get-tuple-element.34), channel_id=1, source_target_pairs={{0,32},{32,64},{64,96},{96,0},{1,33},{33,65},{65,97},{97,1},{2,34}... | collective-permute-start | bytes 983048 | tf_op jit(solution)/shard_map/ppermute | solution.py:30
  38.7 5.9 %copy-start.9 = (bf16[5,32,1280]{2,1,0:T(8,128)(2,1)}, bf16[5,32,1280]{2,1,0:T(8,128)(2,1)S(1)}, u32[]{:S(2)}) copy-start(bf16[5,32,1280]{2,1,0:T(8,128)(2,1)S(1)} %collective-permute-done.1.refs_2_.two_rows) | copy-start | bytes 1228804
  39.3 5.2 %copy-start.11 = (bf16[5,32,1280]{2,1,0:T(8,128)(2,1)}, bf16[5,32,1280]{2,1,0:T(8,128)(2,1)S(1)}, u32[]{:S(2)}) copy-start(bf16[5,32,1280]{2,1,0:T(8,128)(2,1)S(1)} %collective-permute-done.2.refs_3_.three_rows) | copy-start | bytes 1228804
  39.3 30.2 %copy-start.1 = (bf16[1280,1024]{1,0:T(8,128)(2,1)S(1)}, bf16[1280,1024]{1,0:T(8,128)(2,1)}, u32[]{:S(2)}) copy-start(bf16[1280,1024]{1,0:T(8,128)(2,1)} %key_ref.3) | copy-start | bytes 7864324
  44.5 0.7 copy-start.13
  45.3 31.5 %collective-permute-start.3 = (bf16[4,32,1280]{2,1,0:T(8,128)(2,1)}, bf16[4,32,1280]{2,1,0:T(8,128)(2,1)}, u32[]{:S(2)}, u32[]{:S(2)}) collective-permute-start(bf16[4,32,1280]{2,1,0:T(8,128)(2,1)} %get-tuple-element.29), channel_id=1, source_target_pairs={{0,32},{32,64},{64,96},{96,0},{1,33},{33,65},{65,97},{97,1},{2,34}... | collective-permute-start | bytes 983048 | tf_op jit(solution)/shard_map/ppermute | solution.py:30
  46.0 30.8 %collective-permute-start.4 = (bf16[4,32,1280]{2,1,0:T(8,128)(2,1)}, bf16[4,32,1280]{2,1,0:T(8,128)(2,1)}, u32[]{:S(2)}, u32[]{:S(2)}) collective-permute-start(bf16[4,32,1280]{2,1,0:T(8,128)(2,1)} %get-tuple-element.30), channel_id=1, source_target_pairs={{0,64},{32,96},{64,0},{96,32},{1,65},{33,97},{65,1},{97,33},{2,66}... | collective-permute-start | bytes 983048 | tf_op jit(solution)/shard_map/ppermute | solution.py:30
  48.3 0.7 copy-start.17
  49.0 27.8 %collective-permute-start.5 = (bf16[4,32,1280]{2,1,0:T(8,128)(2,1)}, bf16[4,32,1280]{2,1,0:T(8,128)(2,1)}, u32[]{:S(2)}, u32[]{:S(2)}) collective-permute-start(bf16[4,32,1280]{2,1,0:T(8,128)(2,1)} %get-tuple-element.31), channel_id=1, source_target_pairs={{0,96},{32,0},{64,32},{96,64},{1,97},{33,1},{65,33},{97,65},{2,98}... | collective-permute-start | bytes 983048 | tf_op jit(solution)/shard_map/ppermute | solution.py:30
  50.0 1.0 copy-start.10
  51.0 1.0 copy-start.12
  69.5 1.7 %copy-start.2 = (bf16[1280,1024]{1,0:T(8,128)(2,1)S(1)}, bf16[1280,1024]{1,0:T(8,128)(2,1)}, u32[]{:S(2)}) copy-start(bf16[1280,1024]{1,0:T(8,128)(2,1)} %value_ref.3) | copy-start | bytes 7864324
  71.2 1.0 copy-start.16
  72.2 1.0 copy-start.18
  73.2 3.6 %copy-start.14 = (bf16[4,32,1280]{2,1,0:T(8,128)(2,1)S(1)}, bf16[4,32,1280]{2,1,0:T(8,128)(2,1)}, u32[]{:S(2)}) copy-start(bf16[4,32,1280]{2,1,0:T(8,128)(2,1)} %copy-done.13) | copy-start | bytes 983044
  76.8 26.0 %copy-start = (bf16[256,8192]{1,0:T(8,128)(2,1)S(1)}, bf16[256,8192]{1,0:T(8,128)(2,1)}, u32[]{:S(2)}) copy-start(bf16[256,8192]{1,0:T(8,128)(2,1)} %weight_ref.5) | copy-start | bytes 12582916
  94.3 4.5 %collective-permute-start.12 = (bf16[208,128]{1,0:T(8,128)(2,1)S(1)}, bf16[208,128]{1,0:T(8,128)(2,1)S(1)}, u32[]{:S(2)}, u32[]{:S(2)}) collective-permute-start(bf16[208,128]{1,0:T(8,128)(2,1)S(1)} %get-tuple-element.38), channel_id=1, source_target_pairs={{0,32},{32,64},{64,96},{96,0},{1,33},{33,65},{65,97},{97,1},{2,34}... | collective-permute-start | bytes 159752 | tf_op jit(solution)/shard_map/ppermute | solution.py:30
  96.6 5.9 %collective-permute-start.13 = (bf16[208,128]{1,0:T(8,128)(2,1)S(1)}, bf16[208,128]{1,0:T(8,128)(2,1)S(1)}, u32[]{:S(2)}, u32[]{:S(2)}) collective-permute-start(bf16[208,128]{1,0:T(8,128)(2,1)S(1)} %get-tuple-element.39), channel_id=1, source_target_pairs={{0,64},{32,96},{64,0},{96,32},{1,65},{33,97},{65,1},{97,33},{2,66}... | collective-permute-start | bytes 159752 | tf_op jit(solution)/shard_map/ppermute | solution.py:30
  96.7 6.1 %collective-permute-start.14 = (bf16[208,128]{1,0:T(8,128)(2,1)S(1)}, bf16[208,128]{1,0:T(8,128)(2,1)S(1)}, u32[]{:S(2)}, u32[]{:S(2)}) collective-permute-start(bf16[208,128]{1,0:T(8,128)(2,1)S(1)} %get-tuple-element.40), channel_id=1, source_target_pairs={{0,96},{32,0},{64,32},{96,64},{1,97},{33,1},{65,33},{97,65},{2,98}... | collective-permute-start | bytes 159752 | tf_op jit(solution)/shard_map/ppermute | solution.py:30
  103.9 2.4 %collective-permute-start.15 = (bf16[4,4,96,256]{3,2,1,0:T(8,128)(2,1)S(1)}, bf16[4,4,96,256]{3,2,1,0:T(8,128)(2,1)S(1)}, u32[]{:S(2)}, u32[]{:S(2)}) collective-permute-start(bf16[4,4,96,256]{3,2,1,0:T(8,128)(2,1)S(1)} %shard_map.119), channel_id=1, source_target_pairs={{0,1},{1,0},{2,3},{3,2},{4,5},{5,4},{6,7},{7,6},{8,9},{9,8},{10,11... | collective-permute-start | bytes 2359304 | tf_op jit(solution)/shard_map/ppermute | solution.py:40
  106.5 12.4 %collective-permute-start.16 = (bf16[4,96,256]{2,1,0:T(8,128)(2,1)S(1)}, bf16[4,96,256]{2,1,0:T(8,128)(2,1)S(1)}, u32[]{:S(2)}, u32[]{:S(2)}) collective-permute-start(bf16[4,96,256]{2,1,0:T(8,128)(2,1)S(1)} %get-tuple-element.42), channel_id=1, source_target_pairs={{0,8},{1,9},{2,10},{3,11},{4,12},{5,13},{6,14},{7,15},{8,16},{9,17... | collective-permute-start | bytes 589832 | tf_op jit(solution)/shard_map/ppermute | solution.py:40
  107.1 11.8 %collective-permute-start.17 = (bf16[4,96,256]{2,1,0:T(8,128)(2,1)S(1)}, bf16[4,96,256]{2,1,0:T(8,128)(2,1)S(1)}, u32[]{:S(2)}, u32[]{:S(2)}) collective-permute-start(bf16[4,96,256]{2,1,0:T(8,128)(2,1)S(1)} %get-tuple-element.43), channel_id=1, source_target_pairs={{0,16},{1,17},{2,18},{3,19},{4,20},{5,21},{6,22},{7,23},{8,24},{9,... | collective-permute-start | bytes 589832 | tf_op jit(solution)/shard_map/ppermute | solution.py:40
  109.1 10.4 %collective-permute-start.18 = (bf16[4,96,256]{2,1,0:T(8,128)(2,1)S(1)}, bf16[4,96,256]{2,1,0:T(8,128)(2,1)S(1)}, u32[]{:S(2)}, u32[]{:S(2)}) collective-permute-start(bf16[4,96,256]{2,1,0:T(8,128)(2,1)S(1)} %get-tuple-element.44), channel_id=1, source_target_pairs={{0,24},{1,25},{2,26},{3,27},{4,28},{5,29},{6,30},{7,31},{8,0},{9,1... | collective-permute-start | bytes 589832 | tf_op jit(solution)/shard_map/ppermute | solution.py:40
  119.6 5.4 %collective-permute-start.19 = (bf16[96,256]{1,0:T(8,128)(2,1)S(1)}, bf16[96,256]{1,0:T(8,128)(2,1)S(1)}, u32[]{:S(2)}, u32[]{:S(2)}) collective-permute-start(bf16[96,256]{1,0:T(8,128)(2,1)S(1)} %get-tuple-element.46), channel_id=1, source_target_pairs={{0,2},{1,3},{2,4},{3,5},{4,6},{5,7},{6,0},{7,1},{8,10},{9,11},{10,... | collective-permute-start | bytes 147464 | tf_op jit(solution)/shard_map/ppermute | solution.py:40
  120.4 5.6 %collective-permute-start.20 = (bf16[96,256]{1,0:T(8,128)(2,1)S(1)}, bf16[96,256]{1,0:T(8,128)(2,1)S(1)}, u32[]{:S(2)}, u32[]{:S(2)}) collective-permute-start(bf16[96,256]{1,0:T(8,128)(2,1)S(1)} %get-tuple-element.47), channel_id=1, source_target_pairs={{0,4},{1,5},{2,6},{3,7},{4,0},{5,1},{6,2},{7,3},{8,12},{9,13},{10,... | collective-permute-start | bytes 147464 | tf_op jit(solution)/shard_map/ppermute | solution.py:40
  122.6 4.1 %collective-permute-start.21 = (bf16[96,256]{1,0:T(8,128)(2,1)S(1)}, bf16[96,256]{1,0:T(8,128)(2,1)S(1)}, u32[]{:S(2)}, u32[]{:S(2)}) collective-permute-start(bf16[96,256]{1,0:T(8,128)(2,1)S(1)} %get-tuple-element.48), channel_id=1, source_target_pairs={{0,6},{1,7},{2,0},{3,1},{4,2},{5,3},{6,4},{7,5},{8,14},{9,15},{10,... | collective-permute-start | bytes 147464 | tf_op jit(solution)/shard_map/ppermute | solution.py:40

commit v3 on v2

--- a/solution.py
+++ b/solution.py
@@ -14,6 +14,7 @@
 RING = 4
 BLOCK = 256
 TOTAL_ROWS = 16
+ATTEND_MIB = 20
 F32, BF16 = jnp.float32, jnp.bfloat16
 
 epsilon = 1e-05
@@ -80,7 +81,10 @@
 def feed_forward_kernel(
     half, at_ref, patches_ref, own_rows, one_rows, two_rows, three_rows, fc1_ref, fc2_ref, *refs
 ):
-    total_ref, one_ref, two_ref, three_ref, rows_ref, wide_ref = refs[-6:]
+    total_ref, one_ref, two_ref, three_ref, *query_refs, rows_ref, wide_ref = refs[1:]
+    for ref in query_refs:
+        for source, rows in enumerate((own_rows, one_rows, two_rows, three_rows)):
+            ref[source] = rows[RING]
     hidden, width = fc2_ref.shape
     quarter = patches_ref.shape[1]
     rows = RING * quarter
@@ -111,9 +115,9 @@
     sent = jax.ShapeDtypeStruct(shape, BF16)
     return pl.pallas_call(
         functools.partial(feed_forward_kernel, half),
-        out_shape=(sent,) * 4,
+        out_shape=(sent,) * (4 + half),
         in_specs=[SMEM] + [VMEM] * (7 + len(after)),
-        out_specs=(VMEM,) * 4,
+        out_specs=(VMEM,) * (4 + half),
         scratch_shapes=[
             pltpu.VMEM((RING * RING * quarter, width), BF16),
             pltpu.VMEM((RING * RING * quarter, hidden), BF16),
@@ -196,7 +200,7 @@
     slots, steps, heads, capacity, at_ref, enc_ref, req_ref, owner_ref,
     *refs,
 ):
-    *sources, chosen_ref, target_ref = refs
+    sources, chosen_ref, target_ref = refs
     here = at_ref[0]
     columns, requests = enc_ref.shape[1], req_ref.shape[1]
     halves = capacity // RING
@@ -235,14 +239,13 @@
     chosen = jnp.zeros((rows, HEAD_DIM), F32)
     for shift in range(RING):
         group = lax.rem(here - shift + RING, RING)
-        ref = sources[0].at[group] if len(sources) == 1 else sources[shift]
         match = target == iota((rows, per_group), 1) + group * per_group
         chosen = chosen + jnp.dot(
             jnp.where(match, 1.0, 0.0).astype(BF16),
             jnp.concatenate(
                 [
-                    ref[RING, :, lane : lane + HEAD_DIM]
-                    for lane in range(0, per_group // ref.shape[1] * HEAD_DIM, HEAD_DIM)
+                    sources[shift, :, lane : lane + HEAD_DIM]
+                    for lane in range(0, per_group // sources.shape[1] * HEAD_DIM, HEAD_DIM)
                 ],
                 axis=0,
             ),
@@ -259,65 +262,106 @@
             jax.ShapeDtypeStruct((rows, HEAD_DIM), BF16),
             jax.ShapeDtypeStruct((rows, 1), jnp.int32),
         ),
-        in_specs=[SMEM] + [VMEM] * (3 + len(queries)),
+        in_specs=[SMEM] + [VMEM] * 4,
         out_specs=(VMEM, VMEM),
         compiler_params=params(8),
-    )(at, enc, req, owner, *queries)
-
-
-def attend_kernel(half, total_ref, one_ref, two_ref, three_ref, key_ref, value_ref, query_ref, *refs):
-    out_ref = refs[-1]
-    _, quarter, width = total_ref.shape
-    summed = total_ref[...].astype(F32)
-    for ref in (one_ref, two_ref, three_ref):
-        summed = summed + ref[...].astype(F32)
-    vision = summed.astype(BF16).reshape(RING * quarter, width)
+    )(at, enc, req, owner, queries)
+
+
+def attend_kernel(*refs):
+    count = 2 * RING
+    sums, (key_hbm, value_hbm, query_hbm) = refs[:count], refs[count : count + 3]
+    out_ref, sums_ref, rows_ref, key_ref, value_ref, query_ref, sum_sems, weight_sems = refs[count + 3 :]
+    _, ring, quarter, width = sums_ref.shape
     heads, per_head, per_device, _ = query_ref.shape
-    count = per_head * per_device
-    mine = iota((count, 1), 0) % per_device // (per_device // 2) == half
+    pairs = heads * HEAD_DIM // BLOCK
+    copies = [
+        pltpu.make_async_copy(ref, sums_ref.at[i], sum_sems.at[i]) for i, ref in enumerate(sums)
+    ]
+    copies.append(pltpu.make_async_copy(query_hbm, query_ref, sum_sems.at[count]))
+    weight_copies = []
+    for pair in range(pairs):
+        at = pl.ds(pair * BLOCK, BLOCK)
+        weight_copies.append(
+            [
+                pltpu.make_async_copy(hbm.at[:, at], ref.at[:, at], weight_sems.at[i, pair])
+                for i, (hbm, ref) in enumerate(((key_hbm, key_ref), (value_hbm, value_ref)))
+            ]
+        )
+    for copy in copies + weight_copies[0]:
+        copy.start()
+    for more in weight_copies[1:]:
+        for copy in more:
+            copy.start()
+    rows = ring * quarter
+    for half in range(2):
+        for i in range(half * RING, (half + 1) * RING):
+            copies[i].wait()
+        summed = sums_ref[half * RING].astype(F32)
+        for i in range(half * RING + 1, (half + 1) * RING):
+            summed = summed + sums_ref[i].astype(F32)
+        rows_ref[half * rows : (half + 1) * rows] = summed.astype(BF16).reshape(rows, width)
+    copies[count].wait()
+    many = per_head * per_device
+    mine = (
+        iota((many, 2 * rows), 0) % per_device // (per_device // 2)
+        == iota((many, 2 * rows), 1) // rows
+    )
     together = BLOCK // HEAD_DIM
-    for pair in range(heads // together):
+    for pair in range(pairs):
         at = slice(pair * BLOCK, (pair + 1) * BLOCK)
-        keys = jnp.dot(vision, key_ref[:, at], preferred_element_type=F32)
-        values = jnp.dot(vision, value_ref[:, at], preferred_element_type=F32).astype(BF16)
+        for copy in weight_copies[pair]:
+            copy.wait()
+        keys = jnp.dot(rows_ref[...], key_ref[:, at], preferred_element_type=F32)
+        values = jnp.dot(rows_ref[...], value_ref[:, at], preferred_element_type=F32).astype(BF16)
         for place in range(together):
             head = pair * together + place
             at = slice(place * HEAD_DIM, (place + 1) * HEAD_DIM)
             key = keys[:, at]
             mean = jnp.mean(key * key, axis=-1, keepdims=True)
             key = (key / jnp.sqrt(mean + epsilon)).astype(BF16)
-            query = query_ref[head].reshape(count, HEAD_DIM)
+            query = query_ref[head].reshape(many, HEAD_DIM)
             scores = lax.dot_general(
                 query, key, (((1,), (1,)), ((), ())), preferred_element_type=F32
             ) * HEAD_DIM ** (-0.5)
             weights = jnp.where(mine, jnp.exp(scores), 0.0)
             divisor = jnp.sum(weights, axis=-1, keepdims=True)
             numerator = jnp.dot(weights.astype(BF16), values[:, at], preferred_element_type=F32)
-            packed = jnp.concatenate(
-                [numerator, jnp.broadcast_to(divisor, numerator.shape)], axis=1
-            ).reshape(per_head, per_device, 2 * HEAD_DIM)
-            if len(refs) > 1:
-                packed = packed + refs[0][head].astype(F32)
-            out_ref[head] = packed.astype(BF16)
-
-
-def attend(total, received, key_weight, value_weight, queries, half, before):
-    _, quarter, width = total.shape
+            out_ref[head] = (
+                jnp.concatenate(
+                    [numerator, jnp.broadcast_to(divisor, numerator.shape)], axis=1
+                )
+                .reshape(per_head, per_device, 2 * HEAD_DIM)
+                .astype(BF16)
+            )
+
+
+def attend(sums, key_weight, value_weight, queries):
+    shape = sums[0].shape
+    _, quarter, width = shape
     heads, per_head, per_device, _ = queries.shape
     columns = key_weight.shape[1]
-    before = [] if before is None else [before]
-    return pl.pallas_call(
-        functools.partial(attend_kernel, half),
+    return pl.pallas_call(
+        attend_kernel,
         out_shape=jax.ShapeDtypeStruct((heads, per_head, per_device, 2 * HEAD_DIM), BF16),
-        in_specs=[VMEM] * (7 + len(before)),
+        in_specs=[pl.BlockSpec(memory_space=pl.ANY)] * (len(sums) + 3),
         out_specs=VMEM,
-        compiler_params=params(12),
+        scratch_shapes=[
+            pltpu.VMEM((len(sums),) + shape, BF16),
+            pltpu.VMEM((2 * RING * quarter, width), BF16),
+            pltpu.VMEM(key_weight.shape, BF16),
+            pltpu.VMEM(value_weight.shape, BF16),
+            pltpu.VMEM(queries.shape, BF16),
+            pltpu.SemaphoreType.DMA((len(sums) + 1,)),
+            pltpu.SemaphoreType.DMA((2, columns // BLOCK)),
+        ],
+        compiler_params=params(ATTEND_MIB),
         cost_estimate=pl.CostEstimate(
-            flops=4 * RING * quarter * width * columns,
+            flops=8 * RING * quarter * width * columns,
             bytes_accessed=4 * width * columns,
             transcendentals=0,
         ),
-    )(total, *received, key_weight, value_weight, queries, *before)
+    )(*sums, key_weight, value_weight, queries)
 
 
 def combine_kernel(at_ref, target_ref, packed_ref, own_ref, one_ref, two_ref, three_ref):
@@ -473,12 +517,20 @@
 
     own = [normalize(at, patches), second_half(at, text_hidden, query_weight, patches)]
     sources = [[rows] + [pool_shift(rows, s) for s in range(1, RING)] for rows in own]
+    held = hold(fc1_weight, fc2_weight, sources[1][0])
+    sums, queries = [], None
+    for i in range(halves):
+        total, *messages = feed_forward(
+            at, patches, sources[i], fc1_weight, fc2_weight, i, (held,)
+        )
+        queries = messages[-1]
+        sums += [total] + [pool_shift(messages[s - 1], s) for s in range(1, RING)]
     chosen, target = select(
         at,
         enc_tiles.reshape(1, -1),
         req_tiles.reshape(1, -1),
         req_owner,
-        sources[1],
+        queries,
         slots,
         steps,
         local_heads,
@@ -488,16 +540,7 @@
     tile_queries = lax.all_to_all(
         chosen.reshape(devices, per_device, HEAD_DIM), "dev", split_axis=0, concat_axis=0, tiled=True
     ).reshape(KV_HEADS, devices // KV_HEADS, per_device, HEAD_DIM)
-
-    held = hold(fc1_weight, fc2_weight, sources[1][0])
-    packed = None
-    for i in range(halves):
-        total, *messages = feed_forward(
-            at, patches, sources[i], fc1_weight, fc2_weight, i,
-            (held,),
-        )
-        received = [pool_shift(messages[s - 1], s) for s in range(1, RING)]
-        packed = attend(total, received, key_weight, value_weight, tile_queries, i, packed)
+    packed = attend(sums, key_weight, value_weight, tile_queries)
     packed = lax.all_to_all(
         packed.reshape(devices, per_device, 2 * HEAD_DIM),
         "dev",

time: 128 us -> 126 us (0.984)
  waiting for transfers between devices: 23.2 us -> 25.4 us
  local copies, waits for them, and re-layouts: 13.8 us -> 11.8 us
  Pallas kernels: 26.6 us -> 25.1 us
    ppermute x15, waiting for transfers between devices: 10.5 us -> 12.8 us  [pool_shift(): return lax.ppermute(x, 'pool', [(i, (i + by) % RING) for i in range(RING)])]
    unnamed x45 -> x33, local copies, waits for them, and re-layouts: 13 us -> 11 us
    pallas_call x2 -> x1, Pallas kernels: 7.44 us -> 5.97 us  [attend(): pl.pallas_call(attend_kernel, out_shape=jax.ShapeDtypeStruct((heads, per_...]
  transfers between devices with their start and end apart: 22 -> 22, of which waited for: 11 -> 11; matrix products, arithmetic and copies ran while one was open for 1% -> 1% of each run, Pallas kernels for 15% -> 12%
where the time goes in v3:
time: 126 us
  starting transfers between devices  34.4 us (27%)
  blocking collectives  28.7 us (23%)
  waiting for transfers between devices  25.4 us (20%)
  Pallas kernels  25.1 us (20%)
  local copies, waits for them, and re-layouts  11.8 us (9%)
    ppermute x15, starting transfers between devices, pool_shift(): return lax.ppermute(x, 'pool', [(i, (i + by) % RING) for i in range(RING)])  26.7 us
    all_to_all x1, blocking collectives, body(): lax.all_to_all(chosen.reshape(devices, per_device, HEAD_DIM), 'dev', spli...  15.9 us
    ppermute x15, waiting for transfers between devices, pool_shift(): return lax.ppermute(x, 'pool', [(i, (i + by) % RING) for i in range(RING)])  12.8 us
    all_to_all x1, blocking collectives, body(): lax.all_to_all(packed.reshape(devices, per_device, 2 * HEAD_DIM), 'dev',...  12.7 us
    ppermute x7, waiting for transfers between devices, dev_shift(): return lax.ppermute(x, 'dev', pairs)  12.5 us
    unnamed x33, local copies, waits for them, and re-layouts  11 us
    pallas_call x2, Pallas kernels, feed_forward(): pl.pallas_call(functools.partial(feed_forward_kernel, half), out_shape=(s...  10.4 us
    ppermute x7, starting transfers between devices, dev_shift(): return lax.ppermute(x, 'dev', pairs)  7.72 us
  transfers between devices with their start and end apart: 22, of which 11 were waited for; matrix products, arithmetic and copies ran while one was open for 1% of the time, Pallas kernels for 12%

profile of v3, /device:TPU:6, one launch (start us, length us, event | category | flops | bytes accessed | tf_op | source)
XLA Modules:
  0.0 125.7 jit_solution(7892060290325457857)
XLA Ops:
  0.1 1.1 copy-done.6
  1.2 0.8 shard_map.113.own_rows
  2.5 2.5 %collective-permute-start.4 = (bf16[4,32,1280]{2,1,0:T(8,128)(2,1)S(1)}, bf16[4,32,1280]{2,1,0:T(8,128)(2,1)S(1)}, u32[]{:S(2)}, u32[]{:S(2)}) collective-permute-start(bf16[4,32,1280]{2,1,0:T(8,128)(2,1)S(1)} %shard_map.113.own_rows), channel_id=1, source_target_pairs={{0,64},{32,96},{64,0},{96,32},{1,65},{33,97},{65,1},{97,33},{2,66}... | collective-permute-start | bytes 983048 | tf_op jit(solution)/shard_map/ppermute | solution.py:31
  5.0 2.2 %copy-done.1 = bf16[8192,256]{1,0:T(8,128)(2,1)S(1)} copy-done((bf16[8192,256]{1,0:T(8,128)(2,1)S(1)}, bf16[8192,256]{1,0:T(8,128)(2,1)}, u32[]{:S(2)}) %copy-start.1) | copy-done | bytes 4194328
  7.2 1.1 copy-done.7
  8.2 1.4 %copy-done.8 = bf16[24,4,8192]{2,1,0:T(4,128)(2,1)S(1)} copy-done((bf16[24,4,8192]{2,1,0:T(4,128)(2,1)S(1)}, bf16[24,4,8192]{2,1,0:T(4,128)(2,1)}, u32[]{:S(2)}) %copy-start.8) | copy-done | bytes 1572888
  9.7 2.2 %shard_map.109._.own_rows = bf16[5,32,1280]{2,1,0:T(8,128)(2,1)S(1)} custom-call(s32[2]{0:T(128)S(1)} %pad_add_fusion.at_ref, bf16[24,4,8192]{2,1,0:T(4,128)(2,1)S(1)} %copy-done.8, bf16[8192,256]{1,0:T(8,128)(2,1)S(1)} %copy-done.1, bf16[8,32,1280]{2,1,0:T(8,128)(2,1)S(1)} %copy-done.7), custom_call_target="tpu_custom_call" | custom-call | flops 402653184 | bytes 5767168 | tf_op jit(solution)/shard_map/pallas_call | solution.py:174
  11.9 3.3 %collective-permute-start = (bf16[5,32,1280]{2,1,0:T(8,128)(2,1)S(1)}, bf16[5,32,1280]{2,1,0:T(8,128)(2,1)S(1)}, u32[]{:S(2)}, u32[]{:S(2)}) collective-permute-start(bf16[5,32,1280]{2,1,0:T(8,128)(2,1)S(1)} %shard_map.109._.own_rows), channel_id=1, source_target_pairs={{0,32},{32,64},{64,96},{96,0},{1,33},{33,65},{65,97},{97,1},{2,34}... | collective-permute-start | bytes 1228808 | tf_op jit(solution)/shard_map/ppermute | solution.py:31
  15.3 1.3 %collective-permute-start.2 = (bf16[5,32,1280]{2,1,0:T(8,128)(2,1)S(1)}, bf16[5,32,1280]{2,1,0:T(8,128)(2,1)S(1)}, u32[]{:S(2)}, u32[]{:S(2)}) collective-permute-start(bf16[5,32,1280]{2,1,0:T(8,128)(2,1)S(1)} %shard_map.109._.own_rows), channel_id=1, source_target_pairs={{0,96},{32,0},{64,32},{96,64},{1,97},{33,1},{65,33},{97,65},{2,98}... | collective-permute-start | bytes 1228808 | tf_op jit(solution)/shard_map/ppermute | solution.py:31
  16.6 5.1 %collective-permute-done.5.three_rows = bf16[4,32,1280]{2,1,0:T(8,128)(2,1)S(1)} collective-permute-done((bf16[4,32,1280]{2,1,0:T(8,128)(2,1)S(1)}, bf16[4,32,1280]{2,1,0:T(8,128)(2,1)S(1)}, u32[]{:S(2)}, u32[]{:S(2)}) %collective-permute-start.5) | collective-permute-done | bytes 327712 | tf_op jit(solution)/shard_map/ppermute | solution.py:31
  21.7 5.1 %shard_map.114 = (bf16[4,32,1280]{2,1,0:T(8,128)(2,1)S(1)}, bf16[4,32,1280]{2,1,0:T(8,128)(2,1)S(1)}, bf16[4,32,1280]{2,1,0:T(8,128)(2,1)}, bf16[4,32,1280]{2,1,0:T(8,128)(2,1)}) custom-call(s32[2]{0:T(128)S(1)} %pad_add_fusion.at_ref, bf16[8,32,1280]{2,1,0:T(8,128)(2,1)S(1)} %copy-done.7, bf16[4,32,1280]{2,1,0:T(8,128)(2,1)S(1)} %shard_map.113.own_rows, ...), custom_call_target="tpu_custom_call" | custom-call | flops 3355443200 | bytes 6553600 | tf_op jit(solution)/shard_map/pallas_call | solution.py:116
  26.9 0.7 collective-permute-start.6
  27.5 7.8 %collective-permute-start.7 = (bf16[4,32,1280]{2,1,0:T(8,128)(2,1)}, bf16[4,32,1280]{2,1,0:T(8,128)(2,1)}, u32[]{:S(2)}, u32[]{:S(2)}) collective-permute-start(bf16[4,32,1280]{2,1,0:T(8,128)(2,1)} %get-tuple-element.32), channel_id=1, source_target_pairs={{0,64},{32,96},{64,0},{96,32},{1,65},{33,97},{65,1},{97,33},{2,66}... | collective-permute-start | bytes 983048 | tf_op jit(solution)/shard_map/ppermute | solution.py:31
  35.4 1.5 %collective-permute-start.8 = (bf16[4,32,1280]{2,1,0:T(8,128)(2,1)}, bf16[4,32,1280]{2,1,0:T(8,128)(2,1)}, u32[]{:S(2)}, u32[]{:S(2)}) collective-permute-start(bf16[4,32,1280]{2,1,0:T(8,128)(2,1)} %get-tuple-element.33), channel_id=1, source_target_pairs={{0,96},{32,0},{64,32},{96,64},{1,97},{33,1},{65,33},{97,65},{2,98}... | collective-permute-start | bytes 983048 | tf_op jit(solution)/shard_map/ppermute | solution.py:31
  36.9 2.4 %collective-permute-done.2.three_rows = bf16[5,32,1280]{2,1,0:T(8,128)(2,1)S(1)} collective-permute-done((bf16[5,32,1280]{2,1,0:T(8,128)(2,1)S(1)}, bf16[5,32,1280]{2,1,0:T(8,128)(2,1)S(1)}, u32[]{:S(2)}, u32[]{:S(2)}) %collective-permute-start.2) | collective-permute-done | bytes 409632 | tf_op jit(solution)/shard_map/ppermute | solution.py:31
  39.3 5.2 %shard_map.111 = (bf16[4,32,1280]{2,1,0:T(8,128)(2,1)S(1)}, bf16[4,32,1280]{2,1,0:T(8,128)(2,1)}, bf16[4,32,1280]{2,1,0:T(8,128)(2,1)}, bf16[4,32,1280]{2,1,0:T(8,128)(2,1)}, bf16[4,32,1280]{2,1,0:T(8,128)(2,1)S(1)}) custom-call(s32[2]{0:T(128)S(1)} %pad_add_fusion.at_ref, bf16[8,32,1280]{2,1,0:T(8,128)(2,1)S(1)} %copy-done.7, ...), custom_call_target="tpu_custom_call" | custom-call | flops 3355443200 | bytes 6553600 | tf_op jit(solution)/shard_map/pallas_call | solution.py:116
  44.5 0.7 copy-done.9
  45.2 0.7 copy-done.11
  46.0 2.5 %collective-permute-start.10 = (bf16[4,32,1280]{2,1,0:T(8,128)(2,1)}, bf16[4,32,1280]{2,1,0:T(8,128)(2,1)}, u32[]{:S(2)}, u32[]{:S(2)}) collective-permute-start(bf16[4,32,1280]{2,1,0:T(8,128)(2,1)} %get-tuple-element.36), channel_id=1, source_target_pairs={{0,64},{32,96},{64,0},{96,32},{1,65},{33,97},{65,1},{97,33},{2,66}... | collective-permute-start | bytes 983048 | tf_op jit(solution)/shard_map/ppermute | solution.py:31
  48.5 3.2 %collective-permute-start.9 = (bf16[4,32,1280]{2,1,0:T(8,128)(2,1)}, bf16[4,32,1280]{2,1,0:T(8,128)(2,1)}, u32[]{:S(2)}, u32[]{:S(2)}) collective-permute-start(bf16[4,32,1280]{2,1,0:T(8,128)(2,1)} %get-tuple-element.35), channel_id=1, source_target_pairs={{0,32},{32,64},{64,96},{96,0},{1,33},{33,65},{65,97},{97,1},{2,34}... | collective-permute-start | bytes 983048 | tf_op jit(solution)/shard_map/ppermute | solution.py:31
  51.8 1.0 copy-done.12
  52.8 1.5 %shard_map.112 = (bf16[512,128]{1,0:T(8,128)(2,1)S(1)}, s32[512,1]{1,0:T(8,128)S(1)}) custom-call(s32[2]{0:T(128)S(1)} %pad_add_fusion.at_ref, s32[1,32]{1,0:T(1,128)S(1)} %bitcast.12, s32[1,64]{1,0:T(1,128)S(1)} %bitcast.13, s32[64,1]{1,0:T(8,128)S(1)} %copy.12.owner_ref, bf16[4,32,1280]{2,1,0:T(8,128)(2,1)S(1)} %copy-done.12), custom_call_target="tpu_custom_call" | custom-call | tf_op jit(solution)/shard_map/pallas_call | solution.py:259
  54.3 15.9 %all_to_all.10 = bf16[32,16,128]{2,1,0:T(8,128)(2,1)S(1)} all-to-all(bf16[32,16,128]{2,1,0:T(8,128)(2,1)S(1)} %bitcast.11), channel_id=1, replica_groups=mesh['pool'=4,'dev'=32] {'dev'}, dimensions={0} | all-to-all | bytes 262144 | tf_op jit(solution)/shard_map/all_to_all | solution.py:540
  70.3 1.7 %copy-done.5 = bf16[1280,1024]{1,0:T(8,128)(2,1)S(1)} copy-done((bf16[1280,1024]{1,0:T(8,128)(2,1)S(1)}, bf16[1280,1024]{1,0:T(8,128)(2,1)}, u32[]{:S(2)}) %copy-start.5) | copy-done | bytes 2621464
  72.0 1.0 copy-done.10
  73.0 6.0 %shard_map.115 = bf16[8,4,16,256]{3,2,1,0:T(8,128)(2,1)S(1)} custom-call(bf16[4,32,1280]{2,1,0:T(8,128)(2,1)S(1)} %get-tuple-element.30.refs_0_, bf16[4,32,1280]{2,1,0:T(8,128)(2,1)S(1)} %collective-permute-done.6.refs_1_, bf16[4,32,1280]{2,1,0:T(8,128)(2,1)} %collective-permute-done.7.refs_2_, bf16[4,32,1280]{2,1,0:T(8,128)(2,1)} %collective-permute-done.8.refs_3_, ...), custom_call_target="tpu_custom_call" | custom-call | flops 1342177280 | bytes 5242880 | tf_op jit(solution)/shard_map/pallas_call | solution.py:344
  79.0 12.7 %all_to_all.11 = bf16[32,16,256]{2,1,0:T(8,128)(2,1)S(1)} all-to-all(bf16[32,16,256]{2,1,0:T(8,128)(2,1)S(1)} %bitcast.8), channel_id=1, replica_groups=mesh['pool'=4,'dev'=32] {'dev'}, dimensions={0} | all-to-all | bytes 524288 | tf_op jit(solution)/shard_map/all_to_all | solution.py:544
  91.7 1.2 shard_map.116
  92.9 1.1 collective-permute-start.12
  94.0 2.1 %collective-permute-start.13 = (bf16[208,128]{1,0:T(8,128)(2,1)S(1)}, bf16[208,128]{1,0:T(8,128)(2,1)S(1)}, u32[]{:S(2)}, u32[]{:S(2)}) collective-permute-start(bf16[208,128]{1,0:T(8,128)(2,1)S(1)} %get-tuple-element.41), channel_id=1, source_target_pairs={{0,64},{32,96},{64,0},{96,32},{1,65},{33,97},{65,1},{97,33},{2,66}... | collective-permute-start | bytes 159752 | tf_op jit(solution)/shard_map/ppermute | solution.py:31
  96.2 1.4 %collective-permute-done.12.one_ref = bf16[208,128]{1,0:T(8,128)(2,1)S(1)} collective-permute-done((bf16[208,128]{1,0:T(8,128)(2,1)S(1)}, bf16[208,128]{1,0:T(8,128)(2,1)S(1)}, u32[]{:S(2)}, u32[]{:S(2)}) %collective-permute-start.12) | collective-permute-done | bytes 53280 | tf_op jit(solution)/shard_map/ppermute | solution.py:31
  97.5 2.4 %collective-permute-done.13.two_ref = bf16[208,128]{1,0:T(8,128)(2,1)S(1)} collective-permute-done((bf16[208,128]{1,0:T(8,128)(2,1)S(1)}, bf16[208,128]{1,0:T(8,128)(2,1)S(1)}, u32[]{:S(2)}, u32[]{:S(2)}) %collective-permute-start.13) | collective-permute-done | bytes 53280 | tf_op jit(solution)/shard_map/ppermute | solution.py:31
  99.9 1.6 %collective-permute-done.14.three_ref = bf16[208,128]{1,0:T(8,128)(2,1)S(1)} collective-permute-done((bf16[208,128]{1,0:T(8,128)(2,1)S(1)}, bf16[208,128]{1,0:T(8,128)(2,1)S(1)}, u32[]{:S(2)}, u32[]{:S(2)}) %collective-permute-start.14) | collective-permute-done | bytes 53280 | tf_op jit(solution)/shard_map/ppermute | solution.py:31
  101.5 1.1 shard_map.118
  102.7 1.1 shard_map.117.kept_ref
  103.7 1.2 collective-permute-done.15.got_ref
  105.5 2.1 %collective-permute-start.17 = (bf16[4,96,256]{2,1,0:T(8,128)(2,1)S(1)}, bf16[4,96,256]{2,1,0:T(8,128)(2,1)S(1)}, u32[]{:S(2)}, u32[]{:S(2)}) collective-permute-start(bf16[4,96,256]{2,1,0:T(8,128)(2,1)S(1)} %get-tuple-element.45), channel_id=1, source_target_pairs={{0,16},{1,17},{2,18},{3,19},{4,20},{5,21},{6,22},{7,23},{8,24},{9,... | collective-permute-start | bytes 589832 | tf_op jit(solution)/shard_map/ppermute | solution.py:41
  107.6 1.3 %collective-permute-start.18 = (bf16[4,96,256]{2,1,0:T(8,128)(2,1)S(1)}, bf16[4,96,256]{2,1,0:T(8,128)(2,1)S(1)}, u32[]{:S(2)}, u32[]{:S(2)}) collective-permute-start(bf16[4,96,256]{2,1,0:T(8,128)(2,1)S(1)} %get-tuple-element.46), channel_id=1, source_target_pairs={{0,24},{1,25},{2,26},{3,27},{4,28},{5,29},{6,30},{7,31},{8,0},{9,1... | collective-permute-start | bytes 589832 | tf_op jit(solution)/shard_map/ppermute | solution.py:41
  108.9 8.7 %collective-permute-done.16.a_ref = bf16[4,96,256]{2,1,0:T(8,128)(2,1)S(1)} collective-permute-done((bf16[4,96,256]{2,1,0:T(8,128)(2,1)S(1)}, bf16[4,96,256]{2,1,0:T(8,128)(2,1)S(1)}, u32[]{:S(2)}, u32[]{:S(2)}) %collective-permute-start.16) | collective-permute-done | bytes 196640 | tf_op jit(solution)/shard_map/ppermute | solution.py:41
  117.6 0.6 collective-permute-done.18.c_ref
  118.3 0.6 collective-permute-start.19
  118.9 2.0 %collective-permute-start.20 = (bf16[96,256]{1,0:T(8,128)(2,1)S(1)}, bf16[96,256]{1,0:T(8,128)(2,1)S(1)}, u32[]{:S(2)}, u32[]{:S(2)}) collective-permute-start(bf16[96,256]{1,0:T(8,128)(2,1)S(1)} %get-tuple-element.49), channel_id=1, source_target_pairs={{0,4},{1,5},{2,6},{3,7},{4,0},{5,1},{6,2},{7,3},{8,12},{9,13},{10,... | collective-permute-start | bytes 147464 | tf_op jit(solution)/shard_map/ppermute | solution.py:41
  120.9 1.2 collective-permute-start.21
  122.1 0.8 constant_dynamic-slice_fusion.residual_ref
  122.9 0.7 collective-permute-done.19.a_ref
  123.6 0.9 collective-permute-done.20.b_ref
  124.5 0.5 collective-permute-done.21.c_ref
  125.0 0.7 shard_map.121
  (46 shorter events, 1.6 us)
Async XLA Ops:
  0.1 1.1 copy-start.6
  2.0 13.3 %collective-permute-start.3 = (bf16[4,32,1280]{2,1,0:T(8,128)(2,1)S(1)}, bf16[4,32,1280]{2,1,0:T(8,128)(2,1)S(1)}, u32[]{:S(2)}, u32[]{:S(2)}) collective-permute-start(bf16[4,32,1280]{2,1,0:T(8,128)(2,1)S(1)} %shard_map.113.own_rows), channel_id=1, source_target_pairs={{0,32},{32,64},{64,96},{96,0},{1,33},{33,65},{65,97},{97,1},{2,34}... | collective-permute-start | bytes 983048 | tf_op jit(solution)/shard_map/ppermute | solution.py:31
  2.5 14.2 %collective-permute-start.4 = (bf16[4,32,1280]{2,1,0:T(8,128)(2,1)S(1)}, bf16[4,32,1280]{2,1,0:T(8,128)(2,1)S(1)}, u32[]{:S(2)}, u32[]{:S(2)}) collective-permute-start(bf16[4,32,1280]{2,1,0:T(8,128)(2,1)S(1)} %shard_map.113.own_rows), channel_id=1, source_target_pairs={{0,64},{32,96},{64,0},{96,32},{1,65},{33,97},{65,1},{97,33},{2,66}... | collective-permute-start | bytes 983048 | tf_op jit(solution)/shard_map/ppermute | solution.py:31
  5.0 16.8 %collective-permute-start.5 = (bf16[4,32,1280]{2,1,0:T(8,128)(2,1)S(1)}, bf16[4,32,1280]{2,1,0:T(8,128)(2,1)S(1)}, u32[]{:S(2)}, u32[]{:S(2)}) collective-permute-start(bf16[4,32,1280]{2,1,0:T(8,128)(2,1)S(1)} %shard_map.113.own_rows), channel_id=1, source_target_pairs={{0,96},{32,0},{64,32},{96,64},{1,97},{33,1},{65,33},{97,65},{2,98}... | collective-permute-start | bytes 983048 | tf_op jit(solution)/shard_map/ppermute | solution.py:31
  5.0 2.2 %copy-start.1 = (bf16[8192,256]{1,0:T(8,128)(2,1)S(1)}, bf16[8192,256]{1,0:T(8,128)(2,1)}, u32[]{:S(2)}) copy-start(bf16[8192,256]{1,0:T(8,128)(2,1)} %weight_ref.3) | copy-start | bytes 12582916
  7.2 1.1 copy-start.7
  8.2 1.4 %copy-start.8 = (bf16[24,4,8192]{2,1,0:T(4,128)(2,1)S(1)}, bf16[24,4,8192]{2,1,0:T(4,128)(2,1)}, u32[]{:S(2)}) copy-start(bf16[24,4,8192]{2,1,0:T(4,128)(2,1)} %text_ref.1) | copy-start | bytes 4718596
  9.7 7.0 %copy-start.2 = (bf16[1280,1280]{1,0:T(8,128)(2,1)S(1)}, bf16[1280,1280]{1,0:T(8,128)(2,1)}, u32[]{:S(2)}) copy-start(bf16[1280,1280]{1,0:T(8,128)(2,1)} %fc1_ref.3) | copy-start | bytes 9830404
  9.7 7.0 %copy-start.3 = (bf16[1280,1280]{1,0:T(8,128)(2,1)S(1)}, bf16[1280,1280]{1,0:T(8,128)(2,1)}, u32[]{:S(2)}) copy-start(bf16[1280,1280]{1,0:T(8,128)(2,1)} %fc2_ref.3) | copy-start | bytes 9830404
  11.9 23.5 %collective-permute-start = (bf16[5,32,1280]{2,1,0:T(8,128)(2,1)S(1)}, bf16[5,32,1280]{2,1,0:T(8,128)(2,1)S(1)}, u32[]{:S(2)}, u32[]{:S(2)}) collective-permute-start(bf16[5,32,1280]{2,1,0:T(8,128)(2,1)S(1)} %shard_map.109._.own_rows), channel_id=1, source_target_pairs={{0,32},{32,64},{64,96},{96,0},{1,33},{33,65},{65,97},{97,1},{2,34}... | collective-permute-start | bytes 1228808 | tf_op jit(solution)/shard_map/ppermute | solution.py:31
  15.2 21.7 %collective-permute-start.1 = (bf16[5,32,1280]{2,1,0:T(8,128)(2,1)S(1)}, bf16[5,32,1280]{2,1,0:T(8,128)(2,1)S(1)}, u32[]{:S(2)}, u32[]{:S(2)}) collective-permute-start(bf16[5,32,1280]{2,1,0:T(8,128)(2,1)S(1)} %shard_map.109._.own_rows), channel_id=1, source_target_pairs={{0,64},{32,96},{64,0},{96,32},{1,65},{33,97},{65,1},{97,33},{2,66}... | collective-permute-start | bytes 1228808 | tf_op jit(solution)/shard_map/ppermute | solution.py:31
  15.3 24.0 %collective-permute-start.2 = (bf16[5,32,1280]{2,1,0:T(8,128)(2,1)S(1)}, bf16[5,32,1280]{2,1,0:T(8,128)(2,1)S(1)}, u32[]{:S(2)}, u32[]{:S(2)}) collective-permute-start(bf16[5,32,1280]{2,1,0:T(8,128)(2,1)S(1)} %shard_map.109._.own_rows), channel_id=1, source_target_pairs={{0,96},{32,0},{64,32},{96,64},{1,97},{33,1},{65,33},{97,65},{2,98}... | collective-permute-start | bytes 1228808 | tf_op jit(solution)/shard_map/ppermute | solution.py:31
  26.9 21.6 %collective-permute-start.6 = (bf16[4,32,1280]{2,1,0:T(8,128)(2,1)S(1)}, bf16[4,32,1280]{2,1,0:T(8,128)(2,1)S(1)}, u32[]{:S(2)}, u32[]{:S(2)}) collective-permute-start(bf16[4,32,1280]{2,1,0:T(8,128)(2,1)S(1)} %get-tuple-element.31), channel_id=1, source_target_pairs={{0,32},{32,64},{64,96},{96,0},{1,33},{33,65},{65,97},{97,1},{2,34}... | collective-permute-start | bytes 983048 | tf_op jit(solution)/shard_map/ppermute | solution.py:31
  27.5 42.7 %collective-permute-start.7 = (bf16[4,32,1280]{2,1,0:T(8,128)(2,1)}, bf16[4,32,1280]{2,1,0:T(8,128)(2,1)}, u32[]{:S(2)}, u32[]{:S(2)}) collective-permute-start(bf16[4,32,1280]{2,1,0:T(8,128)(2,1)} %get-tuple-element.32), channel_id=1, source_target_pairs={{0,64},{32,96},{64,0},{96,32},{1,65},{33,97},{65,1},{97,33},{2,66}... | collective-permute-start | bytes 983048 | tf_op jit(solution)/shard_map/ppermute | solution.py:31
  35.4 16.3 %copy-start.15 = (s32[64,1]{0,1:T(1,128)S(1)}, s32[64,1]{0,1:T(1,128)}, u32[]{:S(2)}) copy-start(s32[64,1]{0,1:T(1,128)} %param.14) | copy-start | bytes 772
  35.4 16.4 %copy-start.13 = (s32[32]{0:T(128)S(1)}, s32[32]{0:T(128)}, u32[]{:S(2)}) copy-start(s32[32]{0:T(128)} %param.12) | copy-start | bytes 388
  35.4 16.4 %copy-start.14 = (s32[64]{0:T(128)S(1)}, s32[64]{0:T(128)}, u32[]{:S(2)}) copy-start(s32[64]{0:T(128)} %param.13) | copy-start | bytes 772
  35.4 34.9 %copy-start.4 = (bf16[1280,1024]{1,0:T(8,128)(2,1)S(1)}, bf16[1280,1024]{1,0:T(8,128)(2,1)}, u32[]{:S(2)}) copy-start(bf16[1280,1024]{1,0:T(8,128)(2,1)} %refs_8_.1) | copy-start | bytes 7864324
  35.4 34.8 %collective-permute-start.8 = (bf16[4,32,1280]{2,1,0:T(8,128)(2,1)}, bf16[4,32,1280]{2,1,0:T(8,128)(2,1)}, u32[]{:S(2)}, u32[]{:S(2)}) collective-permute-start(bf16[4,32,1280]{2,1,0:T(8,128)(2,1)} %get-tuple-element.33), channel_id=1, source_target_pairs={{0,96},{32,0},{64,32},{96,64},{1,97},{33,1},{65,33},{97,65},{2,98}... | collective-permute-start | bytes 983048 | tf_op jit(solution)/shard_map/ppermute | solution.py:31
  44.5 0.7 copy-start.9
  45.2 0.7 copy-start.11
  46.0 24.3 %collective-permute-start.10 = (bf16[4,32,1280]{2,1,0:T(8,128)(2,1)}, bf16[4,32,1280]{2,1,0:T(8,128)(2,1)}, u32[]{:S(2)}, u32[]{:S(2)}) collective-permute-start(bf16[4,32,1280]{2,1,0:T(8,128)(2,1)} %get-tuple-element.36), channel_id=1, source_target_pairs={{0,64},{32,96},{64,0},{96,32},{1,65},{33,97},{65,1},{97,33},{2,66}... | collective-permute-start | bytes 983048 | tf_op jit(solution)/shard_map/ppermute | solution.py:31
  48.5 21.8 %collective-permute-start.11 = (bf16[4,32,1280]{2,1,0:T(8,128)(2,1)}, bf16[4,32,1280]{2,1,0:T(8,128)(2,1)}, u32[]{:S(2)}, u32[]{:S(2)}) collective-permute-start(bf16[4,32,1280]{2,1,0:T(8,128)(2,1)} %get-tuple-element.37), channel_id=1, source_target_pairs={{0,96},{32,0},{64,32},{96,64},{1,97},{33,1},{65,33},{97,65},{2,98}... | collective-permute-start | bytes 983048 | tf_op jit(solution)/shard_map/ppermute | solution.py:31
  48.5 21.8 %collective-permute-start.9 = (bf16[4,32,1280]{2,1,0:T(8,128)(2,1)}, bf16[4,32,1280]{2,1,0:T(8,128)(2,1)}, u32[]{:S(2)}, u32[]{:S(2)}) collective-permute-start(bf16[4,32,1280]{2,1,0:T(8,128)(2,1)} %get-tuple-element.35), channel_id=1, source_target_pairs={{0,32},{32,64},{64,96},{96,0},{1,33},{33,65},{65,97},{97,1},{2,34}... | collective-permute-start | bytes 983048 | tf_op jit(solution)/shard_map/ppermute | solution.py:31
  51.8 1.0 copy-start.12
  70.3 1.7 %copy-start.5 = (bf16[1280,1024]{1,0:T(8,128)(2,1)S(1)}, bf16[1280,1024]{1,0:T(8,128)(2,1)}, u32[]{:S(2)}) copy-start(bf16[1280,1024]{1,0:T(8,128)(2,1)} %refs_9_.1) | copy-start | bytes 7864324
  72.0 1.0 copy-start.10
  73.0 28.5 %copy-start = (bf16[256,8192]{1,0:T(8,128)(2,1)S(1)}, bf16[256,8192]{1,0:T(8,128)(2,1)}, u32[]{:S(2)}) copy-start(bf16[256,8192]{1,0:T(8,128)(2,1)} %weight_ref.5) | copy-start | bytes 12582916
  92.9 4.6 %collective-permute-start.12 = (bf16[208,128]{1,0:T(8,128)(2,1)S(1)}, bf16[208,128]{1,0:T(8,128)(2,1)S(1)}, u32[]{:S(2)}, u32[]{:S(2)}) collective-permute-start(bf16[208,128]{1,0:T(8,128)(2,1)S(1)} %get-tuple-element.40), channel_id=1, source_target_pairs={{0,32},{32,64},{64,96},{96,0},{1,33},{33,65},{65,97},{97,1},{2,34}... | collective-permute-start | bytes 159752 | tf_op jit(solution)/shard_map/ppermute | solution.py:31
  94.0 5.9 %collective-permute-start.13 = (bf16[208,128]{1,0:T(8,128)(2,1)S(1)}, bf16[208,128]{1,0:T(8,128)(2,1)S(1)}, u32[]{:S(2)}, u32[]{:S(2)}) collective-permute-start(bf16[208,128]{1,0:T(8,128)(2,1)S(1)} %get-tuple-element.41), channel_id=1, source_target_pairs={{0,64},{32,96},{64,0},{96,32},{1,65},{33,97},{65,1},{97,33},{2,66}... | collective-permute-start | bytes 159752 | tf_op jit(solution)/shard_map/ppermute | solution.py:31
  96.1 5.3 %collective-permute-start.14 = (bf16[208,128]{1,0:T(8,128)(2,1)S(1)}, bf16[208,128]{1,0:T(8,128)(2,1)S(1)}, u32[]{:S(2)}, u32[]{:S(2)}) collective-permute-start(bf16[208,128]{1,0:T(8,128)(2,1)S(1)} %get-tuple-element.42), channel_id=1, source_target_pairs={{0,96},{32,0},{64,32},{96,64},{1,97},{33,1},{65,33},{97,65},{2,98}... | collective-permute-start | bytes 159752 | tf_op jit(solution)/shard_map/ppermute | solution.py:31
  102.6 2.4 %collective-permute-start.15 = (bf16[4,4,96,256]{3,2,1,0:T(8,128)(2,1)S(1)}, bf16[4,4,96,256]{3,2,1,0:T(8,128)(2,1)S(1)}, u32[]{:S(2)}, u32[]{:S(2)}) collective-permute-start(bf16[4,4,96,256]{3,2,1,0:T(8,128)(2,1)S(1)} %shard_map.118), channel_id=1, source_target_pairs={{0,1},{1,0},{2,3},{3,2},{4,5},{5,4},{6,7},{7,6},{8,9},{9,8},{10,11... | collective-permute-start | bytes 2359304 | tf_op jit(solution)/shard_map/ppermute | solution.py:41
  105.1 12.4 %collective-permute-start.16 = (bf16[4,96,256]{2,1,0:T(8,128)(2,1)S(1)}, bf16[4,96,256]{2,1,0:T(8,128)(2,1)S(1)}, u32[]{:S(2)}, u32[]{:S(2)}) collective-permute-start(bf16[4,96,256]{2,1,0:T(8,128)(2,1)S(1)} %get-tuple-element.44), channel_id=1, source_target_pairs={{0,8},{1,9},{2,10},{3,11},{4,12},{5,13},{6,14},{7,15},{8,16},{9,17... | collective-permute-start | bytes 589832 | tf_op jit(solution)/shard_map/ppermute | solution.py:41
  105.5 12.0 %collective-permute-start.17 = (bf16[4,96,256]{2,1,0:T(8,128)(2,1)S(1)}, bf16[4,96,256]{2,1,0:T(8,128)(2,1)S(1)}, u32[]{:S(2)}, u32[]{:S(2)}) collective-permute-start(bf16[4,96,256]{2,1,0:T(8,128)(2,1)S(1)} %get-tuple-element.45), channel_id=1, source_target_pairs={{0,16},{1,17},{2,18},{3,19},{4,20},{5,21},{6,22},{7,23},{8,24},{9,... | collective-permute-start | bytes 589832 | tf_op jit(solution)/shard_map/ppermute | solution.py:41
  107.6 10.6 %collective-permute-start.18 = (bf16[4,96,256]{2,1,0:T(8,128)(2,1)S(1)}, bf16[4,96,256]{2,1,0:T(8,128)(2,1)S(1)}, u32[]{:S(2)}, u32[]{:S(2)}) collective-permute-start(bf16[4,96,256]{2,1,0:T(8,128)(2,1)S(1)} %get-tuple-element.46), channel_id=1, source_target_pairs={{0,24},{1,25},{2,26},{3,27},{4,28},{5,29},{6,30},{7,31},{8,0},{9,1... | collective-permute-start | bytes 589832 | tf_op jit(solution)/shard_map/ppermute | solution.py:41
  118.3 5.4 %collective-permute-start.19 = (bf16[96,256]{1,0:T(8,128)(2,1)S(1)}, bf16[96,256]{1,0:T(8,128)(2,1)S(1)}, u32[]{:S(2)}, u32[]{:S(2)}) collective-permute-start(bf16[96,256]{1,0:T(8,128)(2,1)S(1)} %get-tuple-element.48), channel_id=1, source_target_pairs={{0,2},{1,3},{2,4},{3,5},{4,6},{5,7},{6,0},{7,1},{8,10},{9,11},{10,... | collective-permute-start | bytes 147464 | tf_op jit(solution)/shard_map/ppermute | solution.py:41
  118.9 5.6 %collective-permute-start.20 = (bf16[96,256]{1,0:T(8,128)(2,1)S(1)}, bf16[96,256]{1,0:T(8,128)(2,1)S(1)}, u32[]{:S(2)}, u32[]{:S(2)}) collective-permute-start(bf16[96,256]{1,0:T(8,128)(2,1)S(1)} %get-tuple-element.49), channel_id=1, source_target_pairs={{0,4},{1,5},{2,6},{3,7},{4,0},{5,1},{6,2},{7,3},{8,12},{9,13},{10,... | collective-permute-start | bytes 147464 | tf_op jit(solution)/shard_map/ppermute | solution.py:41
  120.9 4.1 %collective-permute-start.21 = (bf16[96,256]{1,0:T(8,128)(2,1)S(1)}, bf16[96,256]{1,0:T(8,128)(2,1)S(1)}, u32[]{:S(2)}, u32[]{:S(2)}) collective-permute-start(bf16[96,256]{1,0:T(8,128)(2,1)S(1)} %get-tuple-element.50), channel_id=1, source_target_pairs={{0,6},{1,7},{2,0},{3,1},{4,2},{5,3},{6,4},{7,5},{8,14},{9,15},{10,... | collective-permute-start | bytes 147464 | tf_op jit(solution)/shard_map/ppermute | solution.py:41

commit v4 on v3

--- a/solution.py
+++ b/solution.py
@@ -81,7 +81,7 @@
 def feed_forward_kernel(
     half, at_ref, patches_ref, own_rows, one_rows, two_rows, three_rows, fc1_ref, fc2_ref, *refs
 ):
-    total_ref, one_ref, two_ref, three_ref, *query_refs, rows_ref, wide_ref = refs[1:]
+    total_ref, one_ref, two_ref, three_ref, *query_refs, rows_ref, wide_ref = refs[2:]
     for ref in query_refs:
         for source, rows in enumerate((own_rows, one_rows, two_rows, three_rows)):
             ref[source] = rows[RING]
@@ -196,16 +196,13 @@
     return lax.broadcasted_iota(jnp.int32, shape, dim)
 
 
-def select_kernel(
-    slots, steps, heads, capacity, at_ref, enc_ref, req_ref, owner_ref,
-    *refs,
+def tables_kernel(
+    slots, steps, heads, capacity, at_ref, enc_ref, req_ref, owner_ref, _, target_ref
 ):
-    sources, chosen_ref, target_ref = refs
-    here = at_ref[0]
     columns, requests = enc_ref.shape[1], req_ref.shape[1]
     halves = capacity // RING
     per_group = heads * slots * steps
-    rows = columns * halves * heads * steps
+    rows = target_ref.shape[0]
     before = iota((requests, requests), 0) < iota((requests, requests), 1)
     equal = iota((requests, requests), 0) == iota((requests, requests), 1)
     req_row = req_ref[...]
@@ -226,46 +223,58 @@
     row = iota((rows, 1), 0)
     per_tile = heads * steps
     column = row // (halves * per_tile)
-    slot = row // per_tile % halves * RING + here
+    slot = row // per_tile % halves * RING + at_ref[0]
+    within = row % per_tile
     hit = column == iota((rows, columns), 1)
     count = jnp.sum(jnp.where(hit, enc_row, 0), axis=1, keepdims=True)
     start = jnp.sum(jnp.where(hit, enc_start, 0), axis=1, keepdims=True)
     tile = jnp.where(slot < count, start + slot, -1)
     has = (req_start <= tile) & (tile < req_start + req_row)
     base = jnp.sum(jnp.where(has, place + 1, 0), axis=1, keepdims=True) - 1
-    within = row % per_tile
-    target = jnp.where(base < 0, -1, base + within // steps * (slots * steps) + within % steps)
-    target_ref[...] = target
-    chosen = jnp.zeros((rows, HEAD_DIM), F32)
+    target_ref[...] = jnp.where(
+        base < 0, -1, base + within // steps * (slots * steps) + within % steps
+    )
+
+
+def tables(at, enc, req, owner, slots, steps, heads, capacity, after):
+    rows = enc.shape[1] * (capacity // RING) * heads * steps
+    return pl.pallas_call(
+        functools.partial(tables_kernel, slots, steps, heads, capacity),
+        out_shape=jax.ShapeDtypeStruct((rows, 1), jnp.int32),
+        in_specs=[SMEM] + [VMEM] * 3 + [pl.BlockSpec(memory_space=pl.ANY)],
+        out_specs=VMEM,
+        compiler_params=params(8),
+    )(at, enc, req, owner, after)
+
+
+def select_kernel(per_group, at_ref, target_ref, sources_ref, chosen_ref):
+    target = target_ref[...]
+    chosen = jnp.zeros(chosen_ref.shape, F32)
     for shift in range(RING):
-        group = lax.rem(here - shift + RING, RING)
-        match = target == iota((rows, per_group), 1) + group * per_group
+        group = lax.rem(at_ref[0] - shift + RING, RING)
+        match = target == iota((target.shape[0], per_group), 1) + group * per_group
+        pieces = per_group // sources_ref.shape[1]
+        queries = jnp.concatenate(
+            [
+                sources_ref[shift, :, i * HEAD_DIM : (i + 1) * HEAD_DIM]
+                for i in range(pieces)
+            ],
+            axis=0,
+        )
         chosen = chosen + jnp.dot(
-            jnp.where(match, 1.0, 0.0).astype(BF16),
-            jnp.concatenate(
-                [
-                    sources[shift, :, lane : lane + HEAD_DIM]
-                    for lane in range(0, per_group // sources.shape[1] * HEAD_DIM, HEAD_DIM)
-                ],
-                axis=0,
-            ),
-            preferred_element_type=F32,
+            jnp.where(match, 1.0, 0.0).astype(BF16), queries, preferred_element_type=F32
         )
     chosen_ref[...] = chosen.astype(BF16)
 
 
-def select(at, enc, req, owner, queries, slots, steps, heads, capacity):
-    rows = enc.shape[1] * (capacity // RING) * heads * steps
-    return pl.pallas_call(
-        functools.partial(select_kernel, slots, steps, heads, capacity),
-        out_shape=(
-            jax.ShapeDtypeStruct((rows, HEAD_DIM), BF16),
-            jax.ShapeDtypeStruct((rows, 1), jnp.int32),
-        ),
-        in_specs=[SMEM] + [VMEM] * 4,
-        out_specs=(VMEM, VMEM),
-        compiler_params=params(8),
-    )(at, enc, req, owner, queries)
+def select(at, target, sources, per_group):
+    return pl.pallas_call(
+        functools.partial(select_kernel, per_group),
+        out_shape=jax.ShapeDtypeStruct((target.shape[0], HEAD_DIM), BF16),
+        in_specs=[SMEM, VMEM, VMEM],
+        out_specs=VMEM,
+        compiler_params=params(8),
+    )(at, target, sources)
 
 
 def attend_kernel(*refs):
@@ -518,24 +527,25 @@
     own = [normalize(at, patches), second_half(at, text_hidden, query_weight, patches)]
     sources = [[rows] + [pool_shift(rows, s) for s in range(1, RING)] for rows in own]
     held = hold(fc1_weight, fc2_weight, sources[1][0])
-    sums, queries = [], None
-    for i in range(halves):
-        total, *messages = feed_forward(
-            at, patches, sources[i], fc1_weight, fc2_weight, i, (held,)
-        )
-        queries = messages[-1]
-        sums += [total] + [pool_shift(messages[s - 1], s) for s in range(1, RING)]
-    chosen, target = select(
+    target = tables(
         at,
         enc_tiles.reshape(1, -1),
         req_tiles.reshape(1, -1),
         req_owner,
-        queries,
         slots,
         steps,
         local_heads,
         capacity,
+        sources[1][0],
     )
+    sums, queries = [], None
+    for i in range(halves):
+        total, *messages = feed_forward(
+            at, patches, sources[i], fc1_weight, fc2_weight, i, (held, target)
+        )
+        queries = messages[-1]
+        sums += [total] + [pool_shift(messages[s - 1], s) for s in range(1, RING)]
+    chosen = select(at, target, queries, local_heads * slots * steps)
     per_device = halves * local_heads * steps
     tile_queries = lax.all_to_all(
         chosen.reshape(devices, per_device, HEAD_DIM), "dev", split_axis=0, concat_axis=0, tiled=True

time: 126 us -> 124 us (0.984)
  waiting for transfers between devices: 25.4 us -> 21.2 us
  blocking collectives: 28.7 us -> 32.4 us
  starting transfers between devices: 34.4 us -> 32.7 us
    ppermute x15, waiting for transfers between devices: 12.8 us -> 8.63 us  [pool_shift(): return lax.ppermute(x, 'pool', [(i, (i + by) % RING) for i in range(RING)])]
    all_to_all x1, blocking collectives: 12.7 us -> 16.5 us  [body(): lax.all_to_all(packed.reshape(devices, per_device, 2 * HEAD_DIM), 'dev',...]
    pallas_call x2, Pallas kernels: 10.4 us -> 8.55 us  [feed_forward(): pl.pallas_call(functools.partial(feed_forward_kernel, half), out_shape=(s...]
    ppermute x15, starting transfers between devices: 26.7 us -> 24.9 us  [pool_shift(): return lax.ppermute(x, 'pool', [(i, (i + by) % RING) for i in range(RING)])]
    unnamed x33 -> x31, local copies, waits for them, and re-layouts: 11 us -> 11.5 us
  transfers between devices with their start and end apart: 22 -> 22, of which waited for: 11 -> 10; matrix products, arithmetic and copies ran while one was open for 1% -> 1% of each run, Pallas kernels for 12% -> 11%
where the time goes in v4:
time: 124 us; the launch traced here: 123 us
  starting transfers between devices  32.7 us (26%)
  blocking collectives  32.4 us (26%)
  Pallas kernels  24.3 us (20%)
  waiting for transfers between devices  21.2 us (17%)
  local copies, waits for them, and re-layouts  12.3 us (10%)
    ppermute x15, starting transfers between devices, pool_shift(): return lax.ppermute(x, 'pool', [(i, (i + by) % RING) for i in range(RING)])  24.9 us
    all_to_all x1, blocking collectives, body(): lax.all_to_all(packed.reshape(devices, per_device, 2 * HEAD_DIM), 'dev',...  16.5 us
    all_to_all x1, blocking collectives, body(): lax.all_to_all(chosen.reshape(devices, per_device, HEAD_DIM), 'dev', spli...  15.9 us
    ppermute x7, waiting for transfers between devices, dev_shift(): return lax.ppermute(x, 'dev', pairs)  12.5 us
    unnamed x31, local copies, waits for them, and re-layouts  11.5 us
    ppermute x15, waiting for transfers between devices, pool_shift(): return lax.ppermute(x, 'pool', [(i, (i + by) % RING) for i in range(RING)])  8.63 us
    pallas_call x2, Pallas kernels, feed_forward(): pl.pallas_call(functools.partial(feed_forward_kernel, half), out_shape=(s...  8.55 us
    ppermute x7, starting transfers between devices, dev_shift(): return lax.ppermute(x, 'dev', pairs)  7.72 us
  transfers between devices with their start and end apart: 22, of which 10 were waited for; matrix products, arithmetic and copies ran while one was open for 1% of the time, Pallas kernels for 11%

profile of v4, /device:TPU:6, one launch (start us, length us, event | category | flops | bytes accessed | tf_op | source)
XLA Modules:
  0.0 123.2 jit_solution(4192405371856001234)
XLA Ops:
  0.1 1.1 copy-done.8
  1.2 0.8 shard_map.111.own_rows
  2.0 0.5 collective-permute-start
  2.5 2.5 %collective-permute-start.1 = (bf16[4,32,1280]{2,1,0:T(8,128)(2,1)S(1)}, bf16[4,32,1280]{2,1,0:T(8,128)(2,1)S(1)}, u32[]{:S(2)}, u32[]{:S(2)}) collective-permute-start(bf16[4,32,1280]{2,1,0:T(8,128)(2,1)S(1)} %shard_map.111.own_rows), channel_id=1, source_target_pairs={{0,64},{32,96},{64,0},{96,32},{1,65},{33,97},{65,1},{97,33},{2,66}... | collective-permute-start | bytes 983048 | tf_op jit(solution)/shard_map/ppermute | solution.py:31
  5.0 2.2 %copy-done.1 = bf16[8192,256]{1,0:T(8,128)(2,1)S(1)} copy-done((bf16[8192,256]{1,0:T(8,128)(2,1)S(1)}, bf16[8192,256]{1,0:T(8,128)(2,1)}, u32[]{:S(2)}) %copy-start.1) | copy-done | bytes 4194328
  7.2 1.1 copy-done.9
  8.2 1.4 %copy-done.11 = bf16[24,4,8192]{2,1,0:T(4,128)(2,1)S(1)} copy-done((bf16[24,4,8192]{2,1,0:T(4,128)(2,1)S(1)}, bf16[24,4,8192]{2,1,0:T(4,128)(2,1)}, u32[]{:S(2)}) %copy-start.11) | copy-done | bytes 1572888
  9.7 2.2 %shard_map.109._.own_rows = bf16[5,32,1280]{2,1,0:T(8,128)(2,1)S(1)} custom-call(s32[2]{0:T(128)S(1)} %pad_add_fusion.at_ref, bf16[24,4,8192]{2,1,0:T(4,128)(2,1)S(1)} %copy-done.11, bf16[8192,256]{1,0:T(8,128)(2,1)S(1)} %copy-done.1, bf16[8,32,1280]{2,1,0:T(8,128)(2,1)S(1)} %copy-done.9), custom_call_target="tpu_custom_call" | custom-call | flops 402653184 | bytes 5767168 | tf_op jit(solution)/shard_map/pallas_call | solution.py:174
  11.9 3.3 %collective-permute-start.6 = (bf16[5,32,1280]{2,1,0:T(8,128)(2,1)S(1)}, bf16[5,32,1280]{2,1,0:T(8,128)(2,1)S(1)}, u32[]{:S(2)}, u32[]{:S(2)}) collective-permute-start(bf16[5,32,1280]{2,1,0:T(8,128)(2,1)S(1)} %shard_map.109._.own_rows), channel_id=1, source_target_pairs={{0,32},{32,64},{64,96},{96,0},{1,33},{33,65},{65,97},{97,1},{2,34}... | collective-permute-start | bytes 1228808 | tf_op jit(solution)/shard_map/ppermute | solution.py:31
  15.3 1.3 %collective-permute-start.8 = (bf16[5,32,1280]{2,1,0:T(8,128)(2,1)S(1)}, bf16[5,32,1280]{2,1,0:T(8,128)(2,1)S(1)}, u32[]{:S(2)}, u32[]{:S(2)}) collective-permute-start(bf16[5,32,1280]{2,1,0:T(8,128)(2,1)S(1)} %shard_map.109._.own_rows), channel_id=1, source_target_pairs={{0,96},{32,0},{64,32},{96,64},{1,97},{33,1},{65,33},{97,65},{2,98}... | collective-permute-start | bytes 1228808 | tf_op jit(solution)/shard_map/ppermute | solution.py:31
  16.7 1.9 %copy-done.2 = bf16[1280,1280]{1,0:T(8,128)(2,1)S(1)} copy-done((bf16[1280,1280]{1,0:T(8,128)(2,1)S(1)}, bf16[1280,1280]{1,0:T(8,128)(2,1)}, u32[]{:S(2)}) %copy-start.2) | copy-done | bytes 3276824
  18.7 1.9 %copy-done.4 = bf16[1280,1280]{1,0:T(8,128)(2,1)S(1)} copy-done((bf16[1280,1280]{1,0:T(8,128)(2,1)S(1)}, bf16[1280,1280]{1,0:T(8,128)(2,1)}, u32[]{:S(2)}) %copy-start.4) | copy-done | bytes 3276824
  20.6 1.2 shard_map.110.refs_1_.target_ref
  21.8 0.7 copy-done.3
  22.5 1.0 copy-done.5
  23.6 4.3 %shard_map.113 = (bf16[4,32,1280]{2,1,0:T(8,128)(2,1)S(1)}, bf16[4,32,1280]{2,1,0:T(8,128)(2,1)S(1)}, bf16[4,32,1280]{2,1,0:T(8,128)(2,1)S(1)}, bf16[4,32,1280]{2,1,0:T(8,128)(2,1)S(1)}) custom-call(s32[2]{0:T(128)S(1)} %pad_add_fusion.at_ref, bf16[8,32,1280]{2,1,0:T(8,128)(2,1)S(1)} %copy-done.10, bf16[4,32,1280]{2,1,0:T(8,128)(2,1)S(1)} %shard_map.111.own_rows, ...), custom_call_target="tpu_custom_call" | custom-call | flops 3355443200 | bytes 6553600 | tf_op jit(solution)/shard_map/pallas_call | solution.py:116
  27.9 2.0 %collective-permute-start.3 = (bf16[4,32,1280]{2,1,0:T(8,128)(2,1)S(1)}, bf16[4,32,1280]{2,1,0:T(8,128)(2,1)S(1)}, u32[]{:S(2)}, u32[]{:S(2)}) collective-permute-start(bf16[4,32,1280]{2,1,0:T(8,128)(2,1)S(1)} %get-tuple-element.27), channel_id=1, source_target_pairs={{0,32},{32,64},{64,96},{96,0},{1,33},{33,65},{65,97},{97,1},{2,34}... | collective-permute-start | bytes 983048 | tf_op jit(solution)/shard_map/ppermute | solution.py:31
  29.8 4.8 %collective-permute-start.4 = (bf16[4,32,1280]{2,1,0:T(8,128)(2,1)S(1)}, bf16[4,32,1280]{2,1,0:T(8,128)(2,1)S(1)}, u32[]{:S(2)}, u32[]{:S(2)}) collective-permute-start(bf16[4,32,1280]{2,1,0:T(8,128)(2,1)S(1)} %get-tuple-element.28), channel_id=1, source_target_pairs={{0,64},{32,96},{64,0},{96,32},{1,65},{33,97},{65,1},{97,33},{2,66}... | collective-permute-start | bytes 983048 | tf_op jit(solution)/shard_map/ppermute | solution.py:31
  34.7 1.3 %collective-permute-start.5 = (bf16[4,32,1280]{2,1,0:T(8,128)(2,1)S(1)}, bf16[4,32,1280]{2,1,0:T(8,128)(2,1)S(1)}, u32[]{:S(2)}, u32[]{:S(2)}) collective-permute-start(bf16[4,32,1280]{2,1,0:T(8,128)(2,1)S(1)} %get-tuple-element.29), channel_id=1, source_target_pairs={{0,96},{32,0},{64,32},{96,64},{1,97},{33,1},{65,33},{97,65},{2,98}... | collective-permute-start | bytes 983048 | tf_op jit(solution)/shard_map/ppermute | solution.py:31
  36.0 3.3 %collective-permute-done.8.three_rows = bf16[5,32,1280]{2,1,0:T(8,128)(2,1)S(1)} collective-permute-done((bf16[5,32,1280]{2,1,0:T(8,128)(2,1)S(1)}, bf16[5,32,1280]{2,1,0:T(8,128)(2,1)S(1)}, u32[]{:S(2)}, u32[]{:S(2)}) %collective-permute-start.8) | collective-permute-done | bytes 409632 | tf_op jit(solution)/shard_map/ppermute | solution.py:31
  39.3 4.3 %shard_map.114 = (bf16[4,32,1280]{2,1,0:T(8,128)(2,1)S(1)}, bf16[4,32,1280]{2,1,0:T(8,128)(2,1)S(1)}, bf16[4,32,1280]{2,1,0:T(8,128)(2,1)S(1)}, bf16[4,32,1280]{2,1,0:T(8,128)(2,1)S(1)}, bf16[4,32,1280]{2,1,0:T(8,128)(2,1)S(1)}) custom-call(s32[2]{0:T(128)S(1)} %pad_add_fusion.at_ref, bf16[8,32,1280]{2,1,0:T(8,128)(2,1)S(1)} %copy-done.10, ...), custom_call_target="tpu_custom_call" | custom-call | flops 3355443200 | bytes 6553600 | tf_op jit(solution)/shard_map/pallas_call | solution.py:116
  43.6 2.6 %collective-permute-start.10 = (bf16[4,32,1280]{2,1,0:T(8,128)(2,1)S(1)}, bf16[4,32,1280]{2,1,0:T(8,128)(2,1)S(1)}, u32[]{:S(2)}, u32[]{:S(2)}) collective-permute-start(bf16[4,32,1280]{2,1,0:T(8,128)(2,1)S(1)} %get-tuple-element.32), channel_id=1, source_target_pairs={{0,64},{32,96},{64,0},{96,32},{1,65},{33,97},{65,1},{97,33},{2,66}... | collective-permute-start | bytes 983048 | tf_op jit(solution)/shard_map/ppermute | solution.py:31
  46.2 3.2 %collective-permute-start.9 = (bf16[4,32,1280]{2,1,0:T(8,128)(2,1)S(1)}, bf16[4,32,1280]{2,1,0:T(8,128)(2,1)S(1)}, u32[]{:S(2)}, u32[]{:S(2)}) collective-permute-start(bf16[4,32,1280]{2,1,0:T(8,128)(2,1)S(1)} %get-tuple-element.31), channel_id=1, source_target_pairs={{0,32},{32,64},{64,96},{96,0},{1,33},{33,65},{65,97},{97,1},{2,34}... | collective-permute-start | bytes 983048 | tf_op jit(solution)/shard_map/ppermute | solution.py:31
  49.4 1.0 shard_map.115
  50.4 15.9 %all_to_all.10 = bf16[32,16,128]{2,1,0:T(8,128)(2,1)S(1)} all-to-all(bf16[32,16,128]{2,1,0:T(8,128)(2,1)S(1)} %bitcast.11), channel_id=1, replica_groups=mesh['pool'=4,'dev'=32] {'dev'}, dimensions={0} | all-to-all | bytes 262144 | tf_op jit(solution)/shard_map/all_to_all | solution.py:550
  66.4 6.3 %shard_map.116 = bf16[8,4,16,256]{3,2,1,0:T(8,128)(2,1)S(1)} custom-call(bf16[4,32,1280]{2,1,0:T(8,128)(2,1)S(1)} %get-tuple-element.26.refs_0_, bf16[4,32,1280]{2,1,0:T(8,128)(2,1)S(1)} %collective-permute-done.3.refs_1_, bf16[4,32,1280]{2,1,0:T(8,128)(2,1)S(1)} %collective-permute-done.4.refs_2_, bf16[4,32,1280]{2,1,0:T(8,128)(2,1)S(1)} %collective-permute-done.5.refs_3_, ...), custom_call_target="tpu_custom_call" | custom-call | flops 1342177280 | bytes 5242880 | tf_op jit(solution)/shard_map/pallas_call | solution.py:353
  72.7 16.5 %all_to_all.11 = bf16[32,16,256]{2,1,0:T(8,128)(2,1)S(1)} all-to-all(bf16[32,16,256]{2,1,0:T(8,128)(2,1)S(1)} %bitcast.8), channel_id=1, replica_groups=mesh['pool'=4,'dev'=32] {'dev'}, dimensions={0} | all-to-all | bytes 524288 | tf_op jit(solution)/shard_map/all_to_all | solution.py:554
  89.2 1.2 shard_map.117
  90.4 1.1 collective-permute-start.12
  91.5 2.1 %collective-permute-start.13 = (bf16[208,128]{1,0:T(8,128)(2,1)S(1)}, bf16[208,128]{1,0:T(8,128)(2,1)S(1)}, u32[]{:S(2)}, u32[]{:S(2)}) collective-permute-start(bf16[208,128]{1,0:T(8,128)(2,1)S(1)} %get-tuple-element.37), channel_id=1, source_target_pairs={{0,64},{32,96},{64,0},{96,32},{1,65},{33,97},{65,1},{97,33},{2,66}... | collective-permute-start | bytes 159752 | tf_op jit(solution)/shard_map/ppermute | solution.py:31
  93.6 1.4 %collective-permute-done.12.one_ref = bf16[208,128]{1,0:T(8,128)(2,1)S(1)} collective-permute-done((bf16[208,128]{1,0:T(8,128)(2,1)S(1)}, bf16[208,128]{1,0:T(8,128)(2,1)S(1)}, u32[]{:S(2)}, u32[]{:S(2)}) %collective-permute-start.12) | collective-permute-done | bytes 53280 | tf_op jit(solution)/shard_map/ppermute | solution.py:31
  95.0 2.4 %collective-permute-done.13.two_ref = bf16[208,128]{1,0:T(8,128)(2,1)S(1)} collective-permute-done((bf16[208,128]{1,0:T(8,128)(2,1)S(1)}, bf16[208,128]{1,0:T(8,128)(2,1)S(1)}, u32[]{:S(2)}, u32[]{:S(2)}) %collective-permute-start.13) | collective-permute-done | bytes 53280 | tf_op jit(solution)/shard_map/ppermute | solution.py:31
  97.4 1.6 %collective-permute-done.14.three_ref = bf16[208,128]{1,0:T(8,128)(2,1)S(1)} collective-permute-done((bf16[208,128]{1,0:T(8,128)(2,1)S(1)}, bf16[208,128]{1,0:T(8,128)(2,1)S(1)}, u32[]{:S(2)}, u32[]{:S(2)}) %collective-permute-start.14) | collective-permute-done | bytes 53280 | tf_op jit(solution)/shard_map/ppermute | solution.py:31
  99.0 1.1 shard_map.119
  100.1 1.1 shard_map.118.kept_ref
  101.2 1.2 collective-permute-done.15.got_ref
  103.0 2.1 %collective-permute-start.17 = (bf16[4,96,256]{2,1,0:T(8,128)(2,1)S(1)}, bf16[4,96,256]{2,1,0:T(8,128)(2,1)S(1)}, u32[]{:S(2)}, u32[]{:S(2)}) collective-permute-start(bf16[4,96,256]{2,1,0:T(8,128)(2,1)S(1)} %get-tuple-element.41), channel_id=1, source_target_pairs={{0,16},{1,17},{2,18},{3,19},{4,20},{5,21},{6,22},{7,23},{8,24},{9,... | collective-permute-start | bytes 589832 | tf_op jit(solution)/shard_map/ppermute | solution.py:41
  105.1 1.3 %collective-permute-start.18 = (bf16[4,96,256]{2,1,0:T(8,128)(2,1)S(1)}, bf16[4,96,256]{2,1,0:T(8,128)(2,1)S(1)}, u32[]{:S(2)}, u32[]{:S(2)}) collective-permute-start(bf16[4,96,256]{2,1,0:T(8,128)(2,1)S(1)} %get-tuple-element.42), channel_id=1, source_target_pairs={{0,24},{1,25},{2,26},{3,27},{4,28},{5,29},{6,30},{7,31},{8,0},{9,1... | collective-permute-start | bytes 589832 | tf_op jit(solution)/shard_map/ppermute | solution.py:41
  106.4 8.7 %collective-permute-done.16.a_ref = bf16[4,96,256]{2,1,0:T(8,128)(2,1)S(1)} collective-permute-done((bf16[4,96,256]{2,1,0:T(8,128)(2,1)S(1)}, bf16[4,96,256]{2,1,0:T(8,128)(2,1)S(1)}, u32[]{:S(2)}, u32[]{:S(2)}) %collective-permute-start.16) | collective-permute-done | bytes 196640 | tf_op jit(solution)/shard_map/ppermute | solution.py:41
  115.0 0.6 collective-permute-done.18.c_ref
  115.7 0.6 collective-permute-start.19
  116.4 2.0 %collective-permute-start.20 = (bf16[96,256]{1,0:T(8,128)(2,1)S(1)}, bf16[96,256]{1,0:T(8,128)(2,1)S(1)}, u32[]{:S(2)}, u32[]{:S(2)}) collective-permute-start(bf16[96,256]{1,0:T(8,128)(2,1)S(1)} %get-tuple-element.45), channel_id=1, source_target_pairs={{0,4},{1,5},{2,6},{3,7},{4,0},{5,1},{6,2},{7,3},{8,12},{9,13},{10,... | collective-permute-start | bytes 147464 | tf_op jit(solution)/shard_map/ppermute | solution.py:41
  118.4 1.2 collective-permute-start.21
  119.6 0.8 constant_dynamic-slice_fusion.residual_ref
  120.4 0.7 collective-permute-done.19.a_ref
  121.1 0.9 collective-permute-done.20.b_ref
  122.0 0.5 collective-permute-done.21.c_ref
  122.5 0.7 shard_map.122
  (45 shorter events, 1.2 us)
Async XLA Ops:
  0.1 1.1 copy-start.8
  1.2 15.5 %copy-start.14 = (s32[64,1]{0,1:T(1,128)S(1)}, s32[64,1]{0,1:T(1,128)}, u32[]{:S(2)}) copy-start(s32[64,1]{0,1:T(1,128)} %param.14) | copy-start | bytes 772
  2.0 13.3 %collective-permute-start = (bf16[4,32,1280]{2,1,0:T(8,128)(2,1)S(1)}, bf16[4,32,1280]{2,1,0:T(8,128)(2,1)S(1)}, u32[]{:S(2)}, u32[]{:S(2)}) collective-permute-start(bf16[4,32,1280]{2,1,0:T(8,128)(2,1)S(1)} %shard_map.111.own_rows), channel_id=1, source_target_pairs={{0,32},{32,64},{64,96},{96,0},{1,33},{33,65},{65,97},{97,1},{2,34}... | collective-permute-start | bytes 983048 | tf_op jit(solution)/shard_map/ppermute | solution.py:31
  2.5 19.3 %collective-permute-start.1 = (bf16[4,32,1280]{2,1,0:T(8,128)(2,1)S(1)}, bf16[4,32,1280]{2,1,0:T(8,128)(2,1)S(1)}, u32[]{:S(2)}, u32[]{:S(2)}) collective-permute-start(bf16[4,32,1280]{2,1,0:T(8,128)(2,1)S(1)} %shard_map.111.own_rows), channel_id=1, source_target_pairs={{0,64},{32,96},{64,0},{96,32},{1,65},{33,97},{65,1},{97,33},{2,66}... | collective-permute-start | bytes 983048 | tf_op jit(solution)/shard_map/ppermute | solution.py:31
  5.0 16.8 %collective-permute-start.2 = (bf16[4,32,1280]{2,1,0:T(8,128)(2,1)S(1)}, bf16[4,32,1280]{2,1,0:T(8,128)(2,1)S(1)}, u32[]{:S(2)}, u32[]{:S(2)}) collective-permute-start(bf16[4,32,1280]{2,1,0:T(8,128)(2,1)S(1)} %shard_map.111.own_rows), channel_id=1, source_target_pairs={{0,96},{32,0},{64,32},{96,64},{1,97},{33,1},{65,33},{97,65},{2,98}... | collective-permute-start | bytes 983048 | tf_op jit(solution)/shard_map/ppermute | solution.py:31
  5.0 2.2 %copy-start.1 = (bf16[8192,256]{1,0:T(8,128)(2,1)S(1)}, bf16[8192,256]{1,0:T(8,128)(2,1)}, u32[]{:S(2)}) copy-start(bf16[8192,256]{1,0:T(8,128)(2,1)} %weight_ref.3) | copy-start | bytes 12582916
  7.2 1.1 copy-start.9
  8.2 1.4 %copy-start.11 = (bf16[24,4,8192]{2,1,0:T(4,128)(2,1)S(1)}, bf16[24,4,8192]{2,1,0:T(4,128)(2,1)}, u32[]{:S(2)}) copy-start(bf16[24,4,8192]{2,1,0:T(4,128)(2,1)} %text_ref.1) | copy-start | bytes 4718596
  9.7 10.9 %copy-start.12 = (s32[32]{0:T(128)S(1)}, s32[32]{0:T(128)}, u32[]{:S(2)}) copy-start(s32[32]{0:T(128)} %param.12) | copy-start | bytes 388
  9.7 11.0 %copy-start.13 = (s32[64]{0:T(128)S(1)}, s32[64]{0:T(128)}, u32[]{:S(2)}) copy-start(s32[64]{0:T(128)} %param.13) | copy-start | bytes 772
  11.9 22.8 %collective-permute-start.6 = (bf16[5,32,1280]{2,1,0:T(8,128)(2,1)S(1)}, bf16[5,32,1280]{2,1,0:T(8,128)(2,1)S(1)}, u32[]{:S(2)}, u32[]{:S(2)}) collective-permute-start(bf16[5,32,1280]{2,1,0:T(8,128)(2,1)S(1)} %shard_map.109._.own_rows), channel_id=1, source_target_pairs={{0,32},{32,64},{64,96},{96,0},{1,33},{33,65},{65,97},{97,1},{2,34}... | collective-permute-start | bytes 1228808 | tf_op jit(solution)/shard_map/ppermute | solution.py:31
  15.2 20.8 %collective-permute-start.7 = (bf16[5,32,1280]{2,1,0:T(8,128)(2,1)S(1)}, bf16[5,32,1280]{2,1,0:T(8,128)(2,1)S(1)}, u32[]{:S(2)}, u32[]{:S(2)}) collective-permute-start(bf16[5,32,1280]{2,1,0:T(8,128)(2,1)S(1)} %shard_map.109._.own_rows), channel_id=1, source_target_pairs={{0,64},{32,96},{64,0},{96,32},{1,65},{33,97},{65,1},{97,33},{2,66}... | collective-permute-start | bytes 1228808 | tf_op jit(solution)/shard_map/ppermute | solution.py:31
  15.3 24.0 %collective-permute-start.8 = (bf16[5,32,1280]{2,1,0:T(8,128)(2,1)S(1)}, bf16[5,32,1280]{2,1,0:T(8,128)(2,1)S(1)}, u32[]{:S(2)}, u32[]{:S(2)}) collective-permute-start(bf16[5,32,1280]{2,1,0:T(8,128)(2,1)S(1)} %shard_map.109._.own_rows), channel_id=1, source_target_pairs={{0,96},{32,0},{64,32},{96,64},{1,97},{33,1},{65,33},{97,65},{2,98}... | collective-permute-start | bytes 1228808 | tf_op jit(solution)/shard_map/ppermute | solution.py:31
  16.7 1.9 %copy-start.2 = (bf16[1280,1280]{1,0:T(8,128)(2,1)S(1)}, bf16[1280,1280]{1,0:T(8,128)(2,1)}, u32[]{:S(2)}) copy-start(bf16[1280,1280]{1,0:T(8,128)(2,1)} %fc1_ref.3) | copy-start | bytes 9830404
  18.7 1.9 %copy-start.4 = (bf16[1280,1280]{1,0:T(8,128)(2,1)S(1)}, bf16[1280,1280]{1,0:T(8,128)(2,1)}, u32[]{:S(2)}) copy-start(bf16[1280,1280]{1,0:T(8,128)(2,1)} %fc2_ref.3) | copy-start | bytes 9830404
  20.6 1.9 %copy-start.3 = (bf16[1280,1280]{1,0:T(8,128)(2,1)S(1)}, bf16[1280,1280]{1,0:T(8,128)(2,1)}, u32[]{:S(2)}) copy-start(bf16[1280,1280]{1,0:T(8,128)(2,1)} %fc1_ref.3) | copy-start | bytes 9830404
  20.6 2.9 %copy-start.5 = (bf16[1280,1280]{1,0:T(8,128)(2,1)S(1)}, bf16[1280,1280]{1,0:T(8,128)(2,1)}, u32[]{:S(2)}) copy-start(bf16[1280,1280]{1,0:T(8,128)(2,1)} %fc2_ref.3) | copy-start | bytes 9830404
  20.6 3.0 %copy-start.10 = (bf16[8,32,1280]{2,1,0:T(8,128)(2,1)S(1)}, bf16[8,32,1280]{2,1,0:T(8,128)(2,1)}, u32[]{:S(2)}) copy-start(bf16[8,32,1280]{2,1,0:T(8,128)(2,1)} %patches_ref.7) | copy-start | bytes 1966084
  27.9 18.3 %collective-permute-start.3 = (bf16[4,32,1280]{2,1,0:T(8,128)(2,1)S(1)}, bf16[4,32,1280]{2,1,0:T(8,128)(2,1)S(1)}, u32[]{:S(2)}, u32[]{:S(2)}) collective-permute-start(bf16[4,32,1280]{2,1,0:T(8,128)(2,1)S(1)} %get-tuple-element.27), channel_id=1, source_target_pairs={{0,32},{32,64},{64,96},{96,0},{1,33},{33,65},{65,97},{97,1},{2,34}... | collective-permute-start | bytes 983048 | tf_op jit(solution)/shard_map/ppermute | solution.py:31
  29.8 36.5 %collective-permute-start.4 = (bf16[4,32,1280]{2,1,0:T(8,128)(2,1)S(1)}, bf16[4,32,1280]{2,1,0:T(8,128)(2,1)S(1)}, u32[]{:S(2)}, u32[]{:S(2)}) collective-permute-start(bf16[4,32,1280]{2,1,0:T(8,128)(2,1)S(1)} %get-tuple-element.28), channel_id=1, source_target_pairs={{0,64},{32,96},{64,0},{96,32},{1,65},{33,97},{65,1},{97,33},{2,66}... | collective-permute-start | bytes 983048 | tf_op jit(solution)/shard_map/ppermute | solution.py:31
  34.7 31.7 %copy-start.6 = (bf16[1280,1024]{1,0:T(8,128)(2,1)S(1)}, bf16[1280,1024]{1,0:T(8,128)(2,1)}, u32[]{:S(2)}) copy-start(bf16[1280,1024]{1,0:T(8,128)(2,1)} %refs_8_.1) | copy-start | bytes 7864324
  34.7 31.7 %copy-start.7 = (bf16[1280,1024]{1,0:T(8,128)(2,1)S(1)}, bf16[1280,1024]{1,0:T(8,128)(2,1)}, u32[]{:S(2)}) copy-start(bf16[1280,1024]{1,0:T(8,128)(2,1)} %refs_9_.1) | copy-start | bytes 7864324
  34.7 31.7 %collective-permute-start.5 = (bf16[4,32,1280]{2,1,0:T(8,128)(2,1)S(1)}, bf16[4,32,1280]{2,1,0:T(8,128)(2,1)S(1)}, u32[]{:S(2)}, u32[]{:S(2)}) collective-permute-start(bf16[4,32,1280]{2,1,0:T(8,128)(2,1)S(1)} %get-tuple-element.29), channel_id=1, source_target_pairs={{0,96},{32,0},{64,32},{96,64},{1,97},{33,1},{65,33},{97,65},{2,98}... | collective-permute-start | bytes 983048 | tf_op jit(solution)/shard_map/ppermute | solution.py:31
  43.6 22.8 %collective-permute-start.10 = (bf16[4,32,1280]{2,1,0:T(8,128)(2,1)S(1)}, bf16[4,32,1280]{2,1,0:T(8,128)(2,1)S(1)}, u32[]{:S(2)}, u32[]{:S(2)}) collective-permute-start(bf16[4,32,1280]{2,1,0:T(8,128)(2,1)S(1)} %get-tuple-element.32), channel_id=1, source_target_pairs={{0,64},{32,96},{64,0},{96,32},{1,65},{33,97},{65,1},{97,33},{2,66}... | collective-permute-start | bytes 983048 | tf_op jit(solution)/shard_map/ppermute | solution.py:31
  46.2 20.2 %collective-permute-start.11 = (bf16[4,32,1280]{2,1,0:T(8,128)(2,1)S(1)}, bf16[4,32,1280]{2,1,0:T(8,128)(2,1)S(1)}, u32[]{:S(2)}, u32[]{:S(2)}) collective-permute-start(bf16[4,32,1280]{2,1,0:T(8,128)(2,1)S(1)} %get-tuple-element.33), channel_id=1, source_target_pairs={{0,96},{32,0},{64,32},{96,64},{1,97},{33,1},{65,33},{97,65},{2,98}... | collective-permute-start | bytes 983048 | tf_op jit(solution)/shard_map/ppermute | solution.py:31
  46.2 20.2 %collective-permute-start.9 = (bf16[4,32,1280]{2,1,0:T(8,128)(2,1)S(1)}, bf16[4,32,1280]{2,1,0:T(8,128)(2,1)S(1)}, u32[]{:S(2)}, u32[]{:S(2)}) collective-permute-start(bf16[4,32,1280]{2,1,0:T(8,128)(2,1)S(1)} %get-tuple-element.31), channel_id=1, source_target_pairs={{0,32},{32,64},{64,96},{96,0},{1,33},{33,65},{65,97},{97,1},{2,34}... | collective-permute-start | bytes 983048 | tf_op jit(solution)/shard_map/ppermute | solution.py:31
  66.4 32.5 %copy-start = (bf16[256,8192]{1,0:T(8,128)(2,1)S(1)}, bf16[256,8192]{1,0:T(8,128)(2,1)}, u32[]{:S(2)}) copy-start(bf16[256,8192]{1,0:T(8,128)(2,1)} %weight_ref.5) | copy-start | bytes 12582916
  90.4 4.6 %collective-permute-start.12 = (bf16[208,128]{1,0:T(8,128)(2,1)S(1)}, bf16[208,128]{1,0:T(8,128)(2,1)S(1)}, u32[]{:S(2)}, u32[]{:S(2)}) collective-permute-start(bf16[208,128]{1,0:T(8,128)(2,1)S(1)} %get-tuple-element.36), channel_id=1, source_target_pairs={{0,32},{32,64},{64,96},{96,0},{1,33},{33,65},{65,97},{97,1},{2,34}... | collective-permute-start | bytes 159752 | tf_op jit(solution)/shard_map/ppermute | solution.py:31
  91.5 5.9 %collective-permute-start.13 = (bf16[208,128]{1,0:T(8,128)(2,1)S(1)}, bf16[208,128]{1,0:T(8,128)(2,1)S(1)}, u32[]{:S(2)}, u32[]{:S(2)}) collective-permute-start(bf16[208,128]{1,0:T(8,128)(2,1)S(1)} %get-tuple-element.37), channel_id=1, source_target_pairs={{0,64},{32,96},{64,0},{96,32},{1,65},{33,97},{65,1},{97,33},{2,66}... | collective-permute-start | bytes 159752 | tf_op jit(solution)/shard_map/ppermute | solution.py:31
  93.6 5.3 %collective-permute-start.14 = (bf16[208,128]{1,0:T(8,128)(2,1)S(1)}, bf16[208,128]{1,0:T(8,128)(2,1)S(1)}, u32[]{:S(2)}, u32[]{:S(2)}) collective-permute-start(bf16[208,128]{1,0:T(8,128)(2,1)S(1)} %get-tuple-element.38), channel_id=1, source_target_pairs={{0,96},{32,0},{64,32},{96,64},{1,97},{33,1},{65,33},{97,65},{2,98}... | collective-permute-start | bytes 159752 | tf_op jit(solution)/shard_map/ppermute | solution.py:31
  100.1 2.4 %collective-permute-start.15 = (bf16[4,4,96,256]{3,2,1,0:T(8,128)(2,1)S(1)}, bf16[4,4,96,256]{3,2,1,0:T(8,128)(2,1)S(1)}, u32[]{:S(2)}, u32[]{:S(2)}) collective-permute-start(bf16[4,4,96,256]{3,2,1,0:T(8,128)(2,1)S(1)} %shard_map.119), channel_id=1, source_target_pairs={{0,1},{1,0},{2,3},{3,2},{4,5},{5,4},{6,7},{7,6},{8,9},{9,8},{10,11... | collective-permute-start | bytes 2359304 | tf_op jit(solution)/shard_map/ppermute | solution.py:41
  102.6 12.4 %collective-permute-start.16 = (bf16[4,96,256]{2,1,0:T(8,128)(2,1)S(1)}, bf16[4,96,256]{2,1,0:T(8,128)(2,1)S(1)}, u32[]{:S(2)}, u32[]{:S(2)}) collective-permute-start(bf16[4,96,256]{2,1,0:T(8,128)(2,1)S(1)} %get-tuple-element.40), channel_id=1, source_target_pairs={{0,8},{1,9},{2,10},{3,11},{4,12},{5,13},{6,14},{7,15},{8,16},{9,17... | collective-permute-start | bytes 589832 | tf_op jit(solution)/shard_map/ppermute | solution.py:41
  103.0 12.0 %collective-permute-start.17 = (bf16[4,96,256]{2,1,0:T(8,128)(2,1)S(1)}, bf16[4,96,256]{2,1,0:T(8,128)(2,1)S(1)}, u32[]{:S(2)}, u32[]{:S(2)}) collective-permute-start(bf16[4,96,256]{2,1,0:T(8,128)(2,1)S(1)} %get-tuple-element.41), channel_id=1, source_target_pairs={{0,16},{1,17},{2,18},{3,19},{4,20},{5,21},{6,22},{7,23},{8,24},{9,... | collective-permute-start | bytes 589832 | tf_op jit(solution)/shard_map/ppermute | solution.py:41
  105.1 10.6 %collective-permute-start.18 = (bf16[4,96,256]{2,1,0:T(8,128)(2,1)S(1)}, bf16[4,96,256]{2,1,0:T(8,128)(2,1)S(1)}, u32[]{:S(2)}, u32[]{:S(2)}) collective-permute-start(bf16[4,96,256]{2,1,0:T(8,128)(2,1)S(1)} %get-tuple-element.42), channel_id=1, source_target_pairs={{0,24},{1,25},{2,26},{3,27},{4,28},{5,29},{6,30},{7,31},{8,0},{9,1... | collective-permute-start | bytes 589832 | tf_op jit(solution)/shard_map/ppermute | solution.py:41
  115.7 5.4 %collective-permute-start.19 = (bf16[96,256]{1,0:T(8,128)(2,1)S(1)}, bf16[96,256]{1,0:T(8,128)(2,1)S(1)}, u32[]{:S(2)}, u32[]{:S(2)}) collective-permute-start(bf16[96,256]{1,0:T(8,128)(2,1)S(1)} %get-tuple-element.44), channel_id=1, source_target_pairs={{0,2},{1,3},{2,4},{3,5},{4,6},{5,7},{6,0},{7,1},{8,10},{9,11},{10,... | collective-permute-start | bytes 147464 | tf_op jit(solution)/shard_map/ppermute | solution.py:41
  116.4 5.6 %collective-permute-start.20 = (bf16[96,256]{1,0:T(8,128)(2,1)S(1)}, bf16[96,256]{1,0:T(8,128)(2,1)S(1)}, u32[]{:S(2)}, u32[]{:S(2)}) collective-permute-start(bf16[96,256]{1,0:T(8,128)(2,1)S(1)} %get-tuple-element.45), channel_id=1, source_target_pairs={{0,4},{1,5},{2,6},{3,7},{4,0},{5,1},{6,2},{7,3},{8,12},{9,13},{10,... | collective-permute-start | bytes 147464 | tf_op jit(solution)/shard_map/ppermute | solution.py:41
  118.4 4.1 %collective-permute-start.21 = (bf16[96,256]{1,0:T(8,128)(2,1)S(1)}, bf16[96,256]{1,0:T(8,128)(2,1)S(1)}, u32[]{:S(2)}, u32[]{:S(2)}) collective-permute-start(bf16[96,256]{1,0:T(8,128)(2,1)S(1)} %get-tuple-element.46), channel_id=1, source_target_pairs={{0,6},{1,7},{2,0},{3,1},{4,2},{5,3},{6,4},{7,5},{8,14},{9,15},{10,... | collective-permute-start | bytes 147464 | tf_op jit(solution)/shard_map/ppermute | solution.py:41

commit v5 on v4

--- a/solution.py
+++ b/solution.py
@@ -131,6 +131,20 @@
     )(at, patches, *sources, fc1, fc2, *after)
 
 
+def pair_sum_kernel(a_ref, b_ref, out_ref):
+    out_ref[...] = (a_ref[...].astype(F32) + b_ref[...].astype(F32)).astype(BF16)
+
+
+def pair_sum(a, b):
+    return pl.pallas_call(
+        pair_sum_kernel,
+        out_shape=jax.ShapeDtypeStruct(a.shape, BF16),
+        in_specs=[VMEM, VMEM],
+        out_specs=VMEM,
+        compiler_params=params(8),
+    )(a, b)
+
+
 def query_kernel(at_ref, text_ref, weight_ref, patches_ref, sent_ref, total_ref, square_ref):
     step = pl.program_id(0)
     rows, columns = total_ref.shape
@@ -278,7 +292,7 @@
 
 
 def attend_kernel(*refs):
-    count = 2 * RING
+    count = 2 * RING - 1
     sums, (key_hbm, value_hbm, query_hbm) = refs[:count], refs[count : count + 3]
     out_ref, sums_ref, rows_ref, key_ref, value_ref, query_ref, sum_sems, weight_sems = refs[count + 3 :]
     _, ring, quarter, width = sums_ref.shape
@@ -303,11 +317,11 @@
         for copy in more:
             copy.start()
     rows = ring * quarter
-    for half in range(2):
-        for i in range(half * RING, (half + 1) * RING):
+    for half, (first, last) in enumerate(((0, RING - 1), (RING - 1, count))):
+        for i in range(first, last):
             copies[i].wait()
-        summed = sums_ref[half * RING].astype(F32)
-        for i in range(half * RING + 1, (half + 1) * RING):
+        summed = sums_ref[first].astype(F32)
+        for i in range(first + 1, last):
             summed = summed + sums_ref[i].astype(F32)
         rows_ref[half * rows : (half + 1) * rows] = summed.astype(BF16).reshape(rows, width)
     copies[count].wait()
@@ -544,7 +558,11 @@
             at, patches, sources[i], fc1_weight, fc2_weight, i, (held, target)
         )
         queries = messages[-1]
-        sums += [total] + [pool_shift(messages[s - 1], s) for s in range(1, RING)]
+        if i == 0:
+            near = pair_sum(messages[0], pool_shift(messages[1], 1))
+            sums += [total, pool_shift(messages[2], -1), pool_shift(near, 1)]
+        else:
+            sums += [total] + [pool_shift(messages[s - 1], s) for s in range(1, RING)]
     chosen = select(at, target, queries, local_heads * slots * steps)
     per_device = halves * local_heads * steps
     tile_queries = lax.all_to_all(

time: 124 us -> 123 us (level)
  waiting for transfers between devices: 21.2 us -> 25.6 us
  starting transfers between devices: 32.7 us -> 29.4 us
    ppermute x15, waiting for transfers between devices: 8.63 us -> 13.1 us  [pool_shift(): return lax.ppermute(x, 'pool', [(i, (i + by) % RING) for i in range(RING)])]
    ppermute x15, starting transfers between devices: 24.9 us -> 21.7 us  [pool_shift(): return lax.ppermute(x, 'pool', [(i, (i + by) % RING) for i in range(RING)])]
    all_to_all x1, blocking collectives: 16.5 us -> 15.3 us  [body(): lax.all_to_all(packed.reshape(devices, per_device, 2 * HEAD_DIM), 'dev',...]
  transfers between devices with their start and end apart: 22 -> 22, of which waited for: 10 -> 11; matrix products, arithmetic and copies ran while one was open for 1% -> 1% of each run, Pallas kernels for 11% -> 11%
where the time goes in v5:
time: 123 us
  blocking collectives  31.2 us (25%)
  starting transfers between devices  29.4 us (24%)
  waiting for transfers between devices  25.6 us (21%)
  Pallas kernels  24.2 us (20%)
  local copies, waits for them, and re-layouts  12.3 us (10%)
    ppermute x15, starting transfers between devices, pool_shift(): return lax.ppermute(x, 'pool', [(i, (i + by) % RING) for i in range(RING)])  21.7 us
    all_to_all x1, blocking collectives, body(): lax.all_to_all(chosen.reshape(devices, per_device, HEAD_DIM), 'dev', spli...  15.9 us
    all_to_all x1, blocking collectives, body(): lax.all_to_all(packed.reshape(devices, per_device, 2 * HEAD_DIM), 'dev',...  15.3 us
    ppermute x15, waiting for transfers between devices, pool_shift(): return lax.ppermute(x, 'pool', [(i, (i + by) % RING) for i in range(RING)])  13.1 us
    ppermute x7, waiting for transfers between devices, dev_shift(): return lax.ppermute(x, 'dev', pairs)  12.5 us
    unnamed x31, local copies, waits for them, and re-layouts  11.5 us
    pallas_call x2, Pallas kernels, feed_forward(): pl.pallas_call(functools.partial(feed_forward_kernel, half), out_shape=(s...  8.55 us
    ppermute x7, starting transfers between devices, dev_shift(): return lax.ppermute(x, 'dev', pairs)  7.72 us
  transfers between devices with their start and end apart: 22, of which 11 were waited for; matrix products, arithmetic and copies ran while one was open for 1% of the time, Pallas kernels for 11%

profile of v5, /device:TPU:6, one launch (start us, length us, event | category | flops | bytes accessed | tf_op | source)
XLA Modules:
  0.0 123.0 jit_solution(3512473906456476067)
XLA Ops:
  0.1 1.1 copy-done.8
  1.2 0.8 shard_map.111.own_rows
  2.0 0.5 collective-permute-start
  2.5 2.5 %collective-permute-start.1 = (bf16[4,32,1280]{2,1,0:T(8,128)(2,1)S(1)}, bf16[4,32,1280]{2,1,0:T(8,128)(2,1)S(1)}, u32[]{:S(2)}, u32[]{:S(2)}) collective-permute-start(bf16[4,32,1280]{2,1,0:T(8,128)(2,1)S(1)} %shard_map.111.own_rows), channel_id=1, source_target_pairs={{0,64},{32,96},{64,0},{96,32},{1,65},{33,97},{65,1},{97,33},{2,66}... | collective-permute-start | bytes 983048 | tf_op jit(solution)/shard_map/ppermute | solution.py:31
  5.0 2.2 %copy-done.1 = bf16[8192,256]{1,0:T(8,128)(2,1)S(1)} copy-done((bf16[8192,256]{1,0:T(8,128)(2,1)S(1)}, bf16[8192,256]{1,0:T(8,128)(2,1)}, u32[]{:S(2)}) %copy-start.1) | copy-done | bytes 4194328
  7.2 1.1 copy-done.9
  8.2 1.4 %copy-done.11 = bf16[24,4,8192]{2,1,0:T(4,128)(2,1)S(1)} copy-done((bf16[24,4,8192]{2,1,0:T(4,128)(2,1)S(1)}, bf16[24,4,8192]{2,1,0:T(4,128)(2,1)}, u32[]{:S(2)}) %copy-start.11) | copy-done | bytes 1572888
  9.7 2.2 %shard_map.109._.own_rows = bf16[5,32,1280]{2,1,0:T(8,128)(2,1)S(1)} custom-call(s32[2]{0:T(128)S(1)} %pad_add_fusion.at_ref, bf16[24,4,8192]{2,1,0:T(4,128)(2,1)S(1)} %copy-done.11, bf16[8192,256]{1,0:T(8,128)(2,1)S(1)} %copy-done.1, bf16[8,32,1280]{2,1,0:T(8,128)(2,1)S(1)} %copy-done.9), custom_call_target="tpu_custom_call" | custom-call | flops 402653184 | bytes 5767168 | tf_op jit(solution)/shard_map/pallas_call | solution.py:188
  11.9 3.3 %collective-permute-start.6 = (bf16[5,32,1280]{2,1,0:T(8,128)(2,1)S(1)}, bf16[5,32,1280]{2,1,0:T(8,128)(2,1)S(1)}, u32[]{:S(2)}, u32[]{:S(2)}) collective-permute-start(bf16[5,32,1280]{2,1,0:T(8,128)(2,1)S(1)} %shard_map.109._.own_rows), channel_id=1, source_target_pairs={{0,32},{32,64},{64,96},{96,0},{1,33},{33,65},{65,97},{97,1},{2,34}... | collective-permute-start | bytes 1228808 | tf_op jit(solution)/shard_map/ppermute | solution.py:31
  15.3 1.3 %collective-permute-start.8 = (bf16[5,32,1280]{2,1,0:T(8,128)(2,1)S(1)}, bf16[5,32,1280]{2,1,0:T(8,128)(2,1)S(1)}, u32[]{:S(2)}, u32[]{:S(2)}) collective-permute-start(bf16[5,32,1280]{2,1,0:T(8,128)(2,1)S(1)} %shard_map.109._.own_rows), channel_id=1, source_target_pairs={{0,96},{32,0},{64,32},{96,64},{1,97},{33,1},{65,33},{97,65},{2,98}... | collective-permute-start | bytes 1228808 | tf_op jit(solution)/shard_map/ppermute | solution.py:31
  16.7 1.9 %copy-done.2 = bf16[1280,1280]{1,0:T(8,128)(2,1)S(1)} copy-done((bf16[1280,1280]{1,0:T(8,128)(2,1)S(1)}, bf16[1280,1280]{1,0:T(8,128)(2,1)}, u32[]{:S(2)}) %copy-start.2) | copy-done | bytes 3276824
  18.7 1.9 %copy-done.4 = bf16[1280,1280]{1,0:T(8,128)(2,1)S(1)} copy-done((bf16[1280,1280]{1,0:T(8,128)(2,1)S(1)}, bf16[1280,1280]{1,0:T(8,128)(2,1)}, u32[]{:S(2)}) %copy-start.4) | copy-done | bytes 3276824
  20.6 1.2 shard_map.110.refs_1_.target_ref
  21.8 0.7 copy-done.3
  22.5 1.0 copy-done.5
  23.6 4.3 %shard_map.113 = (bf16[4,32,1280]{2,1,0:T(8,128)(2,1)S(1)}, bf16[4,32,1280]{2,1,0:T(8,128)(2,1)S(1)}, bf16[4,32,1280]{2,1,0:T(8,128)(2,1)S(1)}, bf16[4,32,1280]{2,1,0:T(8,128)(2,1)S(1)}) custom-call(s32[2]{0:T(128)S(1)} %pad_add_fusion.at_ref, bf16[8,32,1280]{2,1,0:T(8,128)(2,1)S(1)} %copy-done.10, bf16[4,32,1280]{2,1,0:T(8,128)(2,1)S(1)} %shard_map.111.own_rows, ...), custom_call_target="tpu_custom_call" | custom-call | flops 3355443200 | bytes 6553600 | tf_op jit(solution)/shard_map/pallas_call | solution.py:116
  27.9 2.0 %collective-permute-start.4 = (bf16[4,32,1280]{2,1,0:T(8,128)(2,1)S(1)}, bf16[4,32,1280]{2,1,0:T(8,128)(2,1)S(1)}, u32[]{:S(2)}, u32[]{:S(2)}) collective-permute-start(bf16[4,32,1280]{2,1,0:T(8,128)(2,1)S(1)} %get-tuple-element.29), channel_id=1, source_target_pairs={{0,32},{32,64},{64,96},{96,0},{1,33},{33,65},{65,97},{97,1},{2,34}... | collective-permute-start | bytes 983048 | tf_op jit(solution)/shard_map/ppermute | solution.py:31
  30.5 7.3 %collective-permute-done.8.three_rows = bf16[5,32,1280]{2,1,0:T(8,128)(2,1)S(1)} collective-permute-done((bf16[5,32,1280]{2,1,0:T(8,128)(2,1)S(1)}, bf16[5,32,1280]{2,1,0:T(8,128)(2,1)S(1)}, u32[]{:S(2)}, u32[]{:S(2)}) %collective-permute-start.8) | collective-permute-done | bytes 409632 | tf_op jit(solution)/shard_map/ppermute | solution.py:31
  37.8 4.3 %shard_map.115 = (bf16[4,32,1280]{2,1,0:T(8,128)(2,1)S(1)}, bf16[4,32,1280]{2,1,0:T(8,128)(2,1)S(1)}, bf16[4,32,1280]{2,1,0:T(8,128)(2,1)S(1)}, bf16[4,32,1280]{2,1,0:T(8,128)(2,1)S(1)}, bf16[4,32,1280]{2,1,0:T(8,128)(2,1)S(1)}) custom-call(s32[2]{0:T(128)S(1)} %pad_add_fusion.at_ref, bf16[8,32,1280]{2,1,0:T(8,128)(2,1)S(1)} %copy-done.10, ...), custom_call_target="tpu_custom_call" | custom-call | flops 3355443200 | bytes 6553600 | tf_op jit(solution)/shard_map/pallas_call | solution.py:116
  42.1 2.7 %collective-permute-start.10 = (bf16[4,32,1280]{2,1,0:T(8,128)(2,1)S(1)}, bf16[4,32,1280]{2,1,0:T(8,128)(2,1)S(1)}, u32[]{:S(2)}, u32[]{:S(2)}) collective-permute-start(bf16[4,32,1280]{2,1,0:T(8,128)(2,1)S(1)} %get-tuple-element.32), channel_id=1, source_target_pairs={{0,64},{32,96},{64,0},{96,32},{1,65},{33,97},{65,1},{97,33},{2,66}... | collective-permute-start | bytes 983048 | tf_op jit(solution)/shard_map/ppermute | solution.py:31
  44.8 0.5 collective-permute-start.11
  45.2 2.8 %collective-permute-start.9 = (bf16[4,32,1280]{2,1,0:T(8,128)(2,1)S(1)}, bf16[4,32,1280]{2,1,0:T(8,128)(2,1)S(1)}, u32[]{:S(2)}, u32[]{:S(2)}) collective-permute-start(bf16[4,32,1280]{2,1,0:T(8,128)(2,1)S(1)} %get-tuple-element.31), channel_id=1, source_target_pairs={{0,32},{32,64},{64,96},{96,0},{1,33},{33,65},{65,97},{97,1},{2,34}... | collective-permute-start | bytes 983048 | tf_op jit(solution)/shard_map/ppermute | solution.py:31
  48.1 1.4 %collective-permute-start.5 = (bf16[4,32,1280]{2,1,0:T(8,128)(2,1)S(1)}, bf16[4,32,1280]{2,1,0:T(8,128)(2,1)S(1)}, u32[]{:S(2)}, u32[]{:S(2)}) collective-permute-start(bf16[4,32,1280]{2,1,0:T(8,128)(2,1)S(1)} %shard_map.114), channel_id=1, source_target_pairs={{0,32},{32,64},{64,96},{96,0},{1,33},{33,65},{65,97},{97,1},{2,34}... | collective-permute-start | bytes 983048 | tf_op jit(solution)/shard_map/ppermute | solution.py:31
  49.5 1.0 shard_map.116
  50.5 15.9 %all_to_all.10 = bf16[32,16,128]{2,1,0:T(8,128)(2,1)S(1)} all-to-all(bf16[32,16,128]{2,1,0:T(8,128)(2,1)S(1)} %bitcast.11), channel_id=1, replica_groups=mesh['pool'=4,'dev'=32] {'dev'}, dimensions={0} | all-to-all | bytes 262144 | tf_op jit(solution)/shard_map/all_to_all | solution.py:568
  66.5 6.1 %shard_map.117 = bf16[8,4,16,256]{3,2,1,0:T(8,128)(2,1)S(1)} custom-call(bf16[4,32,1280]{2,1,0:T(8,128)(2,1)S(1)} %get-tuple-element.26.refs_0_, bf16[4,32,1280]{2,1,0:T(8,128)(2,1)S(1)} %collective-permute-done.3.refs_1_, bf16[4,32,1280]{2,1,0:T(8,128)(2,1)S(1)} %collective-permute-done.5.refs_2_, bf16[4,32,1280]{2,1,0:T(8,128)(2,1)S(1)} %get-tuple-element.30.refs_3_, ...), custom_call_target="tpu_custom_call" | custom-call | flops 1342177280 | bytes 5242880 | tf_op jit(solution)/shard_map/pallas_call | solution.py:367
  72.5 15.3 %all_to_all.11 = bf16[32,16,256]{2,1,0:T(8,128)(2,1)S(1)} all-to-all(bf16[32,16,256]{2,1,0:T(8,128)(2,1)S(1)} %bitcast.8), channel_id=1, replica_groups=mesh['pool'=4,'dev'=32] {'dev'}, dimensions={0} | all-to-all | bytes 524288 | tf_op jit(solution)/shard_map/all_to_all | solution.py:572
  87.8 1.2 shard_map.118
  89.0 2.7 %collective-permute-start.12 = (bf16[208,128]{1,0:T(8,128)(2,1)S(1)}, bf16[208,128]{1,0:T(8,128)(2,1)S(1)}, u32[]{:S(2)}, u32[]{:S(2)}) collective-permute-start(bf16[208,128]{1,0:T(8,128)(2,1)S(1)} %get-tuple-element.36), channel_id=1, source_target_pairs={{0,32},{32,64},{64,96},{96,0},{1,33},{33,65},{65,97},{97,1},{2,34}... | collective-permute-start | bytes 159752 | tf_op jit(solution)/shard_map/ppermute | solution.py:31
  91.7 1.7 %collective-permute-start.13 = (bf16[208,128]{1,0:T(8,128)(2,1)S(1)}, bf16[208,128]{1,0:T(8,128)(2,1)S(1)}, u32[]{:S(2)}, u32[]{:S(2)}) collective-permute-start(bf16[208,128]{1,0:T(8,128)(2,1)S(1)} %get-tuple-element.37), channel_id=1, source_target_pairs={{0,64},{32,96},{64,0},{96,32},{1,65},{33,97},{65,1},{97,33},{2,66}... | collective-permute-start | bytes 159752 | tf_op jit(solution)/shard_map/ppermute | solution.py:31
  93.5 0.5 collective-permute-done.12.one_ref
  94.0 3.7 %collective-permute-done.13.two_ref = bf16[208,128]{1,0:T(8,128)(2,1)S(1)} collective-permute-done((bf16[208,128]{1,0:T(8,128)(2,1)S(1)}, bf16[208,128]{1,0:T(8,128)(2,1)S(1)}, u32[]{:S(2)}, u32[]{:S(2)}) %collective-permute-start.13) | collective-permute-done | bytes 53280 | tf_op jit(solution)/shard_map/ppermute | solution.py:31
  97.6 1.2 collective-permute-done.14.three_ref
  98.8 1.1 shard_map.120
  100.0 1.1 shard_map.119.kept_ref
  101.1 1.2 collective-permute-done.15.got_ref
  102.9 2.1 %collective-permute-start.17 = (bf16[4,96,256]{2,1,0:T(8,128)(2,1)S(1)}, bf16[4,96,256]{2,1,0:T(8,128)(2,1)S(1)}, u32[]{:S(2)}, u32[]{:S(2)}) collective-permute-start(bf16[4,96,256]{2,1,0:T(8,128)(2,1)S(1)} %get-tuple-element.41), channel_id=1, source_target_pairs={{0,16},{1,17},{2,18},{3,19},{4,20},{5,21},{6,22},{7,23},{8,24},{9,... | collective-permute-start | bytes 589832 | tf_op jit(solution)/shard_map/ppermute | solution.py:41
  104.9 1.3 %collective-permute-start.18 = (bf16[4,96,256]{2,1,0:T(8,128)(2,1)S(1)}, bf16[4,96,256]{2,1,0:T(8,128)(2,1)S(1)}, u32[]{:S(2)}, u32[]{:S(2)}) collective-permute-start(bf16[4,96,256]{2,1,0:T(8,128)(2,1)S(1)} %get-tuple-element.42), channel_id=1, source_target_pairs={{0,24},{1,25},{2,26},{3,27},{4,28},{5,29},{6,30},{7,31},{8,0},{9,1... | collective-permute-start | bytes 589832 | tf_op jit(solution)/shard_map/ppermute | solution.py:41
  106.2 8.7 %collective-permute-done.16.a_ref = bf16[4,96,256]{2,1,0:T(8,128)(2,1)S(1)} collective-permute-done((bf16[4,96,256]{2,1,0:T(8,128)(2,1)S(1)}, bf16[4,96,256]{2,1,0:T(8,128)(2,1)S(1)}, u32[]{:S(2)}, u32[]{:S(2)}) %collective-permute-start.16) | collective-permute-done | bytes 196640 | tf_op jit(solution)/shard_map/ppermute | solution.py:41
  114.9 0.6 collective-permute-done.18.c_ref
  115.6 0.6 collective-permute-start.19
  116.2 2.0 %collective-permute-start.20 = (bf16[96,256]{1,0:T(8,128)(2,1)S(1)}, bf16[96,256]{1,0:T(8,128)(2,1)S(1)}, u32[]{:S(2)}, u32[]{:S(2)}) collective-permute-start(bf16[96,256]{1,0:T(8,128)(2,1)S(1)} %get-tuple-element.45), channel_id=1, source_target_pairs={{0,4},{1,5},{2,6},{3,7},{4,0},{5,1},{6,2},{7,3},{8,12},{9,13},{10,... | collective-permute-start | bytes 147464 | tf_op jit(solution)/shard_map/ppermute | solution.py:41
  118.2 1.2 collective-permute-start.21
  119.4 0.8 constant_dynamic-slice_fusion.residual_ref
  120.3 0.7 collective-permute-done.19.a_ref
  121.0 0.9 collective-permute-done.20.b_ref
  121.8 0.5 collective-permute-done.21.c_ref
  122.3 0.7 shard_map.123
  (46 shorter events, 1.9 us)
Async XLA Ops:
  0.1 1.1 copy-start.8
  1.2 15.5 %copy-start.14 = (s32[64,1]{0,1:T(1,128)S(1)}, s32[64,1]{0,1:T(1,128)}, u32[]{:S(2)}) copy-start(s32[64,1]{0,1:T(1,128)} %param.14) | copy-start | bytes 772
  2.0 13.3 %collective-permute-start = (bf16[4,32,1280]{2,1,0:T(8,128)(2,1)S(1)}, bf16[4,32,1280]{2,1,0:T(8,128)(2,1)S(1)}, u32[]{:S(2)}, u32[]{:S(2)}) collective-permute-start(bf16[4,32,1280]{2,1,0:T(8,128)(2,1)S(1)} %shard_map.111.own_rows), channel_id=1, source_target_pairs={{0,32},{32,64},{64,96},{96,0},{1,33},{33,65},{65,97},{97,1},{2,34}... | collective-permute-start | bytes 983048 | tf_op jit(solution)/shard_map/ppermute | solution.py:31
  2.5 19.3 %collective-permute-start.1 = (bf16[4,32,1280]{2,1,0:T(8,128)(2,1)S(1)}, bf16[4,32,1280]{2,1,0:T(8,128)(2,1)S(1)}, u32[]{:S(2)}, u32[]{:S(2)}) collective-permute-start(bf16[4,32,1280]{2,1,0:T(8,128)(2,1)S(1)} %shard_map.111.own_rows), channel_id=1, source_target_pairs={{0,64},{32,96},{64,0},{96,32},{1,65},{33,97},{65,1},{97,33},{2,66}... | collective-permute-start | bytes 983048 | tf_op jit(solution)/shard_map/ppermute | solution.py:31
  5.0 16.8 %collective-permute-start.2 = (bf16[4,32,1280]{2,1,0:T(8,128)(2,1)S(1)}, bf16[4,32,1280]{2,1,0:T(8,128)(2,1)S(1)}, u32[]{:S(2)}, u32[]{:S(2)}) collective-permute-start(bf16[4,32,1280]{2,1,0:T(8,128)(2,1)S(1)} %shard_map.111.own_rows), channel_id=1, source_target_pairs={{0,96},{32,0},{64,32},{96,64},{1,97},{33,1},{65,33},{97,65},{2,98}... | collective-permute-start | bytes 983048 | tf_op jit(solution)/shard_map/ppermute | solution.py:31
  5.0 2.2 %copy-start.1 = (bf16[8192,256]{1,0:T(8,128)(2,1)S(1)}, bf16[8192,256]{1,0:T(8,128)(2,1)}, u32[]{:S(2)}) copy-start(bf16[8192,256]{1,0:T(8,128)(2,1)} %weight_ref.3) | copy-start | bytes 12582916
  7.2 1.1 copy-start.9
  8.2 1.4 %copy-start.11 = (bf16[24,4,8192]{2,1,0:T(4,128)(2,1)S(1)}, bf16[24,4,8192]{2,1,0:T(4,128)(2,1)}, u32[]{:S(2)}) copy-start(bf16[24,4,8192]{2,1,0:T(4,128)(2,1)} %text_ref.1) | copy-start | bytes 4718596
  9.7 10.9 %copy-start.12 = (s32[32]{0:T(128)S(1)}, s32[32]{0:T(128)}, u32[]{:S(2)}) copy-start(s32[32]{0:T(128)} %param.12) | copy-start | bytes 388
  9.7 11.0 %copy-start.13 = (s32[64]{0:T(128)S(1)}, s32[64]{0:T(128)}, u32[]{:S(2)}) copy-start(s32[64]{0:T(128)} %param.13) | copy-start | bytes 772
  11.9 18.2 %collective-permute-start.6 = (bf16[5,32,1280]{2,1,0:T(8,128)(2,1)S(1)}, bf16[5,32,1280]{2,1,0:T(8,128)(2,1)S(1)}, u32[]{:S(2)}, u32[]{:S(2)}) collective-permute-start(bf16[5,32,1280]{2,1,0:T(8,128)(2,1)S(1)} %shard_map.109._.own_rows), channel_id=1, source_target_pairs={{0,32},{32,64},{64,96},{96,0},{1,33},{33,65},{65,97},{97,1},{2,34}... | collective-permute-start | bytes 1228808 | tf_op jit(solution)/shard_map/ppermute | solution.py:31
  15.2 15.3 %collective-permute-start.7 = (bf16[5,32,1280]{2,1,0:T(8,128)(2,1)S(1)}, bf16[5,32,1280]{2,1,0:T(8,128)(2,1)S(1)}, u32[]{:S(2)}, u32[]{:S(2)}) collective-permute-start(bf16[5,32,1280]{2,1,0:T(8,128)(2,1)S(1)} %shard_map.109._.own_rows), channel_id=1, source_target_pairs={{0,64},{32,96},{64,0},{96,32},{1,65},{33,97},{65,1},{97,33},{2,66}... | collective-permute-start | bytes 1228808 | tf_op jit(solution)/shard_map/ppermute | solution.py:31
  15.3 22.5 %collective-permute-start.8 = (bf16[5,32,1280]{2,1,0:T(8,128)(2,1)S(1)}, bf16[5,32,1280]{2,1,0:T(8,128)(2,1)S(1)}, u32[]{:S(2)}, u32[]{:S(2)}) collective-permute-start(bf16[5,32,1280]{2,1,0:T(8,128)(2,1)S(1)} %shard_map.109._.own_rows), channel_id=1, source_target_pairs={{0,96},{32,0},{64,32},{96,64},{1,97},{33,1},{65,33},{97,65},{2,98}... | collective-permute-start | bytes 1228808 | tf_op jit(solution)/shard_map/ppermute | solution.py:31
  16.7 1.9 %copy-start.2 = (bf16[1280,1280]{1,0:T(8,128)(2,1)S(1)}, bf16[1280,1280]{1,0:T(8,128)(2,1)}, u32[]{:S(2)}) copy-start(bf16[1280,1280]{1,0:T(8,128)(2,1)} %fc1_ref.3) | copy-start | bytes 9830404
  18.7 1.9 %copy-start.4 = (bf16[1280,1280]{1,0:T(8,128)(2,1)S(1)}, bf16[1280,1280]{1,0:T(8,128)(2,1)}, u32[]{:S(2)}) copy-start(bf16[1280,1280]{1,0:T(8,128)(2,1)} %fc2_ref.3) | copy-start | bytes 9830404
  20.6 1.9 %copy-start.3 = (bf16[1280,1280]{1,0:T(8,128)(2,1)S(1)}, bf16[1280,1280]{1,0:T(8,128)(2,1)}, u32[]{:S(2)}) copy-start(bf16[1280,1280]{1,0:T(8,128)(2,1)} %fc1_ref.3) | copy-start | bytes 9830404
  20.6 2.9 %copy-start.5 = (bf16[1280,1280]{1,0:T(8,128)(2,1)S(1)}, bf16[1280,1280]{1,0:T(8,128)(2,1)}, u32[]{:S(2)}) copy-start(bf16[1280,1280]{1,0:T(8,128)(2,1)} %fc2_ref.3) | copy-start | bytes 9830404
  20.6 3.0 %copy-start.10 = (bf16[8,32,1280]{2,1,0:T(8,128)(2,1)S(1)}, bf16[8,32,1280]{2,1,0:T(8,128)(2,1)}, u32[]{:S(2)}) copy-start(bf16[8,32,1280]{2,1,0:T(8,128)(2,1)} %patches_ref.7) | copy-start | bytes 1966084
  27.9 20.1 %collective-permute-start.4 = (bf16[4,32,1280]{2,1,0:T(8,128)(2,1)S(1)}, bf16[4,32,1280]{2,1,0:T(8,128)(2,1)S(1)}, u32[]{:S(2)}, u32[]{:S(2)}) collective-permute-start(bf16[4,32,1280]{2,1,0:T(8,128)(2,1)S(1)} %get-tuple-element.29), channel_id=1, source_target_pairs={{0,32},{32,64},{64,96},{96,0},{1,33},{33,65},{65,97},{97,1},{2,34}... | collective-permute-start | bytes 983048 | tf_op jit(solution)/shard_map/ppermute | solution.py:31
  29.8 36.6 %collective-permute-start.3 = (bf16[4,32,1280]{2,1,0:T(8,128)(2,1)S(1)}, bf16[4,32,1280]{2,1,0:T(8,128)(2,1)S(1)}, u32[]{:S(2)}, u32[]{:S(2)}) collective-permute-start(bf16[4,32,1280]{2,1,0:T(8,128)(2,1)S(1)} %get-tuple-element.27), channel_id=1, source_target_pairs={{0,96},{32,0},{64,32},{96,64},{1,97},{33,1},{65,33},{97,65},{2,98}... | collective-permute-start | bytes 983048 | tf_op jit(solution)/shard_map/ppermute | solution.py:31
  37.8 28.7 %copy-start.6 = (bf16[1280,1024]{1,0:T(8,128)(2,1)S(1)}, bf16[1280,1024]{1,0:T(8,128)(2,1)}, u32[]{:S(2)}) copy-start(bf16[1280,1024]{1,0:T(8,128)(2,1)} %refs_7_.1) | copy-start | bytes 7864324
  37.8 28.7 %copy-start.7 = (bf16[1280,1024]{1,0:T(8,128)(2,1)S(1)}, bf16[1280,1024]{1,0:T(8,128)(2,1)}, u32[]{:S(2)}) copy-start(bf16[1280,1024]{1,0:T(8,128)(2,1)} %refs_8_.1) | copy-start | bytes 7864324
  42.1 24.3 %collective-permute-start.10 = (bf16[4,32,1280]{2,1,0:T(8,128)(2,1)S(1)}, bf16[4,32,1280]{2,1,0:T(8,128)(2,1)S(1)}, u32[]{:S(2)}, u32[]{:S(2)}) collective-permute-start(bf16[4,32,1280]{2,1,0:T(8,128)(2,1)S(1)} %get-tuple-element.32), channel_id=1, source_target_pairs={{0,64},{32,96},{64,0},{96,32},{1,65},{33,97},{65,1},{97,33},{2,66}... | collective-permute-start | bytes 983048 | tf_op jit(solution)/shard_map/ppermute | solution.py:31
  44.8 21.7 %collective-permute-start.11 = (bf16[4,32,1280]{2,1,0:T(8,128)(2,1)S(1)}, bf16[4,32,1280]{2,1,0:T(8,128)(2,1)S(1)}, u32[]{:S(2)}, u32[]{:S(2)}) collective-permute-start(bf16[4,32,1280]{2,1,0:T(8,128)(2,1)S(1)} %get-tuple-element.33), channel_id=1, source_target_pairs={{0,96},{32,0},{64,32},{96,64},{1,97},{33,1},{65,33},{97,65},{2,98}... | collective-permute-start | bytes 983048 | tf_op jit(solution)/shard_map/ppermute | solution.py:31
  45.2 21.2 %collective-permute-start.9 = (bf16[4,32,1280]{2,1,0:T(8,128)(2,1)S(1)}, bf16[4,32,1280]{2,1,0:T(8,128)(2,1)S(1)}, u32[]{:S(2)}, u32[]{:S(2)}) collective-permute-start(bf16[4,32,1280]{2,1,0:T(8,128)(2,1)S(1)} %get-tuple-element.31), channel_id=1, source_target_pairs={{0,32},{32,64},{64,96},{96,0},{1,33},{33,65},{65,97},{97,1},{2,34}... | collective-permute-start | bytes 983048 | tf_op jit(solution)/shard_map/ppermute | solution.py:31
  48.1 18.4 %collective-permute-start.5 = (bf16[4,32,1280]{2,1,0:T(8,128)(2,1)S(1)}, bf16[4,32,1280]{2,1,0:T(8,128)(2,1)S(1)}, u32[]{:S(2)}, u32[]{:S(2)}) collective-permute-start(bf16[4,32,1280]{2,1,0:T(8,128)(2,1)S(1)} %shard_map.114), channel_id=1, source_target_pairs={{0,32},{32,64},{64,96},{96,0},{1,33},{33,65},{65,97},{97,1},{2,34}... | collective-permute-start | bytes 983048 | tf_op jit(solution)/shard_map/ppermute | solution.py:31
  66.5 32.4 %copy-start = (bf16[256,8192]{1,0:T(8,128)(2,1)S(1)}, bf16[256,8192]{1,0:T(8,128)(2,1)}, u32[]{:S(2)}) copy-start(bf16[256,8192]{1,0:T(8,128)(2,1)} %weight_ref.5) | copy-start | bytes 12582916
  89.0 5.0 %collective-permute-start.12 = (bf16[208,128]{1,0:T(8,128)(2,1)S(1)}, bf16[208,128]{1,0:T(8,128)(2,1)S(1)}, u32[]{:S(2)}, u32[]{:S(2)}) collective-permute-start(bf16[208,128]{1,0:T(8,128)(2,1)S(1)} %get-tuple-element.36), channel_id=1, source_target_pairs={{0,32},{32,64},{64,96},{96,0},{1,33},{33,65},{65,97},{97,1},{2,34}... | collective-permute-start | bytes 159752 | tf_op jit(solution)/shard_map/ppermute | solution.py:31
  91.7 5.9 %collective-permute-start.13 = (bf16[208,128]{1,0:T(8,128)(2,1)S(1)}, bf16[208,128]{1,0:T(8,128)(2,1)S(1)}, u32[]{:S(2)}, u32[]{:S(2)}) collective-permute-start(bf16[208,128]{1,0:T(8,128)(2,1)S(1)} %get-tuple-element.37), channel_id=1, source_target_pairs={{0,64},{32,96},{64,0},{96,32},{1,65},{33,97},{65,1},{97,33},{2,66}... | collective-permute-start | bytes 159752 | tf_op jit(solution)/shard_map/ppermute | solution.py:31
  93.5 5.3 %collective-permute-start.14 = (bf16[208,128]{1,0:T(8,128)(2,1)S(1)}, bf16[208,128]{1,0:T(8,128)(2,1)S(1)}, u32[]{:S(2)}, u32[]{:S(2)}) collective-permute-start(bf16[208,128]{1,0:T(8,128)(2,1)S(1)} %get-tuple-element.38), channel_id=1, source_target_pairs={{0,96},{32,0},{64,32},{96,64},{1,97},{33,1},{65,33},{97,65},{2,98}... | collective-permute-start | bytes 159752 | tf_op jit(solution)/shard_map/ppermute | solution.py:31
  99.9 2.4 %collective-permute-start.15 = (bf16[4,4,96,256]{3,2,1,0:T(8,128)(2,1)S(1)}, bf16[4,4,96,256]{3,2,1,0:T(8,128)(2,1)S(1)}, u32[]{:S(2)}, u32[]{:S(2)}) collective-permute-start(bf16[4,4,96,256]{3,2,1,0:T(8,128)(2,1)S(1)} %shard_map.120), channel_id=1, source_target_pairs={{0,1},{1,0},{2,3},{3,2},{4,5},{5,4},{6,7},{7,6},{8,9},{9,8},{10,11... | collective-permute-start | bytes 2359304 | tf_op jit(solution)/shard_map/ppermute | solution.py:41
  102.4 12.4 %collective-permute-start.16 = (bf16[4,96,256]{2,1,0:T(8,128)(2,1)S(1)}, bf16[4,96,256]{2,1,0:T(8,128)(2,1)S(1)}, u32[]{:S(2)}, u32[]{:S(2)}) collective-permute-start(bf16[4,96,256]{2,1,0:T(8,128)(2,1)S(1)} %get-tuple-element.40), channel_id=1, source_target_pairs={{0,8},{1,9},{2,10},{3,11},{4,12},{5,13},{6,14},{7,15},{8,16},{9,17... | collective-permute-start | bytes 589832 | tf_op jit(solution)/shard_map/ppermute | solution.py:41
  102.9 12.0 %collective-permute-start.17 = (bf16[4,96,256]{2,1,0:T(8,128)(2,1)S(1)}, bf16[4,96,256]{2,1,0:T(8,128)(2,1)S(1)}, u32[]{:S(2)}, u32[]{:S(2)}) collective-permute-start(bf16[4,96,256]{2,1,0:T(8,128)(2,1)S(1)} %get-tuple-element.41), channel_id=1, source_target_pairs={{0,16},{1,17},{2,18},{3,19},{4,20},{5,21},{6,22},{7,23},{8,24},{9,... | collective-permute-start | bytes 589832 | tf_op jit(solution)/shard_map/ppermute | solution.py:41
  104.9 10.6 %collective-permute-start.18 = (bf16[4,96,256]{2,1,0:T(8,128)(2,1)S(1)}, bf16[4,96,256]{2,1,0:T(8,128)(2,1)S(1)}, u32[]{:S(2)}, u32[]{:S(2)}) collective-permute-start(bf16[4,96,256]{2,1,0:T(8,128)(2,1)S(1)} %get-tuple-element.42), channel_id=1, source_target_pairs={{0,24},{1,25},{2,26},{3,27},{4,28},{5,29},{6,30},{7,31},{8,0},{9,1... | collective-permute-start | bytes 589832 | tf_op jit(solution)/shard_map/ppermute | solution.py:41
  115.6 5.4 %collective-permute-start.19 = (bf16[96,256]{1,0:T(8,128)(2,1)S(1)}, bf16[96,256]{1,0:T(8,128)(2,1)S(1)}, u32[]{:S(2)}, u32[]{:S(2)}) collective-permute-start(bf16[96,256]{1,0:T(8,128)(2,1)S(1)} %get-tuple-element.44), channel_id=1, source_target_pairs={{0,2},{1,3},{2,4},{3,5},{4,6},{5,7},{6,0},{7,1},{8,10},{9,11},{10,... | collective-permute-start | bytes 147464 | tf_op jit(solution)/shard_map/ppermute | solution.py:41
  116.2 5.6 %collective-permute-start.20 = (bf16[96,256]{1,0:T(8,128)(2,1)S(1)}, bf16[96,256]{1,0:T(8,128)(2,1)S(1)}, u32[]{:S(2)}, u32[]{:S(2)}) collective-permute-start(bf16[96,256]{1,0:T(8,128)(2,1)S(1)} %get-tuple-element.45), channel_id=1, source_target_pairs={{0,4},{1,5},{2,6},{3,7},{4,0},{5,1},{6,2},{7,3},{8,12},{9,13},{10,... | collective-permute-start | bytes 147464 | tf_op jit(solution)/shard_map/ppermute | solution.py:41
  118.2 4.1 %collective-permute-start.21 = (bf16[96,256]{1,0:T(8,128)(2,1)S(1)}, bf16[96,256]{1,0:T(8,128)(2,1)S(1)}, u32[]{:S(2)}, u32[]{:S(2)}) collective-permute-start(bf16[96,256]{1,0:T(8,128)(2,1)S(1)} %get-tuple-element.46), channel_id=1, source_target_pairs={{0,6},{1,7},{2,0},{3,1},{4,2},{5,3},{6,4},{7,5},{8,14},{9,15},{10,... | collective-permute-start | bytes 147464 | tf_op jit(solution)/shard_map/ppermute | solution.py:41

commit v6 on v5

--- a/solution.py
+++ b/solution.py
@@ -540,7 +540,7 @@
 
     own = [normalize(at, patches), second_half(at, text_hidden, query_weight, patches)]
     sources = [[rows] + [pool_shift(rows, s) for s in range(1, RING)] for rows in own]
-    held = hold(fc1_weight, fc2_weight, sources[1][0])
+    held = hold(fc1_weight, fc2_weight, sources[0][0])
     target = tables(
         at,
         enc_tiles.reshape(1, -1),
@@ -550,7 +550,7 @@
         steps,
         local_heads,
         capacity,
-        sources[1][0],
+        sources[0][0],
     )
     sums, queries = [], None
     for i in range(halves):

time: 123 us -> 125 us (1.016)
  Pallas kernels: 24.2 us -> 27.2 us
  local copies, waits for them, and re-layouts: 12.3 us -> 10.3 us
    unnamed x31 -> x33, local copies, waits for them, and re-layouts: 11.5 us -> 9.49 us
    pallas_call x2, Pallas kernels: 8.55 us -> 10.2 us  [feed_forward(): pl.pallas_call(functools.partial(feed_forward_kernel, half), out_shape=(s...]
  transfers between devices with their start and end apart: 22 -> 22, of which waited for: 11 -> 11; matrix products, arithmetic and copies ran while one was open for 1% -> 1% of each run, Pallas kernels for 11% -> 13%
where the time goes in v6:
time: 125 us
  blocking collectives  31.1 us (25%)
  starting transfers between devices  29.3 us (23%)
  Pallas kernels  27.2 us (22%)
  waiting for transfers between devices  26.6 us (21%)
  local copies, waits for them, and re-layouts  10.3 us (8%)
    ppermute x15, starting transfers between devices, pool_shift(): return lax.ppermute(x, 'pool', [(i, (i + by) % RING) for i in range(RING)])  21.6 us
    all_to_all x1, blocking collectives, body(): lax.all_to_all(chosen.reshape(devices, per_device, HEAD_DIM), 'dev', spli...  15.9 us
    all_to_all x1, blocking collectives, body(): lax.all_to_all(packed.reshape(devices, per_device, 2 * HEAD_DIM), 'dev',...  15.2 us
    ppermute x15, waiting for transfers between devices, pool_shift(): return lax.ppermute(x, 'pool', [(i, (i + by) % RING) for i in range(RING)])  14.1 us
    ppermute x7, waiting for transfers between devices, dev_shift(): return lax.ppermute(x, 'dev', pairs)  12.5 us
    pallas_call x2, Pallas kernels, feed_forward(): pl.pallas_call(functools.partial(feed_forward_kernel, half), out_shape=(s...  10.2 us
    unnamed x33, local copies, waits for them, and re-layouts  9.49 us
    ppermute x7, starting transfers between devices, dev_shift(): return lax.ppermute(x, 'dev', pairs)  7.72 us
  transfers between devices with their start and end apart: 22, of which 11 were waited for; matrix products, arithmetic and copies ran while one was open for 1% of the time, Pallas kernels for 13%

profile of v6, /device:TPU:6, one launch (start us, length us, event | category | flops | bytes accessed | tf_op | source)
XLA Modules:
  0.0 124.9 jit_solution(2873564017352533935)
XLA Ops:
  0.1 1.1 copy-done.7
  1.2 1.6 %shard_map.109._.own_rows = bf16[4,32,1280]{2,1,0:T(8,128)(2,1)} custom-call(s32[2]{0:T(128)S(1)} %pad_add_fusion.at_ref, bf16[8,32,1280]{2,1,0:T(8,128)(2,1)S(1)} %copy-done.7), custom_call_target="tpu_custom_call" | custom-call | tf_op jit(solution)/shard_map/pallas_call | solution.py:58
  3.1 2.5 %collective-permute-start.1 = (bf16[4,32,1280]{2,1,0:T(8,128)(2,1)}, bf16[4,32,1280]{2,1,0:T(8,128)(2,1)}, u32[]{:S(2)}, u32[]{:S(2)}) collective-permute-start(bf16[4,32,1280]{2,1,0:T(8,128)(2,1)} %shard_map.109._.own_rows), channel_id=1, source_target_pairs={{0,64},{32,96},{64,0},{96,32},{1,65},{33,97},{65,1},{97,33},{2,66}... | collective-permute-start | bytes 983048 | tf_op jit(solution)/shard_map/ppermute | solution.py:31
  5.6 2.2 %copy-done.1 = bf16[8192,256]{1,0:T(8,128)(2,1)S(1)} copy-done((bf16[8192,256]{1,0:T(8,128)(2,1)S(1)}, bf16[8192,256]{1,0:T(8,128)(2,1)}, u32[]{:S(2)}) %copy-start.1) | copy-done | bytes 4194328
  7.8 1.1 copy-done.8
  8.9 1.4 %copy-done.10 = bf16[24,4,8192]{2,1,0:T(4,128)(2,1)S(1)} copy-done((bf16[24,4,8192]{2,1,0:T(4,128)(2,1)S(1)}, bf16[24,4,8192]{2,1,0:T(4,128)(2,1)}, u32[]{:S(2)}) %copy-start.10) | copy-done | bytes 1572888
  10.3 2.9 %shard_map.114.own_rows = bf16[5,32,1280]{2,1,0:T(8,128)(2,1)} custom-call(s32[2]{0:T(128)S(1)} %pad_add_fusion.at_ref, bf16[24,4,8192]{2,1,0:T(4,128)(2,1)S(1)} %copy-done.10, bf16[8192,256]{1,0:T(8,128)(2,1)S(1)} %copy-done.1, bf16[8,32,1280]{2,1,0:T(8,128)(2,1)S(1)} %copy-done.8), custom_call_target="tpu_custom_call" | custom-call | flops 402653184 | bytes 5767168 | tf_op jit(solution)/shard_map/pallas_call | solution.py:188
  13.3 3.2 %collective-permute-start.6 = (bf16[5,32,1280]{2,1,0:T(8,128)(2,1)}, bf16[5,32,1280]{2,1,0:T(8,128)(2,1)}, u32[]{:S(2)}, u32[]{:S(2)}) collective-permute-start(bf16[5,32,1280]{2,1,0:T(8,128)(2,1)} %shard_map.114.own_rows), channel_id=1, source_target_pairs={{0,32},{32,64},{64,96},{96,0},{1,33},{33,65},{65,97},{97,1},{2,34}... | collective-permute-start | bytes 1228808 | tf_op jit(solution)/shard_map/ppermute | solution.py:31
  16.5 0.7 copy-done.13
  17.2 1.4 %collective-permute-start.8 = (bf16[5,32,1280]{2,1,0:T(8,128)(2,1)}, bf16[5,32,1280]{2,1,0:T(8,128)(2,1)}, u32[]{:S(2)}, u32[]{:S(2)}) collective-permute-start(bf16[5,32,1280]{2,1,0:T(8,128)(2,1)} %shard_map.114.own_rows), channel_id=1, source_target_pairs={{0,96},{32,0},{64,32},{96,64},{1,97},{33,1},{65,33},{97,65},{2,98}... | collective-permute-start | bytes 1228808 | tf_op jit(solution)/shard_map/ppermute | solution.py:31
  18.8 1.9 %copy-done.3 = bf16[1280,1280]{1,0:T(8,128)(2,1)S(1)} copy-done((bf16[1280,1280]{1,0:T(8,128)(2,1)S(1)}, bf16[1280,1280]{1,0:T(8,128)(2,1)}, u32[]{:S(2)}) %copy-start.3) | copy-done | bytes 3276824
  20.7 0.6 copy-done.11
  21.4 1.2 shard_map.110.refs_1_.target_ref
  22.9 4.9 %shard_map.112 = (bf16[4,32,1280]{2,1,0:T(8,128)(2,1)S(1)}, bf16[4,32,1280]{2,1,0:T(8,128)(2,1)S(1)}, bf16[4,32,1280]{2,1,0:T(8,128)(2,1)S(1)}, bf16[4,32,1280]{2,1,0:T(8,128)(2,1)S(1)}) custom-call(s32[2]{0:T(128)S(1)} %pad_add_fusion.at_ref, bf16[8,32,1280]{2,1,0:T(8,128)(2,1)S(1)} %copy-done.9, bf16[4,32,1280]{2,1,0:T(8,128)(2,1)} %shard_map.109._.own_rows, ...), custom_call_target="tpu_custom_call" | custom-call | flops 3355443200 | bytes 6553600 | tf_op jit(solution)/shard_map/pallas_call | solution.py:116
  27.8 1.9 %collective-permute-start.4 = (bf16[4,32,1280]{2,1,0:T(8,128)(2,1)S(1)}, bf16[4,32,1280]{2,1,0:T(8,128)(2,1)S(1)}, u32[]{:S(2)}, u32[]{:S(2)}) collective-permute-start(bf16[4,32,1280]{2,1,0:T(8,128)(2,1)S(1)} %get-tuple-element.29), channel_id=1, source_target_pairs={{0,32},{32,64},{64,96},{96,0},{1,33},{33,65},{65,97},{97,1},{2,34}... | collective-permute-start | bytes 983048 | tf_op jit(solution)/shard_map/ppermute | solution.py:31
  30.0 1.3 %collective-permute-done.7.two_rows = bf16[5,32,1280]{2,1,0:T(8,128)(2,1)} collective-permute-done((bf16[5,32,1280]{2,1,0:T(8,128)(2,1)}, bf16[5,32,1280]{2,1,0:T(8,128)(2,1)}, u32[]{:S(2)}, u32[]{:S(2)}) %collective-permute-start.7) | collective-permute-done | bytes 409632 | tf_op jit(solution)/shard_map/ppermute | solution.py:31
  31.3 7.5 %collective-permute-done.8.three_rows = bf16[5,32,1280]{2,1,0:T(8,128)(2,1)} collective-permute-done((bf16[5,32,1280]{2,1,0:T(8,128)(2,1)}, bf16[5,32,1280]{2,1,0:T(8,128)(2,1)}, u32[]{:S(2)}, u32[]{:S(2)}) %collective-permute-start.8) | collective-permute-done | bytes 409632 | tf_op jit(solution)/shard_map/ppermute | solution.py:31
  38.7 5.3 %shard_map.115 = (bf16[4,32,1280]{2,1,0:T(8,128)(2,1)S(1)}, bf16[4,32,1280]{2,1,0:T(8,128)(2,1)S(1)}, bf16[4,32,1280]{2,1,0:T(8,128)(2,1)S(1)}, bf16[4,32,1280]{2,1,0:T(8,128)(2,1)S(1)}, bf16[4,32,1280]{2,1,0:T(8,128)(2,1)S(1)}) custom-call(s32[2]{0:T(128)S(1)} %pad_add_fusion.at_ref, bf16[8,32,1280]{2,1,0:T(8,128)(2,1)S(1)} %copy-done.9, ...), custom_call_target="tpu_custom_call" | custom-call | flops 3355443200 | bytes 6553600 | tf_op jit(solution)/shard_map/pallas_call | solution.py:116
  44.0 2.4 %collective-permute-start.10 = (bf16[4,32,1280]{2,1,0:T(8,128)(2,1)S(1)}, bf16[4,32,1280]{2,1,0:T(8,128)(2,1)S(1)}, u32[]{:S(2)}, u32[]{:S(2)}) collective-permute-start(bf16[4,32,1280]{2,1,0:T(8,128)(2,1)S(1)} %get-tuple-element.32), channel_id=1, source_target_pairs={{0,64},{32,96},{64,0},{96,32},{1,65},{33,97},{65,1},{97,33},{2,66}... | collective-permute-start | bytes 983048 | tf_op jit(solution)/shard_map/ppermute | solution.py:31
  46.4 0.7 collective-permute-start.11
  47.1 2.5 %collective-permute-start.9 = (bf16[4,32,1280]{2,1,0:T(8,128)(2,1)S(1)}, bf16[4,32,1280]{2,1,0:T(8,128)(2,1)S(1)}, u32[]{:S(2)}, u32[]{:S(2)}) collective-permute-start(bf16[4,32,1280]{2,1,0:T(8,128)(2,1)S(1)} %get-tuple-element.31), channel_id=1, source_target_pairs={{0,32},{32,64},{64,96},{96,0},{1,33},{33,65},{65,97},{97,1},{2,34}... | collective-permute-start | bytes 983048 | tf_op jit(solution)/shard_map/ppermute | solution.py:31
  49.7 1.7 %collective-permute-start.5 = (bf16[4,32,1280]{2,1,0:T(8,128)(2,1)S(1)}, bf16[4,32,1280]{2,1,0:T(8,128)(2,1)S(1)}, u32[]{:S(2)}, u32[]{:S(2)}) collective-permute-start(bf16[4,32,1280]{2,1,0:T(8,128)(2,1)S(1)} %shard_map.113), channel_id=1, source_target_pairs={{0,32},{32,64},{64,96},{96,0},{1,33},{33,65},{65,97},{97,1},{2,34}... | collective-permute-start | bytes 983048 | tf_op jit(solution)/shard_map/ppermute | solution.py:31
  51.4 1.0 shard_map.116
  52.4 15.9 %all_to_all.10 = bf16[32,16,128]{2,1,0:T(8,128)(2,1)S(1)} all-to-all(bf16[32,16,128]{2,1,0:T(8,128)(2,1)S(1)} %bitcast.11), channel_id=1, replica_groups=mesh['pool'=4,'dev'=32] {'dev'}, dimensions={0} | all-to-all | bytes 262144 | tf_op jit(solution)/shard_map/all_to_all | solution.py:568
  68.4 6.1 %shard_map.117 = bf16[8,4,16,256]{3,2,1,0:T(8,128)(2,1)S(1)} custom-call(bf16[4,32,1280]{2,1,0:T(8,128)(2,1)S(1)} %get-tuple-element.26.refs_0_, bf16[4,32,1280]{2,1,0:T(8,128)(2,1)S(1)} %collective-permute-done.3.refs_1_, bf16[4,32,1280]{2,1,0:T(8,128)(2,1)S(1)} %collective-permute-done.5.refs_2_, bf16[4,32,1280]{2,1,0:T(8,128)(2,1)S(1)} %get-tuple-element.30.refs_3_, ...), custom_call_target="tpu_custom_call" | custom-call | flops 1342177280 | bytes 5242880 | tf_op jit(solution)/shard_map/pallas_call | solution.py:367
  74.5 15.2 %all_to_all.11 = bf16[32,16,256]{2,1,0:T(8,128)(2,1)S(1)} all-to-all(bf16[32,16,256]{2,1,0:T(8,128)(2,1)S(1)} %bitcast.8), channel_id=1, replica_groups=mesh['pool'=4,'dev'=32] {'dev'}, dimensions={0} | all-to-all | bytes 524288 | tf_op jit(solution)/shard_map/all_to_all | solution.py:572
  89.7 1.2 shard_map.118
  90.9 2.7 %collective-permute-start.12 = (bf16[208,128]{1,0:T(8,128)(2,1)S(1)}, bf16[208,128]{1,0:T(8,128)(2,1)S(1)}, u32[]{:S(2)}, u32[]{:S(2)}) collective-permute-start(bf16[208,128]{1,0:T(8,128)(2,1)S(1)} %get-tuple-element.36), channel_id=1, source_target_pairs={{0,32},{32,64},{64,96},{96,0},{1,33},{33,65},{65,97},{97,1},{2,34}... | collective-permute-start | bytes 159752 | tf_op jit(solution)/shard_map/ppermute | solution.py:31
  93.6 1.8 %collective-permute-start.13 = (bf16[208,128]{1,0:T(8,128)(2,1)S(1)}, bf16[208,128]{1,0:T(8,128)(2,1)S(1)}, u32[]{:S(2)}, u32[]{:S(2)}) collective-permute-start(bf16[208,128]{1,0:T(8,128)(2,1)S(1)} %get-tuple-element.37), channel_id=1, source_target_pairs={{0,64},{32,96},{64,0},{96,32},{1,65},{33,97},{65,1},{97,33},{2,66}... | collective-permute-start | bytes 159752 | tf_op jit(solution)/shard_map/ppermute | solution.py:31
  95.4 0.5 collective-permute-done.12.one_ref
  95.9 3.7 %collective-permute-done.13.two_ref = bf16[208,128]{1,0:T(8,128)(2,1)S(1)} collective-permute-done((bf16[208,128]{1,0:T(8,128)(2,1)S(1)}, bf16[208,128]{1,0:T(8,128)(2,1)S(1)}, u32[]{:S(2)}, u32[]{:S(2)}) %collective-permute-start.13) | collective-permute-done | bytes 53280 | tf_op jit(solution)/shard_map/ppermute | solution.py:31
  99.6 1.2 collective-permute-done.14.three_ref
  100.8 1.1 shard_map.120
  101.9 1.1 shard_map.119.kept_ref
  103.0 1.2 collective-permute-done.15.got_ref
  104.4 0.4 collective-permute-start.16
  104.8 2.1 %collective-permute-start.17 = (bf16[4,96,256]{2,1,0:T(8,128)(2,1)S(1)}, bf16[4,96,256]{2,1,0:T(8,128)(2,1)S(1)}, u32[]{:S(2)}, u32[]{:S(2)}) collective-permute-start(bf16[4,96,256]{2,1,0:T(8,128)(2,1)S(1)} %get-tuple-element.41), channel_id=1, source_target_pairs={{0,16},{1,17},{2,18},{3,19},{4,20},{5,21},{6,22},{7,23},{8,24},{9,... | collective-permute-start | bytes 589832 | tf_op jit(solution)/shard_map/ppermute | solution.py:41
  106.9 1.3 %collective-permute-start.18 = (bf16[4,96,256]{2,1,0:T(8,128)(2,1)S(1)}, bf16[4,96,256]{2,1,0:T(8,128)(2,1)S(1)}, u32[]{:S(2)}, u32[]{:S(2)}) collective-permute-start(bf16[4,96,256]{2,1,0:T(8,128)(2,1)S(1)} %get-tuple-element.42), channel_id=1, source_target_pairs={{0,24},{1,25},{2,26},{3,27},{4,28},{5,29},{6,30},{7,31},{8,0},{9,1... | collective-permute-start | bytes 589832 | tf_op jit(solution)/shard_map/ppermute | solution.py:41
  108.2 8.7 %collective-permute-done.16.a_ref = bf16[4,96,256]{2,1,0:T(8,128)(2,1)S(1)} collective-permute-done((bf16[4,96,256]{2,1,0:T(8,128)(2,1)S(1)}, bf16[4,96,256]{2,1,0:T(8,128)(2,1)S(1)}, u32[]{:S(2)}, u32[]{:S(2)}) %collective-permute-start.16) | collective-permute-done | bytes 196640 | tf_op jit(solution)/shard_map/ppermute | solution.py:41
  116.8 0.6 collective-permute-done.18.c_ref
  117.5 0.6 collective-permute-start.19
  118.2 2.0 %collective-permute-start.20 = (bf16[96,256]{1,0:T(8,128)(2,1)S(1)}, bf16[96,256]{1,0:T(8,128)(2,1)S(1)}, u32[]{:S(2)}, u32[]{:S(2)}) collective-permute-start(bf16[96,256]{1,0:T(8,128)(2,1)S(1)} %get-tuple-element.45), channel_id=1, source_target_pairs={{0,4},{1,5},{2,6},{3,7},{4,0},{5,1},{6,2},{7,3},{8,12},{9,13},{10,... | collective-permute-start | bytes 147464 | tf_op jit(solution)/shard_map/ppermute | solution.py:41
  120.2 1.2 collective-permute-start.21
  121.4 0.8 constant_dynamic-slice_fusion.residual_ref
  122.2 0.7 collective-permute-done.19.a_ref
  122.9 0.9 collective-permute-done.20.b_ref
  123.8 0.5 collective-permute-done.21.c_ref
  124.3 0.7 shard_map.123
  (48 shorter events, 1.7 us)
Async XLA Ops:
  0.1 1.1 copy-start.7
  1.2 17.5 %copy-start.15 = (s32[64,1]{0,1:T(1,128)S(1)}, s32[64,1]{0,1:T(1,128)}, u32[]{:S(2)}) copy-start(s32[64,1]{0,1:T(1,128)} %param.14) | copy-start | bytes 772
  2.7 13.8 %collective-permute-start = (bf16[4,32,1280]{2,1,0:T(8,128)(2,1)}, bf16[4,32,1280]{2,1,0:T(8,128)(2,1)S(1)}, u32[]{:S(2)}, u32[]{:S(2)}) collective-permute-start(bf16[4,32,1280]{2,1,0:T(8,128)(2,1)} %shard_map.109._.own_rows), channel_id=1, source_target_pairs={{0,32},{32,64},{64,96},{96,0},{1,33},{33,65},{65,97},{97,1},{2,34}... | collective-permute-start | bytes 983048 | tf_op jit(solution)/shard_map/ppermute | solution.py:31
  3.1 19.4 %collective-permute-start.1 = (bf16[4,32,1280]{2,1,0:T(8,128)(2,1)}, bf16[4,32,1280]{2,1,0:T(8,128)(2,1)}, u32[]{:S(2)}, u32[]{:S(2)}) collective-permute-start(bf16[4,32,1280]{2,1,0:T(8,128)(2,1)} %shard_map.109._.own_rows), channel_id=1, source_target_pairs={{0,64},{32,96},{64,0},{96,32},{1,65},{33,97},{65,1},{97,33},{2,66}... | collective-permute-start | bytes 983048 | tf_op jit(solution)/shard_map/ppermute | solution.py:31
  5.6 16.9 %collective-permute-start.2 = (bf16[4,32,1280]{2,1,0:T(8,128)(2,1)}, bf16[4,32,1280]{2,1,0:T(8,128)(2,1)}, u32[]{:S(2)}, u32[]{:S(2)}) collective-permute-start(bf16[4,32,1280]{2,1,0:T(8,128)(2,1)} %shard_map.109._.own_rows), channel_id=1, source_target_pairs={{0,96},{32,0},{64,32},{96,64},{1,97},{33,1},{65,33},{97,65},{2,98}... | collective-permute-start | bytes 983048 | tf_op jit(solution)/shard_map/ppermute | solution.py:31
  5.6 2.2 %copy-start.1 = (bf16[8192,256]{1,0:T(8,128)(2,1)S(1)}, bf16[8192,256]{1,0:T(8,128)(2,1)}, u32[]{:S(2)}) copy-start(bf16[8192,256]{1,0:T(8,128)(2,1)} %weight_ref.3) | copy-start | bytes 12582916
  7.8 1.1 copy-start.8
  8.9 1.4 %copy-start.10 = (bf16[24,4,8192]{2,1,0:T(4,128)(2,1)S(1)}, bf16[24,4,8192]{2,1,0:T(4,128)(2,1)}, u32[]{:S(2)}) copy-start(bf16[24,4,8192]{2,1,0:T(4,128)(2,1)} %text_ref.1) | copy-start | bytes 4718596
  10.3 8.5 %copy-start.2 = (bf16[1280,1280]{1,0:T(8,128)(2,1)S(1)}, bf16[1280,1280]{1,0:T(8,128)(2,1)}, u32[]{:S(2)}) copy-start(bf16[1280,1280]{1,0:T(8,128)(2,1)} %fc1_ref.3) | copy-start | bytes 9830404
  13.3 16.7 %collective-permute-start.6 = (bf16[5,32,1280]{2,1,0:T(8,128)(2,1)}, bf16[5,32,1280]{2,1,0:T(8,128)(2,1)}, u32[]{:S(2)}, u32[]{:S(2)}) collective-permute-start(bf16[5,32,1280]{2,1,0:T(8,128)(2,1)} %shard_map.114.own_rows), channel_id=1, source_target_pairs={{0,32},{32,64},{64,96},{96,0},{1,33},{33,65},{65,97},{97,1},{2,34}... | collective-permute-start | bytes 1228808 | tf_op jit(solution)/shard_map/ppermute | solution.py:31
  16.5 14.8 %collective-permute-start.7 = (bf16[5,32,1280]{2,1,0:T(8,128)(2,1)}, bf16[5,32,1280]{2,1,0:T(8,128)(2,1)}, u32[]{:S(2)}, u32[]{:S(2)}) collective-permute-start(bf16[5,32,1280]{2,1,0:T(8,128)(2,1)} %shard_map.114.own_rows), channel_id=1, source_target_pairs={{0,64},{32,96},{64,0},{96,32},{1,65},{33,97},{65,1},{97,33},{2,66}... | collective-permute-start | bytes 1228808 | tf_op jit(solution)/shard_map/ppermute | solution.py:31
  16.5 0.7 copy-start.13
  17.2 21.5 %collective-permute-start.8 = (bf16[5,32,1280]{2,1,0:T(8,128)(2,1)}, bf16[5,32,1280]{2,1,0:T(8,128)(2,1)}, u32[]{:S(2)}, u32[]{:S(2)}) collective-permute-start(bf16[5,32,1280]{2,1,0:T(8,128)(2,1)} %shard_map.114.own_rows), channel_id=1, source_target_pairs={{0,96},{32,0},{64,32},{96,64},{1,97},{33,1},{65,33},{97,65},{2,98}... | collective-permute-start | bytes 1228808 | tf_op jit(solution)/shard_map/ppermute | solution.py:31
  18.8 1.9 %copy-start.3 = (bf16[1280,1280]{1,0:T(8,128)(2,1)S(1)}, bf16[1280,1280]{1,0:T(8,128)(2,1)}, u32[]{:S(2)}) copy-start(bf16[1280,1280]{1,0:T(8,128)(2,1)} %fc2_ref.3) | copy-start | bytes 9830404
  20.7 0.7 copy-start.11
  20.7 0.7 copy-start.12
  20.7 2.0 %copy-start.4 = (bf16[1280,1280]{1,0:T(8,128)(2,1)S(1)}, bf16[1280,1280]{1,0:T(8,128)(2,1)}, u32[]{:S(2)}) copy-start(bf16[1280,1280]{1,0:T(8,128)(2,1)} %fc2_ref.3) | copy-start | bytes 9830404
  20.7 2.1 %copy-start.9 = (bf16[8,32,1280]{2,1,0:T(8,128)(2,1)S(1)}, bf16[8,32,1280]{2,1,0:T(8,128)(2,1)}, u32[]{:S(2)}) copy-start(bf16[8,32,1280]{2,1,0:T(8,128)(2,1)} %patches_ref.7) | copy-start | bytes 1966084
  20.7 2.2 %copy-start.14 = (bf16[4,32,1280]{2,1,0:T(8,128)(2,1)S(1)}, bf16[4,32,1280]{2,1,0:T(8,128)(2,1)}, u32[]{:S(2)}) copy-start(bf16[4,32,1280]{2,1,0:T(8,128)(2,1)} %copy-done.13) | copy-start | bytes 983044
  27.8 21.9 %collective-permute-start.4 = (bf16[4,32,1280]{2,1,0:T(8,128)(2,1)S(1)}, bf16[4,32,1280]{2,1,0:T(8,128)(2,1)S(1)}, u32[]{:S(2)}, u32[]{:S(2)}) collective-permute-start(bf16[4,32,1280]{2,1,0:T(8,128)(2,1)S(1)} %get-tuple-element.29), channel_id=1, source_target_pairs={{0,32},{32,64},{64,96},{96,0},{1,33},{33,65},{65,97},{97,1},{2,34}... | collective-permute-start | bytes 983048 | tf_op jit(solution)/shard_map/ppermute | solution.py:31
  29.7 38.7 %collective-permute-start.3 = (bf16[4,32,1280]{2,1,0:T(8,128)(2,1)S(1)}, bf16[4,32,1280]{2,1,0:T(8,128)(2,1)S(1)}, u32[]{:S(2)}, u32[]{:S(2)}) collective-permute-start(bf16[4,32,1280]{2,1,0:T(8,128)(2,1)S(1)} %get-tuple-element.27), channel_id=1, source_target_pairs={{0,96},{32,0},{64,32},{96,64},{1,97},{33,1},{65,33},{97,65},{2,98}... | collective-permute-start | bytes 983048 | tf_op jit(solution)/shard_map/ppermute | solution.py:31
  38.7 29.7 %copy-start.5 = (bf16[1280,1024]{1,0:T(8,128)(2,1)S(1)}, bf16[1280,1024]{1,0:T(8,128)(2,1)}, u32[]{:S(2)}) copy-start(bf16[1280,1024]{1,0:T(8,128)(2,1)} %refs_7_.1) | copy-start | bytes 7864324
  38.7 29.7 %copy-start.6 = (bf16[1280,1024]{1,0:T(8,128)(2,1)S(1)}, bf16[1280,1024]{1,0:T(8,128)(2,1)}, u32[]{:S(2)}) copy-start(bf16[1280,1024]{1,0:T(8,128)(2,1)} %refs_8_.1) | copy-start | bytes 7864324
  44.0 24.4 %collective-permute-start.10 = (bf16[4,32,1280]{2,1,0:T(8,128)(2,1)S(1)}, bf16[4,32,1280]{2,1,0:T(8,128)(2,1)S(1)}, u32[]{:S(2)}, u32[]{:S(2)}) collective-permute-start(bf16[4,32,1280]{2,1,0:T(8,128)(2,1)S(1)} %get-tuple-element.32), channel_id=1, source_target_pairs={{0,64},{32,96},{64,0},{96,32},{1,65},{33,97},{65,1},{97,33},{2,66}... | collective-permute-start | bytes 983048 | tf_op jit(solution)/shard_map/ppermute | solution.py:31
  46.4 21.9 %collective-permute-start.11 = (bf16[4,32,1280]{2,1,0:T(8,128)(2,1)S(1)}, bf16[4,32,1280]{2,1,0:T(8,128)(2,1)S(1)}, u32[]{:S(2)}, u32[]{:S(2)}) collective-permute-start(bf16[4,32,1280]{2,1,0:T(8,128)(2,1)S(1)} %get-tuple-element.33), channel_id=1, source_target_pairs={{0,96},{32,0},{64,32},{96,64},{1,97},{33,1},{65,33},{97,65},{2,98}... | collective-permute-start | bytes 983048 | tf_op jit(solution)/shard_map/ppermute | solution.py:31
  47.1 21.2 %collective-permute-start.9 = (bf16[4,32,1280]{2,1,0:T(8,128)(2,1)S(1)}, bf16[4,32,1280]{2,1,0:T(8,128)(2,1)S(1)}, u32[]{:S(2)}, u32[]{:S(2)}) collective-permute-start(bf16[4,32,1280]{2,1,0:T(8,128)(2,1)S(1)} %get-tuple-element.31), channel_id=1, source_target_pairs={{0,32},{32,64},{64,96},{96,0},{1,33},{33,65},{65,97},{97,1},{2,34}... | collective-permute-start | bytes 983048 | tf_op jit(solution)/shard_map/ppermute | solution.py:31
  49.7 18.6 %collective-permute-start.5 = (bf16[4,32,1280]{2,1,0:T(8,128)(2,1)S(1)}, bf16[4,32,1280]{2,1,0:T(8,128)(2,1)S(1)}, u32[]{:S(2)}, u32[]{:S(2)}) collective-permute-start(bf16[4,32,1280]{2,1,0:T(8,128)(2,1)S(1)} %shard_map.113), channel_id=1, source_target_pairs={{0,32},{32,64},{64,96},{96,0},{1,33},{33,65},{65,97},{97,1},{2,34}... | collective-permute-start | bytes 983048 | tf_op jit(solution)/shard_map/ppermute | solution.py:31
  68.4 32.4 %copy-start = (bf16[256,8192]{1,0:T(8,128)(2,1)S(1)}, bf16[256,8192]{1,0:T(8,128)(2,1)}, u32[]{:S(2)}) copy-start(bf16[256,8192]{1,0:T(8,128)(2,1)} %weight_ref.5) | copy-start | bytes 12582916
  90.9 5.0 %collective-permute-start.12 = (bf16[208,128]{1,0:T(8,128)(2,1)S(1)}, bf16[208,128]{1,0:T(8,128)(2,1)S(1)}, u32[]{:S(2)}, u32[]{:S(2)}) collective-permute-start(bf16[208,128]{1,0:T(8,128)(2,1)S(1)} %get-tuple-element.36), channel_id=1, source_target_pairs={{0,32},{32,64},{64,96},{96,0},{1,33},{33,65},{65,97},{97,1},{2,34}... | collective-permute-start | bytes 159752 | tf_op jit(solution)/shard_map/ppermute | solution.py:31
  93.6 5.9 %collective-permute-start.13 = (bf16[208,128]{1,0:T(8,128)(2,1)S(1)}, bf16[208,128]{1,0:T(8,128)(2,1)S(1)}, u32[]{:S(2)}, u32[]{:S(2)}) collective-permute-start(bf16[208,128]{1,0:T(8,128)(2,1)S(1)} %get-tuple-element.37), channel_id=1, source_target_pairs={{0,64},{32,96},{64,0},{96,32},{1,65},{33,97},{65,1},{97,33},{2,66}... | collective-permute-start | bytes 159752 | tf_op jit(solution)/shard_map/ppermute | solution.py:31
  95.4 5.3 %collective-permute-start.14 = (bf16[208,128]{1,0:T(8,128)(2,1)S(1)}, bf16[208,128]{1,0:T(8,128)(2,1)S(1)}, u32[]{:S(2)}, u32[]{:S(2)}) collective-permute-start(bf16[208,128]{1,0:T(8,128)(2,1)S(1)} %get-tuple-element.38), channel_id=1, source_target_pairs={{0,96},{32,0},{64,32},{96,64},{1,97},{33,1},{65,33},{97,65},{2,98}... | collective-permute-start | bytes 159752 | tf_op jit(solution)/shard_map/ppermute | solution.py:31
  101.8 2.4 %collective-permute-start.15 = (bf16[4,4,96,256]{3,2,1,0:T(8,128)(2,1)S(1)}, bf16[4,4,96,256]{3,2,1,0:T(8,128)(2,1)S(1)}, u32[]{:S(2)}, u32[]{:S(2)}) collective-permute-start(bf16[4,4,96,256]{3,2,1,0:T(8,128)(2,1)S(1)} %shard_map.120), channel_id=1, source_target_pairs={{0,1},{1,0},{2,3},{3,2},{4,5},{5,4},{6,7},{7,6},{8,9},{9,8},{10,11... | collective-permute-start | bytes 2359304 | tf_op jit(solution)/shard_map/ppermute | solution.py:41
  104.4 12.4 %collective-permute-start.16 = (bf16[4,96,256]{2,1,0:T(8,128)(2,1)S(1)}, bf16[4,96,256]{2,1,0:T(8,128)(2,1)S(1)}, u32[]{:S(2)}, u32[]{:S(2)}) collective-permute-start(bf16[4,96,256]{2,1,0:T(8,128)(2,1)S(1)} %get-tuple-element.40), channel_id=1, source_target_pairs={{0,8},{1,9},{2,10},{3,11},{4,12},{5,13},{6,14},{7,15},{8,16},{9,17... | collective-permute-start | bytes 589832 | tf_op jit(solution)/shard_map/ppermute | solution.py:41
  104.8 12.0 %collective-permute-start.17 = (bf16[4,96,256]{2,1,0:T(8,128)(2,1)S(1)}, bf16[4,96,256]{2,1,0:T(8,128)(2,1)S(1)}, u32[]{:S(2)}, u32[]{:S(2)}) collective-permute-start(bf16[4,96,256]{2,1,0:T(8,128)(2,1)S(1)} %get-tuple-element.41), channel_id=1, source_target_pairs={{0,16},{1,17},{2,18},{3,19},{4,20},{5,21},{6,22},{7,23},{8,24},{9,... | collective-permute-start | bytes 589832 | tf_op jit(solution)/shard_map/ppermute | solution.py:41
  106.9 10.6 %collective-permute-start.18 = (bf16[4,96,256]{2,1,0:T(8,128)(2,1)S(1)}, bf16[4,96,256]{2,1,0:T(8,128)(2,1)S(1)}, u32[]{:S(2)}, u32[]{:S(2)}) collective-permute-start(bf16[4,96,256]{2,1,0:T(8,128)(2,1)S(1)} %get-tuple-element.42), channel_id=1, source_target_pairs={{0,24},{1,25},{2,26},{3,27},{4,28},{5,29},{6,30},{7,31},{8,0},{9,1... | collective-permute-start | bytes 589832 | tf_op jit(solution)/shard_map/ppermute | solution.py:41
  117.5 5.4 %collective-permute-start.19 = (bf16[96,256]{1,0:T(8,128)(2,1)S(1)}, bf16[96,256]{1,0:T(8,128)(2,1)S(1)}, u32[]{:S(2)}, u32[]{:S(2)}) collective-permute-start(bf16[96,256]{1,0:T(8,128)(2,1)S(1)} %get-tuple-element.44), channel_id=1, source_target_pairs={{0,2},{1,3},{2,4},{3,5},{4,6},{5,7},{6,0},{7,1},{8,10},{9,11},{10,... | collective-permute-start | bytes 147464 | tf_op jit(solution)/shard_map/ppermute | solution.py:41
  118.2 5.6 %collective-permute-start.20 = (bf16[96,256]{1,0:T(8,128)(2,1)S(1)}, bf16[96,256]{1,0:T(8,128)(2,1)S(1)}, u32[]{:S(2)}, u32[]{:S(2)}) collective-permute-start(bf16[96,256]{1,0:T(8,128)(2,1)S(1)} %get-tuple-element.45), channel_id=1, source_target_pairs={{0,4},{1,5},{2,6},{3,7},{4,0},{5,1},{6,2},{7,3},{8,12},{9,13},{10,... | collective-permute-start | bytes 147464 | tf_op jit(solution)/shard_map/ppermute | solution.py:41
  120.2 4.1 %collective-permute-start.21 = (bf16[96,256]{1,0:T(8,128)(2,1)S(1)}, bf16[96,256]{1,0:T(8,128)(2,1)S(1)}, u32[]{:S(2)}, u32[]{:S(2)}) collective-permute-start(bf16[96,256]{1,0:T(8,128)(2,1)S(1)} %get-tuple-element.46), channel_id=1, source_target_pairs={{0,6},{1,7},{2,0},{3,1},{4,2},{5,3},{6,4},{7,5},{8,14},{9,15},{10,... | collective-permute-start | bytes 147464 | tf_op jit(solution)/shard_map/ppermute | solution.py:41
